TPU v7x, 256 devices: a whole 4x4x8 slice. The times are simulated.
256 devices in a mesh: lender: 32 (over y, z), tensor: 8 (over x, core).
Axes of the slice: x: 4, y: 4, z: 8, core: 2. Of those that a mesh axis runs over, the one named last changes fastest.
Arguments:
- draft_queries: bfloat16 [64, 4, 128, 192], P('lender', None, 'tensor'), may hold values from -6.5 to 6.5
- draft_latents: bfloat16 [64, 4, 576], P('lender'), may hold values from -15 to 15
- latent_pool: bfloat16 [1024, 192, 576], P('lender'), may hold values from -6 to 6
- key_absorb: bfloat16 [128, 128, 512], P('tensor'), may hold values from -0.5 to 0.5
- value_absorb: bfloat16 [128, 512, 128], P('tensor'), may hold values from -0.25 to 0.25
- out_proj: bfloat16 [16384, 7168], P('tensor', 'lender'), may hold values from -0.046875 to 0.046875
- slot_request: int32 [32, 32], replicated, may hold values from 0 to 63, as said below
- context_lengths: int32 [64], replicated, may hold values from 1 to 5952, as said below
Outputs:
- mixed: bfloat16 [64, 4, 7168], P('tensor', None, 'lender')
Inputs may be any that keep to these rules, and one draw needn't show every extreme that they name: slot_request[d, e] lies in e * 2 to (e + 1) * 2 - 1, and every request holds at least one slot. With n slots holding request r, context_lengths[r] lies in 192 (n - 1) + 1 to 192 n; the maximum 192 (31) is reached in every draw.
All inputs are finite; a program needn't handle non-finite values.
Results may differ from a plain program's by a relative error of at most 0.02.
Values may be sent and summed in bfloat16 or wider, within the bound.
No kernel may reach another device: no remote copies, remote signals or barrier semaphores. Data moves between devices by JAX's collectives and lax.ppermute only.
A program may use at most 64 MiB of HBM per device.

v0:
```python
import math

import jax
import jax.numpy as jnp
from jax import lax
from jax.sharding import PartitionSpec as P

MSCALE_SQ = (0.1 * math.log(40.0) + 1.0) ** 2
NEG_FILL = -1e30


def absorb(queries, key_absorb):
    nope_width = key_absorb.shape[1]
    latent_part = jnp.einsum(
        "nshc,hcl->nshl", queries[..., :nope_width], key_absorb, preferred_element_type=jnp.float32
    )
    return jnp.concatenate([latent_part.astype(jnp.bfloat16), queries[..., nope_width:]], axis=-1)


def live_tokens(slot_request, context_lengths, slot_tokens):
    lenders = slot_request.shape[0]
    owners = jnp.arange(context_lengths.shape[0], dtype=jnp.int32)
    lengths = jnp.sum(
        jnp.where(
            slot_request[:, :, None] == owners[None, None, :], context_lengths[None, None, :], 0
        ),
        axis=-1,
    )
    matching = slot_request[:, None, :] == slot_request[None, :, :]
    before = jnp.arange(lenders)[:, None] < jnp.arange(lenders)[None, :]
    slot_rank = jnp.sum(jnp.where(matching & before[:, :, None], 1, 0), axis=0)
    return jnp.clip(lengths - slot_tokens * slot_rank, 0, slot_tokens)


def slot_partials(queries, blocks, live_here, score_scale, latent_width):
    scores = (
        jnp.einsum("nshk,ntk->nsht", queries, blocks, preferred_element_type=jnp.float32)
        * score_scale
    )
    usable = jnp.arange(blocks.shape[1])[None, :] < live_here[:, None]
    scores = jnp.where(usable[:, None, None, :], scores, NEG_FILL)
    slot_top = jnp.max(scores, axis=-1)
    weights = jnp.exp(scores - slot_top[..., None])
    slot_total = jnp.sum(weights, axis=-1)
    weighted = jnp.einsum(
        "nsht,ntl->nshl",
        weights.astype(jnp.bfloat16),
        blocks[:, :, :latent_width],
        preferred_element_type=jnp.float32,
    )
    return ((weighted / slot_total[..., None]).astype(jnp.bfloat16), slot_top, slot_total)


def project_values(slot_mean, value_absorb):
    return jnp.einsum(
        "nshl,hlc->nshc", slot_mean, value_absorb, preferred_element_type=jnp.float32
    ).astype(jnp.bfloat16)


def finish(
    numerator, denominator, slot_top, absorbed, drafts, value_absorb, score_scale, latent_width
):
    scores = (
        jnp.einsum("ishk,ijk->ishj", absorbed, drafts, preferred_element_type=jnp.float32)
        * score_scale
    )
    steps_count = drafts.shape[1]
    causal = jnp.arange(steps_count)[:, None] >= jnp.arange(steps_count)[None, :]
    scores = jnp.where(causal[None, :, None, :], scores, NEG_FILL)
    row_top = jnp.maximum(slot_top, jnp.max(scores, axis=-1))
    draft_weights = jnp.exp(scores - row_top[..., None])
    shrink = jnp.exp(slot_top - row_top)
    draft_values = jnp.einsum(
        "ijl,hlc->ijhc",
        drafts[:, :, :latent_width],
        value_absorb,
        preferred_element_type=jnp.float32,
    )
    full_num = numerator * shrink[..., None] + jnp.einsum(
        "ishj,ijhc->ishc", draft_weights, draft_values, precision=lax.Precision.HIGHEST
    )
    full_den = denominator * shrink + jnp.sum(draft_weights, axis=-1)
    return (full_num / full_den[..., None]).astype(jnp.bfloat16)


def body(
    draft_queries,
    draft_latents,
    latent_pool,
    key_absorb,
    value_absorb,
    out_proj,
    slot_request,
    context_lengths,
):
    home_index = lax.axis_index("lender")
    latent_width = value_absorb.shape[1]
    rows_here = draft_queries.shape[0]
    score_scale = draft_queries.shape[-1] ** (-0.5) * MSCALE_SQ
    absorbed = absorb(draft_queries, key_absorb)
    column = lax.dynamic_slice_in_dim(slot_request, home_index, 1, 1)[:, 0]
    local_rows = column - home_index * rows_here
    live_all = live_tokens(slot_request, context_lengths, latent_pool.shape[1])
    live_here = lax.dynamic_slice_in_dim(live_all, home_index, 1, 0)[0]
    outgoing = jnp.take(absorbed, local_rows, axis=0)
    arrived = lax.all_to_all(outgoing, "lender", split_axis=0, concat_axis=0, tiled=True)
    slot_mean, slot_top, slot_total = slot_partials(
        arrived, latent_pool, live_here, score_scale, latent_width
    )
    mean_back = lax.all_to_all(slot_mean, "lender", split_axis=0, concat_axis=0, tiled=True)
    value_back = project_values(mean_back, value_absorb)
    top_back, total_back = (
        lax.all_to_all(slot_top, "lender", split_axis=0, concat_axis=0, tiled=True),
        lax.all_to_all(slot_total, "lender", split_axis=0, concat_axis=0, tiled=True),
    )
    member = (local_rows[:, None] == jnp.arange(rows_here)[None, :])[:, :, None, None]
    row_peak = jnp.max(jnp.where(member, top_back[:, None], NEG_FILL), axis=0)
    weight = jnp.where(
        member,
        total_back[:, None]
        * jnp.exp(jnp.where(member, top_back[:, None] - row_peak[None], NEG_FILL)),
        0.0,
    )
    numerator = jnp.einsum(
        "dish,dshc->ishc", weight, value_back.astype(jnp.float32), precision=lax.Precision.HIGHEST
    )
    denominator = jnp.sum(weight, axis=0)
    heads_out = finish(
        numerator,
        denominator,
        row_peak,
        absorbed,
        draft_latents,
        value_absorb,
        score_scale,
        latent_width,
    )
    flattened = heads_out.reshape(
        rows_here, heads_out.shape[1], heads_out.shape[2] * heads_out.shape[3]
    )
    partial_terms = jnp.einsum(
        "isc,cd->isd",
        lax.all_gather(flattened, "lender", axis=0, tiled=True),
        out_proj,
        preferred_element_type=jnp.float32,
    )
    return lax.psum_scatter(
        partial_terms.astype(jnp.bfloat16), "tensor", scatter_dimension=0, tiled=True
    )


def solution(mesh):
    in_specs = (
        P("lender", None, "tensor", None),
        P("lender", None, None),
        P("lender", None, None),
        P("tensor", None, None),
        P("tensor", None, None),
        P("tensor", "lender"),
        P(),
        P(),
    )
    out_specs = P("tensor", None, "lender")
    return jax.shard_map(body, mesh=mesh, in_specs=in_specs, out_specs=out_specs, check_vma=False)
```

profile of v0, /device:TPU:1, one launch (start us, length us, event | category | flops | bytes accessed | tf_op | source)
XLA Modules:
  0.0 339.3 jit_solution(4927317682696354507)
XLA Ops:
  6.5 1.1 and_reduce_fusion
  7.6 0.9 fusion.48
  8.5 0.8 slice.12
  9.3 0.8 slice.13
  10.0 2.0 fusion.31
  12.0 0.1 pad_maximum_fusion
  12.1 4.3 %gather_fusion = bf16[32,4,16,576]{3,1,2,0:T(4,128)(2,1)} fusion(bf16[2,4,16,576]{3,1,0,2:T(4,128)(2,1)S(1)} %pad_maximum_fusion, s32[1024]{0:T(1024)S(1)} %pad_clamp_fusion), kind=kCustom, calls=%fused_computation | custom fusion | bytes 4718720 | tf_op jit(solution)/shard_map/jit(_take)/gather | solution.py:105
  16.4 4.5 %broadcast_select_fusion = bf16[32,4,16,576]{3,1,2,0:T(4,128)(2,1)} fusion(bf16[32,4,16,576]{3,1,2,0:T(4,128)(2,1)} %gather_fusion, pred[32]{0:T(512)(128)(4,1)S(1)} %and_reduce_fusion), kind=kLoop, calls=%fused_computation.8 | loop fusion | flops 1179648 | bytes 4718624 | tf_op jit(solution)/shard_map/jit(_take)/select_n | solution.py:105
  21.0 12.3 %all-to-all-start = ((bf16[32,4,16,576]{3,1,2,0:T(4,128)(2,1)}), bf16[32,4,16,576]{3,1,2,0:T(4,128)(2,1)}, u32[]{:S(2)}, u32[]{:S(2)}) async-start(bf16[32,4,16,576]{3,1,2,0:T(4,128)(2,1)} %broadcast_select_fusion), calls=%async_computation | async-start | bytes 5242880 | tf_op jit(solution)/shard_map/all_to_all | solution.py:106
  33.3 0.8 select_reduce_fusion.1
  34.1 0.2 select_reduce_fusion
  34.3 0.1 iota_compare_fusion.1
  34.4 58.8 %all-to-all-done = bf16[32,4,16,576]{3,1,2,0:T(4,128)(2,1)} async-done(((bf16[32,4,16,576]{3,1,2,0:T(4,128)(2,1)}), bf16[32,4,16,576]{3,1,2,0:T(4,128)(2,1)}, u32[]{:S(2)}, u32[]{:S(2)}) %all-to-all-start) | async-done | bytes 2359328 | tf_op jit(solution)/shard_map/all_to_all | solution.py:106
  93.2 9.1 %fusion.13 = (f32[32,4,16]{2,1,0:T(4,128)}, f32[32,4,16,192]{3,2,1,0:T(8,128)}) fusion(pred[32,192]{1,0:T(8,128)(4,1)S(1)} %iota_compare_fusion.1, bf16[32,192,576]{2,1,0:T(8,128)(2,1)} %param.10, bf16[32,4,16,576]{3,1,2,0:T(4,128)(2,1)} %all-to-all-done), kind=kOutput, calls=%fused_computation.18 | convolution fusion | flops 454162432 | bytes 11024384 | tf_op jit(solution)/shard_map/nshk,ntk->nsht/dot_general | solution.py:37
  102.3 7.4 %all-to-all-start.3 = ((f32[32,4,16]{2,1,0:T(4,128)}), f32[32,4,16]{2,1,0:T(4,128)S(1)}, u32[]{:S(2)}, u32[]{:S(2)}) async-start(f32[32,4,16]{2,1,0:T(4,128)} %get-tuple-element.11), calls=%async_computation.3 | async-start | bytes 131072 | tf_op jit(solution)/shard_map/all_to_all | solution.py:113
  109.7 3.1 fusion.14
  112.7 5.8 %all-to-all-done.3 = f32[32,4,16]{2,1,0:T(4,128)S(1)} async-done(((f32[32,4,16]{2,1,0:T(4,128)}), f32[32,4,16]{2,1,0:T(4,128)S(1)}, u32[]{:S(2)}, u32[]{:S(2)}) %all-to-all-start.3) | async-done | bytes 8224 | tf_op jit(solution)/shard_map/all_to_all | solution.py:113
  118.5 3.9 %all-to-all-start.2 = ((f32[32,4,16]{2,1,0:T(4,128)}), f32[32,4,16]{2,1,0:T(4,128)S(1)}, u32[]{:S(2)}, u32[]{:S(2)}) async-start(f32[32,4,16]{2,1,0:T(4,128)} %fusion.14), calls=%async_computation.2 | async-start | bytes 131072 | tf_op jit(solution)/shard_map/all_to_all | solution.py:114
  122.4 6.5 %divide_convert_fusion = bf16[32,4,16,512]{3,2,1,0:T(8,128)(2,1)} fusion(f32[32,4,16]{2,1,0:T(4,128)} %fusion.14, bf16[32,192,576]{2,1,0:T(8,128)(2,1)} %param.10, f32[32,4,16,192]{3,2,1,0:T(8,128)} %get-tuple-element.12, f32[32,4,16]{2,1,0:T(4,128)} %get-tuple-element.11, pred[32,192]{1,0:T(8,128)(4,1)S(1)} %iota_compare_fusion.1), kind=kOutput, calls=%fused_computation.6 | convolution fusion | flops 406323200 | bytes 10622976 | tf_op jit(solution)/shard_map/nsht,ntl->nshl/dot_general | solution.py:45
  128.8 2.5 all-to-all-done.2
  131.3 7.0 %all-to-all-start.1 = ((bf16[32,4,16,512]{3,2,1,0:T(8,128)(2,1)}), bf16[32,4,16,512]{3,2,1,0:T(8,128)(2,1)}, u32[]{:S(2)}, u32[]{:S(2)}) async-start(bf16[32,4,16,512]{3,2,1,0:T(8,128)(2,1)} %divide_convert_fusion), calls=%async_computation.1 | async-start | bytes 4194304 | tf_op jit(solution)/shard_map/all_to_all | solution.py:110
  138.3 0.2 all-gather.2.cloned.1.call-start
  138.6 0.4 fusion.61
  139.0 0.4 fusion.8
  139.4 0.1 copy.93
  139.4 0.1 select_reduce_fusion.2
  139.6 0.1 copy.96
  139.7 0.1 copy.92
  139.8 0.3 fusion.59
  140.1 0.1 copy.100
  140.2 0.1 copy.101
  140.3 0.1 copy.97
  140.4 0.1 copy.98
  140.5 0.3 fusion.62
  140.9 45.8 %all-to-all-done.1 = bf16[32,4,16,512]{3,2,1,0:T(8,128)(2,1)} async-done(((bf16[32,4,16,512]{3,2,1,0:T(8,128)(2,1)}), bf16[32,4,16,512]{3,2,1,0:T(8,128)(2,1)}, u32[]{:S(2)}, u32[]{:S(2)}) %all-to-all-start.1) | async-done | bytes 2097184 | tf_op jit(solution)/shard_map/all_to_all | solution.py:110
  186.7 4.1 %fusion.21 = bf16[32,4,16,128]{3,0,2,1:T(8,128)(2,1)S(1)} fusion(bf16[16,512,128]{2,1,0:T(8,128)(2,1)S(1)} %copy-done, bf16[32,4,16,512]{3,2,1,0:T(8,128)(2,1)} %all-to-all-done.1), kind=kOutput, calls=%fused_computation.22 | convolution fusion | flops 268697600 | bytes 4718592 | tf_op jit(solution)/shard_map/nshl,hlc->nshc/dot_general | solution.py:55
  190.7 0.0 copy-start.5
  190.7 0.6 fusion.37
  191.4 0.6 reshape.103
  192.0 0.0 all-gather.2.cloned.1.call-update
  192.0 0.0 all-reduce.3.cloned.1.call-start
  192.1 71.5 %all-gather.2.cloned.1.call-done = bf16[64,4,2048]{2,1,0:T(4,128)(2,1)} async-done(((bf16[2,4,2048]{2,1,0:T(4,128)(2,1)}), bf16[64,4,2048]{2,1,0:T(4,128)(2,1)}) %all-gather.2.cloned.1.call-update) | async-done | bytes 1048592 | tf_op jit(solution)/shard_map/all_gather | solution.py:143
  263.6 3.2 convolution_convert_fusion
  266.8 0.0 all-reduce.3.cloned.1.call-update
  266.8 0.6 dynamic-slice
  268.0 63.1 %all-reduce.3.cloned.1.call-done = bf16[64,4,224]{2,0,1:T(8,128)(2,1)} async-done(((bf16[64,4,224]{2,0,1:T(8,128)(2,1)}), bf16[64,4,224]{2,0,1:T(8,128)(2,1)}) %all-reduce.3.cloned.1.call-update) | async-done | bytes 114704
  331.2 0.7 constant_dynamic-slice_fusion.2
  331.9 0.6 copy.104
  (21 shorter events, 0.1 us)
Async XLA Ops:
  6.5 132.4 %copy-start = (bf16[16,512,128]{2,1,0:T(8,128)(2,1)S(1)}, bf16[16,512,128]{2,1,0:T(8,128)(2,1)}, u32[]{:S(2)}) copy-start(bf16[16,512,128]{2,1,0:T(8,128)(2,1)} %param.12) | copy-start | bytes 6291460
  21.0 12.3 %copy-start.1 = (s32[32,32]{1,0:T(8,128)S(1)}, s32[32,32]{1,0:T(8,128)}, u32[]{:S(2)}) copy-start(s32[32,32]{1,0:T(8,128)} %param.14) | copy-start | bytes 12292
  21.0 12.3 %copy-start.3 = (s32[64]{0:T(128)S(1)}, s32[64]{0:T(128)}, u32[]{:S(2)}) copy-start(s32[64]{0:T(128)} %param.15) | copy-start | bytes 772
  21.0 72.2 %all-to-all-start = ((bf16[32,4,16,576]{3,1,2,0:T(4,128)(2,1)}), bf16[32,4,16,576]{3,1,2,0:T(4,128)(2,1)}, u32[]{:S(2)}, u32[]{:S(2)}) async-start(bf16[32,4,16,576]{3,1,2,0:T(4,128)(2,1)} %broadcast_select_fusion), calls=%async_computation | async-start | bytes 5242880 | tf_op jit(solution)/shard_map/all_to_all | solution.py:106
  102.3 16.2 %all-to-all-start.3 = ((f32[32,4,16]{2,1,0:T(4,128)}), f32[32,4,16]{2,1,0:T(4,128)S(1)}, u32[]{:S(2)}, u32[]{:S(2)}) async-start(f32[32,4,16]{2,1,0:T(4,128)} %get-tuple-element.11), calls=%async_computation.3 | async-start | bytes 131072 | tf_op jit(solution)/shard_map/all_to_all | solution.py:113
  118.5 12.8 %all-to-all-start.2 = ((f32[32,4,16]{2,1,0:T(4,128)}), f32[32,4,16]{2,1,0:T(4,128)S(1)}, u32[]{:S(2)}, u32[]{:S(2)}) async-start(f32[32,4,16]{2,1,0:T(4,128)} %fusion.14), calls=%async_computation.2 | async-start | bytes 131072 | tf_op jit(solution)/shard_map/all_to_all | solution.py:114
  128.8 9.8 %copy-start.2 = (bf16[2,4,576]{2,1,0:T(4,128)(2,1)S(1)}, bf16[2,4,576]{2,1,0:T(4,128)(2,1)}, u32[]{:S(2)}) copy-start(bf16[2,4,576]{2,1,0:T(4,128)(2,1)} %param.9) | copy-start | bytes 27652
  131.3 55.3 %all-to-all-start.1 = ((bf16[32,4,16,512]{3,2,1,0:T(8,128)(2,1)}), bf16[32,4,16,512]{3,2,1,0:T(8,128)(2,1)}, u32[]{:S(2)}, u32[]{:S(2)}) async-start(bf16[32,4,16,512]{3,2,1,0:T(8,128)(2,1)} %divide_convert_fusion), calls=%async_computation.1 | async-start | bytes 4194304 | tf_op jit(solution)/shard_map/all_to_all | solution.py:110
  138.3 125.2 %all-gather.2.cloned.1.call-start = ((), (), s32[]{:S(2)}) async-start(), calls=%async_computation.4 | async-start | bytes 1081344 | tf_op jit(solution)/shard_map/all_gather | solution.py:143
  190.7 72.8 %copy-start.4 = (bf16[2048,224]{0,1:T(8,128)(2,1)S(1)}, bf16[2048,224]{0,1:T(8,128)(2,1)}, u32[]{:S(2)}) copy-start(bf16[2048,224]{0,1:T(8,128)(2,1)} %param.13) | copy-start | bytes 2752516
  190.7 76.1 %copy-start.5 = (u32[256]{0:T(256)S(1)}, u32[256]{0:T(256)}, u32[]{:S(2)}) copy-start(u32[256]{0:T(256)} %constant.43) | copy-start | bytes 3076
  192.0 139.1 %all-reduce.3.cloned.1.call-start = ((), (), s32[]{:S(2)}) async-start(), calls=%async_computation.5 | async-start | bytes 262144
Sparse Core Ops, SparseCore 0:
  192.1 71.3 all-gather.1
  266.9 64.2 all-reduce.2
where the time goes:
time: 341 us; the launch traced here: 339 us
  waiting for transfers between devices  247 us (72%)
  starting transfers between devices  30.8 us (9%)
  matrix products  26.5 us (8%)
  between operations  14.3 us (4%)
  other arithmetic  11.2 us (3%)
  local copies, waits for them, and re-layouts  9.11 us (3%)
    all_gather x1, waiting for transfers between devices, body(): lax.all_gather(flattened, 'lender', axis=0, tiled=True)  71.5 us
    unnamed x3, waiting for transfers between devices  63.2 us
    all_to_all x1, waiting for transfers between devices, body(): lax.all_to_all(outgoing, 'lender', split_axis=0, concat_axis=0, tiled=True)  58.8 us
    all_to_all x1, waiting for transfers between devices, body(): lax.all_to_all(slot_mean, 'lender', split_axis=0, concat_axis=0, tiled=True)  45.8 us
    all_to_all x1, starting transfers between devices, body(): lax.all_to_all(outgoing, 'lender', split_axis=0, concat_axis=0, tiled=True)  12.3 us
    dot_general x1, matrix products, slot_partials(): jnp.einsum('nshk,ntk->nsht', queries, blocks, preferred_element_type=jnp....  9.07 us
    all_to_all x1, starting transfers between devices, body(): lax.all_to_all(slot_top, 'lender', split_axis=0, concat_axis=0, tiled=True)  7.37 us
    all_to_all x1, starting transfers between devices, body(): lax.all_to_all(slot_mean, 'lender', split_axis=0, concat_axis=0, tiled=True)  7.01 us
  transfers between devices with their start and end apart: 6, of which 6 were waited for; matrix products, arithmetic and copies ran while one was open for 4% of the time, Pallas kernels for 0%

commit v1 on v0

v1 whole, which is shorter than its diff:
```python
import math

import jax
import jax.numpy as jnp
from jax import lax
from jax.sharding import PartitionSpec as P

MSCALE_SQ = (0.1 * math.log(40.0) + 1.0) ** 2
NEG_FILL = -1e30
BF16 = jnp.bfloat16
F32 = jnp.float32


def live_tokens(slot_request, context_lengths, slot_tokens):
    lenders = slot_request.shape[0]
    owners = jnp.arange(context_lengths.shape[0], dtype=jnp.int32)
    lengths = jnp.sum(
        jnp.where(
            slot_request[:, :, None] == owners[None, None, :], context_lengths[None, None, :], 0
        ),
        axis=-1,
    )
    matching = slot_request[:, None, :] == slot_request[None, :, :]
    before = jnp.arange(lenders)[:, None] < jnp.arange(lenders)[None, :]
    slot_rank = jnp.sum(jnp.where(matching & before[:, :, None], 1, 0), axis=0)
    return jnp.clip(lengths - slot_tokens * slot_rank, 0, slot_tokens)


def three_parts(x):
    high = lax.reduce_precision(x, 8, 7)
    rest = x - high
    middle = lax.reduce_precision(rest, 8, 7)
    return high.astype(BF16), middle.astype(BF16), (rest - middle).astype(BF16)


def body(
    draft_queries,
    draft_latents,
    latent_pool,
    key_absorb,
    value_absorb,
    out_proj,
    slot_request,
    context_lengths,
):
    home = lax.axis_index("lender")
    reqs, drafts, heads, width = draft_queries.shape
    nope, latent = key_absorb.shape[1:]
    rope = width - nope
    slots, tokens = latent_pool.shape[:2]
    vhead = value_absorb.shape[-1]
    rows = heads * drafts
    scale = width ** (-0.5) * MSCALE_SQ

    column = lax.dynamic_slice_in_dim(slot_request, home, 1, 1)[:, 0]
    local = column - home * reqs
    q = jnp.swapaxes(draft_queries, 1, 2).reshape(reqs, rows, width)
    q_rope = q[:, :, nope:]
    packed = jnp.concatenate(
        [q[:, :, :nope], jnp.concatenate([q_rope[:, : rows // 2], q_rope[:, rows // 2 :]], -1)], 1
    )
    outgoing = packed[0][None]
    for i in range(1, reqs):
        outgoing = jnp.where((local == i)[:, None, None], packed[i][None], outgoing)
    arrived = lax.all_to_all(outgoing, "lender", split_axis=0, concat_axis=0, tiled=True)

    def absorb(nope_part, rope_part):
        n = nope_part.shape[0]
        part = jnp.einsum(
            "nhsc,hcl->nhsl",
            nope_part.reshape(n, heads, drafts, nope),
            key_absorb,
            preferred_element_type=F32,
        ).astype(BF16)
        return jnp.concatenate([part.reshape(n, rows, latent), rope_part], -1)

    live_all = live_tokens(slot_request, context_lengths, tokens)
    live_here = lax.dynamic_slice_in_dim(live_all, home, 1, 0)[0]
    arrived_rope = arrived[:, rows:]
    queries = absorb(
        arrived[:, :rows],
        jnp.concatenate([arrived_rope[:, :, :rope], arrived_rope[:, :, rope:]], 1),
    )
    scores = jnp.einsum("nrk,ntk->nrt", queries, latent_pool, preferred_element_type=F32) * scale
    usable = jnp.arange(tokens)[None, :] < live_here[:, None]
    scores = jnp.where(usable[:, None, :], scores, NEG_FILL)
    top = jnp.max(scores, axis=-1)
    weights = jnp.exp(scores - top[..., None])
    total = jnp.sum(weights, axis=-1)
    weighted = jnp.einsum(
        "nrt,ntl->nrl",
        weights.astype(BF16),
        latent_pool[:, :, :latent],
        preferred_element_type=F32,
    )
    mean = (weighted / total[..., None]).astype(BF16)
    value = jnp.einsum(
        "nhsl,hlc->nhsc",
        mean.reshape(slots, heads, drafts, latent),
        value_absorb,
        preferred_element_type=F32,
    ).astype(BF16)
    mass = jnp.stack(three_parts(top + jnp.log(total)), axis=1)
    mass = jnp.pad(mass, ((0, 0), (0, 16 - 3), (0, vhead - rows)))
    sending = jnp.concatenate([value.reshape(slots, rows, vhead), mass], axis=1)
    back = lax.all_to_all(sending, "lender", split_axis=0, concat_axis=0, tiled=True)

    own = absorb(q[:, :, :nope], q_rope)
    draft_scores = (
        jnp.einsum("irk,ijk->irj", own, draft_latents, preferred_element_type=F32) * scale
    )
    causal = (jnp.arange(rows) % drafts)[:, None] >= jnp.arange(drafts)[None, :]
    draft_scores = jnp.where(causal[None], draft_scores, NEG_FILL)
    draft_values = jnp.einsum(
        "ijl,hlc->ijhc", draft_latents[:, :, :latent], value_absorb, preferred_element_type=F32
    )
    mass_back = jnp.sum(back[:, rows : rows + 3, :rows].astype(F32), axis=1)
    value_back = back[:, :rows].astype(F32)
    member = (local[:, None] == jnp.arange(reqs)[None, :])[:, :, None]
    mass_of = jnp.where(member, mass_back[:, None], NEG_FILL)
    row_top = jnp.maximum(jnp.max(mass_of, axis=0), jnp.max(draft_scores, axis=-1))
    weight = jnp.where(member, jnp.exp(mass_of - row_top[None]), 0.0)
    draft_weight = jnp.exp(draft_scores - row_top[..., None])
    numerator = jnp.sum(weight[..., None] * value_back[:, None], axis=0)
    numerator = numerator + jnp.sum(
        draft_weight.reshape(reqs, heads, drafts, drafts)[..., None]
        * jnp.swapaxes(draft_values, 1, 2)[:, :, None],
        axis=3,
    ).reshape(reqs, rows, vhead)
    denominator = jnp.sum(weight, axis=0) + jnp.sum(draft_weight, axis=-1)
    out = (numerator / denominator[..., None]).astype(BF16)
    out = jnp.swapaxes(out.reshape(reqs, heads, drafts, vhead), 1, 2)
    out = out.reshape(reqs * drafts, heads * vhead)

    copies = jnp.broadcast_to(out[None], (slots,) + out.shape)
    everyone = lax.all_to_all(copies, "lender", split_axis=0, concat_axis=0, tiled=True)
    partial = jnp.dot(
        everyone.reshape(-1, heads * vhead), out_proj, preferred_element_type=F32
    ).astype(BF16)
    parts = lax.axis_size("tensor")
    terms = lax.all_to_all(
        partial.reshape(parts, -1, partial.shape[-1]), "tensor", split_axis=0, concat_axis=0
    )
    mixed = jnp.sum(terms.astype(F32), axis=0).astype(BF16)
    return mixed.reshape(-1, drafts, partial.shape[-1])


def solution(mesh):
    in_specs = (
        P("lender", None, "tensor", None),
        P("lender", None, None),
        P("lender", None, None),
        P("tensor", None, None),
        P("tensor", None, None),
        P("tensor", "lender"),
        P(),
        P(),
    )
    out_specs = P("tensor", None, "lender")
    return jax.shard_map(body, mesh=mesh, in_specs=in_specs, out_specs=out_specs, check_vma=False)
```

time: 341 us -> 125 us (0.37)
  waiting for transfers between devices: 247 us -> 31.9 us
  blocking collectives: 0 us -> 46.8 us
  between operations: 14.3 us -> 0.45 us
  matrix products: 26.5 us -> 12.8 us
  starting transfers between devices: 30.8 us -> 20.4 us
  other arithmetic: 11.2 us -> 6.74 us
    all_gather x1 -> x0, waiting for transfers between devices: 71.5 us -> none  [body(): lax.all_gather(flattened, 'lender', axis=0, tiled=True)]
    unnamed x3 -> x0, waiting for transfers between devices: 63.2 us -> none
    all_to_all x0 -> x2, blocking collectives: none -> 46.8 us  [the longest x1 32.1 us: body(): lax.all_to_all(copies, 'lender', split_axis=0, concat_axis=0, tiled=True)]
    all_to_all x1, waiting for transfers between devices: 58.8 us -> 18.1 us  [body(): lax.all_to_all(outgoing, 'lender', split_axis=0, concat_axis=0, tiled=True)]
    all_to_all x3 -> x1, waiting for transfers between devices: 54 us -> 13.8 us  [body(): lax.all_to_all(sending, 'lender', split_axis=0, concat_axis=0, tiled=True)]
    dot_general x9 -> x8, matrix products: 26.5 us -> 12.8 us  [the longest x1 6.32 us: body(): jnp.einsum('nrk,ntk->nrt', queries, latent_pool, preferred_element_type=F32)]
    all_to_all x3 -> x1, starting transfers between devices: 18.2 us -> 8.36 us  [body(): lax.all_to_all(sending, 'lender', split_axis=0, concat_axis=0, tiled=True)]
    gather x1 -> x0, local copies, waits for them, and re-layouts: 4.33 us -> none  [body(): outgoing = jnp.take(absorbed, local_rows, axis=0)]
  transfers between devices with their start and end apart: 6 -> 2, of which waited for: 6 -> 2; matrix products, arithmetic and copies ran while one was open for 4% -> 3% of each run, Pallas kernels for 0% -> 0%
where the time goes in v1:
time: 125 us
  blocking collectives  46.8 us (37%)
  waiting for transfers between devices  31.9 us (26%)
  starting transfers between devices  20.4 us (16%)
  matrix products  12.8 us (10%)
  other arithmetic  6.74 us (5%)
  local copies, waits for them, and re-layouts  6.01 us (5%)
    all_to_all x1, blocking collectives, body(): lax.all_to_all(copies, 'lender', split_axis=0, concat_axis=0, tiled=True)  32.1 us
    all_to_all x1, waiting for transfers between devices, body(): lax.all_to_all(outgoing, 'lender', split_axis=0, concat_axis=0, tiled=True)  18.1 us
    all_to_all x1, blocking collectives, body(): lax.all_to_all(partial.reshape(parts, -1, partial.shape[-1]), 'tensor', s...  14.7 us
    all_to_all x1, waiting for transfers between devices, body(): lax.all_to_all(sending, 'lender', split_axis=0, concat_axis=0, tiled=True)  13.8 us
    all_to_all x1, starting transfers between devices, body(): lax.all_to_all(outgoing, 'lender', split_axis=0, concat_axis=0, tiled=True)  12 us
    all_to_all x1, starting transfers between devices, body(): lax.all_to_all(sending, 'lender', split_axis=0, concat_axis=0, tiled=True)  8.36 us
    dot_general x1, matrix products, body(): jnp.einsum('nrk,ntk->nrt', queries, latent_pool, preferred_element_type=F32)  6.32 us
  transfers between devices with their start and end apart: 2, of which 2 were waited for; matrix products, arithmetic and copies ran while one was open for 3% of the time, Pallas kernels for 0%

profile of v1, /device:TPU:1, one launch (start us, length us, event | category | flops | bytes accessed | tf_op | source)
XLA Modules:
  0.0 125.0 jit_solution(16106991252954836861)
XLA Ops:
  0.0 1.0 copy.62
  1.1 0.1 maximum_maximum_fusion
  1.2 0.9 compare_reduce_fusion
  2.1 1.0 broadcast_select_fusion
  3.1 12.0 %all-to-all-start = ((bf16[32,96,128]{2,1,0:T(8,128)(2,1)}), bf16[32,96,128]{2,1,0:T(8,128)(2,1)S(1)}, u32[]{:S(2)}, u32[]{:S(2)}) async-start(bf16[32,96,128]{2,1,0:T(8,128)(2,1)} %broadcast_select_fusion), calls=%async_computation | async-start | bytes 1572864 | tf_op jit(solution)/shard_map/all_to_all | solution.py:65
  15.2 0.8 select_reduce_fusion.1
  16.0 0.2 select_reduce_fusion
  16.2 0.1 iota_compare_fusion.2
  16.3 18.1 %all-to-all-done = bf16[32,96,128]{2,1,0:T(8,128)(2,1)S(1)} async-done(((bf16[32,96,128]{2,1,0:T(8,128)(2,1)}), bf16[32,96,128]{2,1,0:T(8,128)(2,1)S(1)}, u32[]{:S(2)}, u32[]{:S(2)}) %all-to-all-start) | async-done | bytes 786464 | tf_op jit(solution)/shard_map/all_to_all | solution.py:65
  34.5 0.3 copy.63
  34.9 0.7 fusion.16
  35.6 1.2 copy.64
  36.7 0.1 fusion.67
  36.9 0.0 slice-start.1
  36.9 6.3 %fusion.19 = (f32[32,64]{1,0:T(8,128)S(1)}, f32[32,64,192]{2,1,0:T(8,128)S(1)}) fusion(pred[32,192]{1,0:T(8,128)(4,1)S(1)} %iota_compare_fusion.2, bf16[32,192,576]{2,1,0:T(8,128)(2,1)} %param.10, bf16[32,32,64]{2,1,0:T(8,128)(2,1)S(1)} %get-tuple-element.8, bf16[32,32,64]{2,1,0:T(8,128)(2,1)S(1)} %get-tuple-element.7, bf16[32,64,512]{2,1,0:T(8,128)(2,1)S(1)} %copy.64), kind=kOutput, calls=%fused_computation.21 | convolution fusion | flops 461240320 | bytes 11024384 | tf_op jit(solution)/shard_map/nrk,ntk->nrt/dot_general | solution.py:84
  43.2 1.2 fusion.20
  44.5 2.0 %divide_convert_fusion = bf16[32,64,512]{2,1,0:T(8,128)(2,1)S(1)} fusion(f32[32,64]{1,0:T(8,128)S(1)} %fusion.20, bf16[32,192,576]{2,1,0:T(8,128)(2,1)S(1)} %bitcast.87, f32[32,64,192]{2,1,0:T(8,128)S(1)} %get-tuple-element.19, f32[32,64]{1,0:T(8,128)S(1)} %get-tuple-element.18, pred[32,192]{1,0:T(8,128)(4,1)S(1)} %iota_compare_fusion.2), kind=kOutput, calls=%fused_computation.2 | convolution fusion | flops 406323200 | bytes 10526720 | tf_op jit(solution)/shard_map/nrt,ntl->nrl/dot_general | solution.py:90
  46.5 0.0 copy-start.1
  46.5 1.2 copy.80
  47.7 0.4 copy-done.1
  48.1 0.7 fusion.23
  48.8 0.0 copy-start.5
  48.8 0.2 copy.66
  49.1 0.9 fusion.44
  49.9 8.4 %all-to-all-start.1 = ((bf16[32,80,128]{2,1,0:T(8,128)(2,1)}), bf16[32,80,128]{2,1,0:T(8,128)(2,1)S(1)}, u32[]{:S(2)}, u32[]{:S(2)}) async-start(bf16[32,80,128]{2,1,0:T(8,128)(2,1)} %fusion.44), calls=%async_computation.1 | async-start | bytes 1310720 | tf_op jit(solution)/shard_map/all_to_all | solution.py:106
  58.3 2.0 %fusion.34 = f32[2,16,4,128]{3,2,1,0:T(4,128)S(1)} fusion(bf16[16,512,128]{2,1,0:T(8,128)(2,1)} %param.12, bf16[2,4,576]{2,1,0:T(4,128)(2,1)S(1)} %copy-done.5), kind=kOutput, calls=%fused_computation.30 | convolution fusion | flops 16777216 | bytes 2170880 | tf_op jit(solution)/shard_map/ijl,hlc->ijhc/dot_general | solution.py:114
  60.3 0.4 fusion.31
  60.7 0.1 copy.69
  60.9 0.2 fusion.54
  61.1 0.2 fusion.69
  61.3 13.8 %all-to-all-done.1 = bf16[32,80,128]{2,1,0:T(8,128)(2,1)S(1)} async-done(((bf16[32,80,128]{2,1,0:T(8,128)(2,1)}), bf16[32,80,128]{2,1,0:T(8,128)(2,1)S(1)}, u32[]{:S(2)}, u32[]{:S(2)}) %all-to-all-start.1) | async-done | bytes 655392 | tf_op jit(solution)/shard_map/all_to_all | solution.py:106
  75.1 0.1 select_reduce_fusion.2
  75.2 0.1 fusion.65
  75.3 0.1 add.57
  75.4 0.1 copy.75
  75.6 0.1 mul.56
  75.7 0.1 copy.72
  75.8 0.1 multiply_reduce_fusion.1
  75.9 0.1 slice_convert_fusion
  76.0 0.0 copy-start.2
  76.1 0.7 multiply_reduce_fusion
  76.8 0.1 fusion.49
  76.9 0.1 broadcast_in_dim.153
  77.0 32.1 %all_to_all.20 = bf16[32,8,2048]{2,1,0:T(8,128)(2,1)S(1)} all-to-all(bf16[32,8,2048]{2,1,0:T(8,128)(2,1)S(1)} %broadcast_in_dim.153), channel_id=1, replica_groups=mesh['lender'=32,'tensor'=8] {'lender'}, dimensions={0} | all-to-all | bytes 2097152 | tf_op jit(solution)/shard_map/all_to_all | solution.py:136
  109.1 0.5 convolution_convert_fusion
  109.6 0.1 copy.76
  109.7 14.7 %all_to_all.21 = bf16[8,32,224]{2,1,0:T(8,128)(2,1)S(1)} all-to-all(bf16[8,32,224]{2,1,0:T(8,128)(2,1)S(1)} %bitcast.80), channel_id=1, replica_groups=mesh['lender'=32,'tensor'=8] {'tensor'}, dimensions={0} | all-to-all | bytes 229376 | tf_op jit(solution)/shard_map/all_to_all | solution.py:141
  124.4 0.6 reshape.222
  (38 shorter events, 0.4 us)
Async XLA Ops:
  0.0 34.9 %copy-start = (bf16[16,128,512]{2,1,0:T(8,128)(2,1)S(1)}, bf16[16,128,512]{2,1,0:T(8,128)(2,1)}, u32[]{:S(2)}) copy-start(bf16[16,128,512]{2,1,0:T(8,128)(2,1)} %param.11) | copy-start | bytes 6291460
  0.0 15.2 %copy-start.4 = (s32[32,32]{1,0:T(8,128)S(1)}, s32[32,32]{1,0:T(8,128)}, u32[]{:S(2)}) copy-start(s32[32,32]{1,0:T(8,128)} %param.14) | copy-start | bytes 12292
  0.0 15.2 %copy-start.6 = (s32[64]{0:T(128)S(1)}, s32[64]{0:T(128)}, u32[]{:S(2)}) copy-start(s32[64]{0:T(128)} %param.15) | copy-start | bytes 772
  1.1 33.8 %copy-start.3 = (bf16[2,64,192]{2,1,0:T(8,128)(2,1)}, bf16[2,64,192]{2,1,0:T(8,128)(2,1)S(1)}, u32[]{:S(2)}) copy-start(bf16[2,64,192]{2,1,0:T(8,128)(2,1)S(1)} %reshape.213) | copy-start | bytes 147460
  3.1 31.3 %all-to-all-start = ((bf16[32,96,128]{2,1,0:T(8,128)(2,1)}), bf16[32,96,128]{2,1,0:T(8,128)(2,1)S(1)}, u32[]{:S(2)}, u32[]{:S(2)}) async-start(bf16[32,96,128]{2,1,0:T(8,128)(2,1)} %broadcast_select_fusion), calls=%async_computation | async-start | bytes 1572864 | tf_op jit(solution)/shard_map/all_to_all | solution.py:65
  36.9 7.6 %slice-start.1 = ((s8[7864320]{0:T(1024)(128)(4,1)}), s8[4194304]{0:T(1024)(128)(4,1)S(1)}, s32[]{:S(2)}) async-start(s8[7864320]{0:T(1024)(128)(4,1)} %bitcast.86), calls=%async_computation.5 | async-start | bytes 8388608
  36.9 7.5 %slice-start.2 = ((s8[7864320]{0:T(1024)(128)(4,1)}), s8[3670016]{0:T(1024)(128)(4,1)S(1)}, s32[]{:S(2)}) async-start(s8[7864320]{0:T(1024)(128)(4,1)} %bitcast.86), calls=%async_computation.6 | async-start | bytes 7340032
  46.5 1.6 %copy-start.1 = (bf16[16,512,128]{2,1,0:T(8,128)(2,1)S(1)}, bf16[16,512,128]{2,1,0:T(8,128)(2,1)}, u32[]{:S(2)}) copy-start(bf16[16,512,128]{2,1,0:T(8,128)(2,1)} %param.12) | copy-start | bytes 6291460
  48.8 9.5 %copy-start.5 = (bf16[2,4,576]{2,1,0:T(4,128)(2,1)S(1)}, bf16[2,4,576]{2,1,0:T(4,128)(2,1)}, u32[]{:S(2)}) copy-start(bf16[2,4,576]{2,1,0:T(4,128)(2,1)} %param.9) | copy-start | bytes 27652
  49.9 25.1 %all-to-all-start.1 = ((bf16[32,80,128]{2,1,0:T(8,128)(2,1)}), bf16[32,80,128]{2,1,0:T(8,128)(2,1)S(1)}, u32[]{:S(2)}, u32[]{:S(2)}) async-start(bf16[32,80,128]{2,1,0:T(8,128)(2,1)} %fusion.44), calls=%async_computation.1 | async-start | bytes 1310720 | tf_op jit(solution)/shard_map/all_to_all | solution.py:106
  58.3 2.8 %slice-start = ((bf16[2,64,192]{2,1,0:T(8,128)(2,1)}), bf16[2,64,64]{2,1,0:T(8,128)(2,1)S(1)}, s32[]{:S(2)}) async-start(bf16[2,64,192]{2,1,0:T(8,128)(2,1)} %copy-done.3), calls=%async_computation.4 | async-start | bytes 65536 | tf_op jit(solution)/shard_map/slice | solution.py:58
  76.0 33.1 %copy-start.2 = (bf16[2048,224]{0,1:T(8,128)(2,1)S(1)}, bf16[2048,224]{0,1:T(8,128)(2,1)}, u32[]{:S(2)}) copy-start(bf16[2048,224]{0,1:T(8,128)(2,1)} %param.13) | copy-start | bytes 2752516

commit v2 on v1

v2 whole, which is shorter than its diff:
```python
import functools
import math

import jax
import jax.numpy as jnp
from jax import lax
from jax.experimental import pallas as pl
from jax.experimental.pallas import tpu as pltpu
from jax.sharding import PartitionSpec as P

MSCALE_SQ = (0.1 * math.log(40.0) + 1.0) ** 2
NEG_FILL = -1e30
BF16 = jnp.bfloat16
F32 = jnp.float32
PARTS = 3


def live_tokens(slot_request, context_lengths, slot_tokens):
    lenders = slot_request.shape[0]
    owners = jnp.arange(context_lengths.shape[0], dtype=jnp.int32)
    lengths = jnp.sum(
        jnp.where(
            slot_request[:, :, None] == owners[None, None, :], context_lengths[None, None, :], 0
        ),
        axis=-1,
    )
    matching = slot_request[:, None, :] == slot_request[None, :, :]
    before = jnp.arange(lenders)[:, None] < jnp.arange(lenders)[None, :]
    slot_rank = jnp.sum(jnp.where(matching & before[:, :, None], 1, 0), axis=0)
    return jnp.clip(lengths - slot_tokens * slot_rank, 0, slot_tokens)


def pack_kernel(
    home_ref, slot_request_ref, queries_ref, out_ref, nope_ref, rope_ref, packed_ref, sems
):
    reqs, drafts, heads, width = queries_ref.shape
    nope = nope_ref.shape[-1]
    half = heads * drafts // 2
    for i in range(reqs):
        for s in range(drafts):
            x = queries_ref[i, s].astype(F32)
            nope_ref[pl.ds(s, heads, stride=drafts), :] = x[:, :nope]
            rope_ref[pl.ds(s, heads, stride=drafts), :] = x[:, nope:]
        rope = rope_ref[...]
        rope = jnp.concatenate([rope[:half], rope[half:]], 1)
        packed_ref[i] = jnp.concatenate([nope_ref[...], rope], 0).astype(BF16)
    home = home_ref[0]
    copies = [
        pltpu.make_async_copy(
            packed_ref.at[jnp.clip(slot_request_ref[d, home] - home * reqs, 0, reqs - 1)],
            out_ref.at[d],
            sems.at[d],
        )
        for d in range(out_ref.shape[0])
    ]
    for copy in copies:
        copy.start()
    for copy in copies:
        copy.wait()


def pack(home, slot_request, queries, nope):
    reqs, drafts, heads, width = queries.shape
    rows = heads * drafts
    smem = pl.BlockSpec(memory_space=pltpu.SMEM)
    vmem = pl.BlockSpec(memory_space=pltpu.VMEM)
    slots = slot_request.shape[0]
    return pl.pallas_call(
        pack_kernel,
        out_shape=pltpu.HBM((slots, rows + rows // 2, nope), BF16),
        in_specs=[smem, smem, vmem],
        out_specs=pl.BlockSpec(memory_space=pltpu.HBM),
        scratch_shapes=[
            pltpu.VMEM((rows, nope), F32),
            pltpu.VMEM((rows, width - nope), F32),
            pltpu.VMEM((reqs, rows + rows // 2, nope), BF16),
            pltpu.SemaphoreType.DMA((slots,)),
        ],
        name="pack",
    )(home, slot_request, queries)


def lend_kernel(
    scale,
    group,
    live_ref,
    arrived_any,
    keys_ref,
    values_any,
    pool_any,
    out_any,
    out_ref,
    arrived_ref,
    values_ref,
    pool_ref,
    query_ref,
    mean_ref,
    sems,
):
    slots, _, nope = arrived_ref.shape
    heads, _, latent = keys_ref.shape
    vhead = values_ref.shape[-1]
    rows, width = query_ref.shape[1:]
    drafts = rows // heads
    rope = width - latent
    tokens = pool_ref.shape[1]
    pair = 2 * drafts
    blocks = rows // 16
    trips = slots // group

    def arrival(b):
        at = pl.ds(16 * b, 16) if b < blocks else pl.ds(rows, rows // 2)
        return pltpu.make_async_copy(arrived_any.at[:, at], arrived_ref.at[:, at], sems.at[b])

    def pool_part(t):
        at = pl.ds(t * group, group)
        return pltpu.make_async_copy(pool_any.at[at], pool_ref.at[at], sems.at[blocks + 2 + t])

    def leaving(b):
        at = pl.ds(16 * b, 16)
        sem = sems.at[blocks + 2 + trips + b]
        return pltpu.make_async_copy(out_ref.at[:, at], out_any.at[:, at], sem)

    values_copy = pltpu.make_async_copy(values_any, values_ref, sems.at[blocks + 1])
    for b in range(blocks + 1):
        arrival(b).start()
    for t in range(trips):
        pool_part(t).start()
    values_copy.start()

    first = lax.broadcasted_iota(jnp.int32, (slots * pair, 1), 0) % pair < drafts

    for block in range(blocks):
        arrival(block).wait()
        part = arrived_ref[:, 16 * block : 16 * block + 16, :].astype(F32)
        done = []
        for half in range(16 // pair):
            rows_in = part[:, pair * half : pair * half + pair].reshape(slots * pair, nope)
            rows_in = rows_in.astype(BF16)
            h = 16 // drafts * block + 2 * half
            one = jnp.dot(rows_in, keys_ref[h], preferred_element_type=F32)
            two = jnp.dot(rows_in, keys_ref[h + 1], preferred_element_type=F32)
            done.append(jnp.where(first, one, two).reshape(slots, pair, latent))
        query_ref[:, 16 * block : 16 * block + 16, :latent] = jnp.concatenate(done, 1).astype(BF16)
    arrival(blocks).wait()
    half_rows = rows // 2
    query_ref[:, :half_rows, latent:] = arrived_ref[:, rows : rows + half_rows, :rope]
    query_ref[:, half_rows:, latent:] = arrived_ref[:, rows : rows + half_rows, rope : 2 * rope]

    eye = lax.broadcasted_iota(jnp.int32, (rows, vhead), 0) == lax.broadcasted_iota(
        jnp.int32, (rows, vhead), 1
    )
    line = lax.broadcasted_iota(jnp.int32, (16, vhead), 0)
    token = lax.broadcasted_iota(jnp.int32, (rows, tokens), 1)

    for t in range(trips):
        pool_part(t).wait()
        ns = [t * group + k for k in range(group)]
        scores = [
            lax.dot_general(
                query_ref[n], pool_ref[n], (((1,), (1,)), ((), ())), preferred_element_type=F32
            )
            * scale
            for n in ns
        ]
        scores = [jnp.where(token < live_ref[n], x, NEG_FILL) for n, x in zip(ns, scores)]
        tops = [jnp.max(x, axis=1, keepdims=True) for x in scores]
        weights = [jnp.exp(x - top) for x, top in zip(scores, tops)]
        totals = [jnp.sum(x, axis=1, keepdims=True) for x in weights]
        weighted = [
            jnp.dot(x.astype(BF16), pool_ref[n, :, :latent], preferred_element_type=F32)
            for n, x in zip(ns, weights)
        ]
        for n, top, total, x in zip(ns, tops, totals, weighted):
            mean_ref[n] = (x * (1.0 / total)).astype(BF16)
            mass = jnp.sum(jnp.where(eye, top + jnp.log(total), 0.0), axis=0, keepdims=True)
            high = mass.astype(BF16).astype(F32)
            middle = (mass - high).astype(BF16).astype(F32)
            low = mass - high - middle
            parts = jnp.where(line == 0, high, jnp.where(line == 1, middle, low))
            out_ref[n, rows:, :] = jnp.where(line < PARTS, parts, 0.0).astype(BF16)

    leaving(blocks).start()
    values_copy.wait()
    for block in range(blocks):
        part = mean_ref[:, 16 * block : 16 * block + 16, :].astype(F32)
        done = []
        for half in range(16 // pair):
            rows_in = part[:, pair * half : pair * half + pair].reshape(slots * pair, latent)
            rows_in = rows_in.astype(BF16)
            h = 16 // drafts * block + 2 * half
            both = jnp.concatenate([values_ref[h], values_ref[h + 1]], 1)
            both = jnp.dot(rows_in, both, preferred_element_type=F32)
            both = jnp.where(first, both[:, :vhead], both[:, vhead:])
            done.append(both.reshape(slots, pair, vhead))
        out_ref[:, 16 * block : 16 * block + 16, :] = jnp.concatenate(done, 1).astype(BF16)
        leaving(block).start()
    for block in range(blocks + 1):
        leaving(block).wait()


def lend(live, arrived, key_absorb, value_absorb, pool, scale, group=8):
    slots, _, width = pool.shape
    latent = key_absorb.shape[2]
    vhead = value_absorb.shape[-1]
    rows = arrived.shape[1] * 2 // 3
    vmem = pl.BlockSpec(memory_space=pltpu.VMEM)
    hbm = pl.BlockSpec(memory_space=pl.ANY)
    return pl.pallas_call(
        functools.partial(lend_kernel, scale, group),
        out_shape=pltpu.HBM((slots, rows + 16, vhead), BF16),
        in_specs=[pl.BlockSpec(memory_space=pltpu.SMEM), hbm, vmem, hbm, hbm],
        out_specs=pl.BlockSpec(memory_space=pltpu.HBM),
        scratch_shapes=[
            pltpu.VMEM((slots, rows + 16, vhead), BF16),
            pltpu.VMEM(arrived.shape, BF16),
            pltpu.VMEM(value_absorb.shape, BF16),
            pltpu.VMEM(pool.shape, BF16),
            pltpu.VMEM((slots, rows, width), BF16),
            pltpu.VMEM((slots, rows, latent), BF16),
            pltpu.SemaphoreType.DMA((2 * (rows // 16) + 3 + slots // group,)),
        ],
        compiler_params=pltpu.CompilerParams(vmem_limit_bytes=28 * 2**20),
        name="lend",
    )(
        live,
        pltpu.with_memory_space_constraint(arrived, pltpu.HBM),
        key_absorb,
        pltpu.with_memory_space_constraint(value_absorb, pltpu.HBM),
        pltpu.with_memory_space_constraint(pool, pltpu.HBM),
    )


def settle_kernel(back_ref, local_ref, draft_scores_ref, draft_values_ref, out_ref, rows_ref, wide_ref):
    slots, _, vhead = back_ref.shape
    reqs, rows, drafts = draft_scores_ref.shape
    heads = rows // drafts
    mass = jnp.sum(back_ref[:, rows:, :].astype(F32), axis=1)
    mass = jnp.transpose(mass)[:rows]
    local = local_ref[...]
    for i in range(reqs):
        member = local == i
        draft = draft_scores_ref[i]
        own = jnp.where(member, mass, NEG_FILL)
        top = jnp.maximum(
            jnp.max(own, axis=1, keepdims=True), jnp.max(draft, axis=1, keepdims=True)
        )
        weight = jnp.where(member, jnp.exp(own - top), 0.0)
        draft = jnp.exp(draft - top)
        total = jnp.sum(weight, axis=1, keepdims=True) + jnp.sum(draft, axis=1, keepdims=True)
        value = jnp.zeros((rows, vhead), F32)
        for n in range(slots):
            value = value + weight[:, n : n + 1] * back_ref[n, :rows, :].astype(F32)
        for j in range(drafts):
            for s in range(drafts):
                wide_ref[pl.ds(j * rows + s, heads, stride=drafts), :] = draft_values_ref[i, j]
            value = value + draft[:, j : j + 1] * wide_ref[j * rows : (j + 1) * rows]
        value = value / total
        for h in range(heads):
            at = (h * reqs + i) * drafts
            rows_ref[at : at + drafts, :] = value[h * drafts : (h + 1) * drafts]
    size = reqs * drafts
    joined = jnp.concatenate([rows_ref[h * size : (h + 1) * size] for h in range(heads)], 1)
    joined = joined.astype(BF16)
    for n in range(out_ref.shape[0]):
        out_ref[n] = joined


def settle(back, local, draft_scores, draft_values, copies):
    _, _, vhead = back.shape
    reqs, rows, drafts = draft_scores.shape
    vmem = pl.BlockSpec(memory_space=pltpu.VMEM)
    return pl.pallas_call(
        settle_kernel,
        out_shape=jax.ShapeDtypeStruct((copies, reqs * drafts, rows // drafts * vhead), BF16),
        in_specs=[vmem] * 4,
        out_specs=vmem,
        scratch_shapes=[
            pltpu.VMEM((reqs * rows, vhead), F32),
            pltpu.VMEM((drafts * rows, vhead), F32),
        ],
        compiler_params=pltpu.CompilerParams(vmem_limit_bytes=8 * 2**20),
        name="settle",
    )(back, local, draft_scores, draft_values)


def body(
    draft_queries,
    draft_latents,
    latent_pool,
    key_absorb,
    value_absorb,
    out_proj,
    slot_request,
    context_lengths,
):
    home = lax.axis_index("lender")
    reqs, drafts, heads, width = draft_queries.shape
    nope, latent = key_absorb.shape[1:]
    tokens = latent_pool.shape[1]
    rows = heads * drafts
    scale = width ** (-0.5) * MSCALE_SQ

    outgoing = pack(jnp.full((1,), home, jnp.int32), slot_request, draft_queries, nope)
    outgoing, slot_request, context_lengths, draft_queries, draft_latents = (
        lax.optimization_barrier(
            (outgoing, slot_request, context_lengths, draft_queries, draft_latents)
        )
    )
    arrived = lax.all_to_all(outgoing, "lender", split_axis=0, concat_axis=0, tiled=True)

    live_all = live_tokens(slot_request, context_lengths, tokens)
    live_here = lax.dynamic_slice_in_dim(live_all, home, 1, 0)[0]
    local = lax.dynamic_slice_in_dim(slot_request, home, 1, 1).reshape(1, -1) - home * reqs
    part = jnp.einsum(
        "ishc,hcl->ihsl", draft_queries[..., :nope], key_absorb, preferred_element_type=F32
    ).astype(BF16)
    own = jnp.concatenate([part, jnp.swapaxes(draft_queries[..., nope:], 1, 2)], -1)
    draft_scores = (
        jnp.einsum("ihsk,ijk->ihsj", own, draft_latents, preferred_element_type=F32) * scale
    )
    causal = jnp.arange(drafts)[:, None] >= jnp.arange(drafts)[None, :]
    draft_scores = jnp.where(causal, draft_scores, NEG_FILL).reshape(reqs, rows, drafts)
    draft_values = jnp.einsum(
        "ijl,hlc->ijhc", draft_latents[:, :, :latent], value_absorb, preferred_element_type=F32
    )
    arrived, live_here, local, draft_scores, draft_values = lax.optimization_barrier(
        (arrived, live_here, local, draft_scores, draft_values)
    )

    sending = lend(live_here, arrived, key_absorb, value_absorb, latent_pool, scale)
    back = lax.all_to_all(sending, "lender", split_axis=0, concat_axis=0, tiled=True)

    copies = settle(back, local, draft_scores, draft_values, 8)
    lenders = latent_pool.shape[0]
    inner = [[8 * y + z for z in range(8)] for y in range(lenders // 8)]
    outer = [[8 * y + z for y in range(lenders // 8)] for z in range(8)]
    plane = lax.all_to_all(
        copies, "lender", split_axis=0, concat_axis=0, tiled=True, axis_index_groups=inner
    )
    plane = jnp.broadcast_to(plane[None], (lenders // 8,) + plane.shape)
    everyone = lax.all_to_all(
        plane, "lender", split_axis=0, concat_axis=0, tiled=True, axis_index_groups=outer
    )
    partial = jnp.dot(
        everyone.reshape(-1, everyone.shape[-1]), out_proj, preferred_element_type=F32
    ).astype(BF16)
    parts = lax.axis_size("tensor")
    terms = lax.all_to_all(
        partial.reshape(parts, -1, partial.shape[-1]), "tensor", split_axis=0, concat_axis=0
    )
    mixed = jnp.sum(terms.astype(F32), axis=0).astype(BF16)
    return mixed.reshape(-1, drafts, partial.shape[-1])


def solution(mesh):
    in_specs = (
        P("lender", None, "tensor", None),
        P("lender", None, None),
        P("lender", None, None),
        P("tensor", None, None),
        P("tensor", None, None),
        P("tensor", "lender"),
        P(),
        P(),
    )
    out_specs = P("tensor", None, "lender")
    return jax.shard_map(body, mesh=mesh, in_specs=in_specs, out_specs=out_specs, check_vma=False)
```

time: 125 us -> 116 us (0.928)
  Pallas kernels: 0 us -> 13.5 us
  matrix products: 12.8 us -> 3.19 us
  other arithmetic: 6.74 us -> 1.31 us
  local copies, waits for them, and re-layouts: 6.01 us -> 1.05 us
  blocking collectives: 46.8 us -> 43.7 us
    pallas_call x0 -> x3, Pallas kernels: none -> 13.5 us  [the longest x1 9.63 us: lend(): pl.pallas_call(functools.partial(lend_kernel, scale, group), out_shape=pl...]
    dot_general x7 -> x3, matrix products: 10.8 us -> 1.19 us  [the longest x1 0.48 us: body(): jnp.dot(everyone.reshape(-1, everyone.shape[-1]), out_proj, preferred_ele...]
    all_to_all x1, waiting for transfers between devices: 18.1 us -> 15 us  [body(): lax.all_to_all(outgoing, 'lender', split_axis=0, concat_axis=0, tiled=True)]
    all_to_all x1, waiting for transfers between devices: 13.8 us -> 16.7 us  [body(): lax.all_to_all(sending, 'lender', split_axis=0, concat_axis=0, tiled=True)]
    reshape x5 -> x0, local copies, waits for them, and re-layouts: 2.6 us -> none  [the longest x2 1.19 us: absorb(): return jnp.concatenate([part.reshape(n, rows, latent), rope_part], -1)]
    all_to_all x1 -> x2, blocking collectives: 32.1 us -> 29.7 us  [the longest x1 15.3 us: body(): lax.all_to_all(plane, 'lender', split_axis=0, concat_axis=0, tiled=True,...]
    reduce_sum x6 -> x0, other arithmetic: 2.2 us -> none  [the longest x1 1.19 us: body(): total = jnp.sum(weights, axis=-1)]
  transfers between devices with their start and end apart: 2 -> 2, of which waited for: 2 -> 2; matrix products, arithmetic and copies ran while one was open for 3% -> 4% of each run, Pallas kernels for 0% -> 0%
where the time goes in v2:
time: 116 us; the launch traced here: 115 us
  blocking collectives  43.7 us (38%)
  waiting for transfers between devices  31.7 us (27%)
  starting transfers between devices  20.7 us (18%)
  Pallas kernels  13.5 us (12%)
  matrix products  3.19 us (3%)
  other arithmetic  1.31 us (1%)
    all_to_all x1, waiting for transfers between devices, body(): lax.all_to_all(sending, 'lender', split_axis=0, concat_axis=0, tiled=True)  16.7 us
    all_to_all x1, blocking collectives, body(): lax.all_to_all(plane, 'lender', split_axis=0, concat_axis=0, tiled=True,...  15.3 us
    all_to_all x1, waiting for transfers between devices, body(): lax.all_to_all(outgoing, 'lender', split_axis=0, concat_axis=0, tiled=True)  15 us
    all_to_all x1, blocking collectives, body(): lax.all_to_all(copies, 'lender', split_axis=0, concat_axis=0, tiled=True,...  14.5 us
    all_to_all x1, blocking collectives, body(): lax.all_to_all(partial.reshape(parts, -1, partial.shape[-1]), 'tensor', s...  14 us
    all_to_all x1, starting transfers between devices, body(): lax.all_to_all(outgoing, 'lender', split_axis=0, concat_axis=0, tiled=True)  12.3 us
    pallas_call x1, Pallas kernels, lend(): pl.pallas_call(functools.partial(lend_kernel, scale, group), out_shape=pl...  9.63 us
    all_to_all x1, starting transfers between devices, body(): lax.all_to_all(sending, 'lender', split_axis=0, concat_axis=0, tiled=True)  8.37 us
  transfers between devices with their start and end apart: 2, of which 2 were waited for; matrix products, arithmetic and copies ran while one was open for 4% of the time, Pallas kernels for 0%

profile of v2, /device:TPU:1, one launch (start us, length us, event | category | flops | bytes accessed | tf_op | source)
XLA Modules:
  0.0 115.3 jit_solution(993979311676569914)
XLA Ops:
  0.0 0.0 copy-start
  0.0 0.0 copy-start.3
  0.0 0.0 copy-start.1
  0.0 2.3 %pack.1 = bf16[32,96,128]{2,1,0:T(8,128)(2,1)} custom-call(s32[1]{0:T(128)} %bitcast.home_ref, s32[32,32]{1,0:T(8,128)} %slot_request_ref.1, bf16[2,4,16,192]{3,2,1,0:T(8,128)(2,1)} %queries_ref.1), custom_call_target="tpu_custom_call" | custom-call | tf_op jit(solution)/shard_map/pack/pallas_call | solution.py:68
  2.4 0.0 copy-start.4
  2.4 0.0 copy-start.2
  2.4 0.0 copy-start.5
  2.4 12.3 %all-to-all-start = ((bf16[32,96,128]{2,1,0:T(8,128)(2,1)}), bf16[32,96,128]{2,1,0:T(8,128)(2,1)}, u32[]{:S(2)}, u32[]{:S(2)}) async-start(bf16[32,96,128]{2,1,0:T(8,128)(2,1)} %pack.1), calls=%async_computation | async-start | bytes 1572864 | tf_op jit(solution)/shard_map/all_to_all | solution.py:310
  14.7 0.0 copy-done.3
  14.8 0.0 copy-done.1
  14.8 0.4 fusion.7
  15.2 0.1 pad_maximum_fusion
  15.3 0.0 copy-done.4
  15.3 0.3 fusion.10
  15.6 0.1 copy.17
  15.8 0.0 copy-done.2
  15.8 0.2 subtract_reduce_fusion
  16.0 0.0 copy-done.5
  16.0 0.8 select_reduce_fusion.1
  16.8 0.2 select_reduce_fusion
  17.0 2.0 %fusion.2 = f32[2,4,16,128]{3,1,2,0:T(4,128)S(1)} fusion(bf16[16,512,128]{2,1,0:T(8,128)(2,1)} %values_any.1, bf16[2,4,576]{2,1,0:T(4,128)(2,1)S(1)} %copy-done.4), kind=kOutput, calls=%fused_computation.2 | convolution fusion | flops 16777216 | bytes 2170880 | tf_op jit(solution)/shard_map/ijl,hlc->ijhc/dot_general | solution.py:324
  19.0 15.0 %all-to-all-done.arrived_any = bf16[32,96,128]{2,1,0:T(8,128)(2,1)} async-done(((bf16[32,96,128]{2,1,0:T(8,128)(2,1)}), bf16[32,96,128]{2,1,0:T(8,128)(2,1)}, u32[]{:S(2)}, u32[]{:S(2)}) %all-to-all-start) | async-done | bytes 786464 | tf_op jit(solution)/shard_map/all_to_all | solution.py:310
  33.9 9.6 %lend.1 = bf16[32,80,128]{2,1,0:T(8,128)(2,1)} custom-call(s32[32]{0:T(128)S(1)} %fusion.19.live_ref, bf16[32,96,128]{2,1,0:T(8,128)(2,1)} %all-to-all-done.arrived_any, bf16[16,128,512]{2,1,0:T(8,128)(2,1)S(1)} %copy-done.1, bf16[16,512,128]{2,1,0:T(8,128)(2,1)} %values_any.1, bf16[32,192,576]{2,1,0:T(8,128)(2,1)} %pool_any.1), custom_call_target="tpu_custom_call" | custom-call | tf_op jit(solution)/shard_map/lend/pallas_call | solution.py:209
  43.6 8.4 %all-to-all-start.1 = ((bf16[32,80,128]{2,1,0:T(8,128)(2,1)}), bf16[32,80,128]{2,1,0:T(8,128)(2,1)S(1)}, u32[]{:S(2)}, u32[]{:S(2)}) async-start(bf16[32,80,128]{2,1,0:T(8,128)(2,1)} %lend.1), calls=%async_computation.1 | async-start | bytes 1310720 | tf_op jit(solution)/shard_map/all_to_all | solution.py:332
  52.0 16.7 %all-to-all-done.1.back_ref = bf16[32,80,128]{2,1,0:T(8,128)(2,1)S(1)} async-done(((bf16[32,80,128]{2,1,0:T(8,128)(2,1)}), bf16[32,80,128]{2,1,0:T(8,128)(2,1)S(1)}, u32[]{:S(2)}, u32[]{:S(2)}) %all-to-all-start.1) | async-done | bytes 655392 | tf_op jit(solution)/shard_map/all_to_all | solution.py:332
  68.7 1.6 %settle.1 = bf16[8,8,2048]{2,1,0:T(8,128)(2,1)S(1)} custom-call(bf16[32,80,128]{2,1,0:T(8,128)(2,1)S(1)} %all-to-all-done.1.back_ref, s32[1,32]{1,0:T(1,128)S(1)} %bitcast.36, f32[2,64,4]{2,1,0:T(8,128)S(1)} %bitcast.35, f32[2,4,16,128]{3,2,1,0:T(8,128)S(1)} %copy.18.draft_values_ref), custom_call_target="tpu_custom_call" | custom-call | tf_op jit(solution)/shard_map/settle/pallas_call | solution.py:273
  70.3 14.5 %all_to_all.25 = bf16[8,8,2048]{2,1,0:T(8,128)(2,1)S(1)} all-to-all(bf16[8,8,2048]{2,1,0:T(8,128)(2,1)S(1)} %settle.1), channel_id=1, replica_groups={{0,8,16,24,32,40,48,56},{64,72,80,88,96,104,112,120},{128,136,144,152,1..., dimensions={0} | all-to-all | bytes 524288 | tf_op jit(solution)/shard_map/all_to_all | solution.py:338
  84.7 0.1 broadcast_in_dim.54
  84.8 15.3 %all_to_all.26 = bf16[4,8,8,2048]{3,2,1,0:T(8,128)(2,1)S(1)} all-to-all(bf16[4,8,8,2048]{3,2,1,0:T(8,128)(2,1)S(1)} %broadcast_in_dim.54), channel_id=1, replica_groups={{0,64,128,192},{8,72,136,200},{16,80,144,208},{24,88,152,216},{32,96,16..., dimensions={0} | all-to-all | bytes 2097152 | tf_op jit(solution)/shard_map/all_to_all | solution.py:342
  100.1 0.0 copy-done
  100.1 0.5 convolution_convert_fusion
  100.6 0.1 copy.19
  100.7 14.0 %all_to_all.27 = bf16[8,32,224]{2,1,0:T(8,128)(2,1)S(1)} all-to-all(bf16[8,32,224]{2,1,0:T(8,128)(2,1)S(1)} %bitcast.38), channel_id=1, replica_groups=mesh['lender'=32,'tensor'=8] {'tensor'}, dimensions={0} | all-to-all | bytes 229376 | tf_op jit(solution)/shard_map/all_to_all | solution.py:349
  114.7 0.6 reshape.47
  (7 shorter events, 0.1 us)
Async XLA Ops:
  0.0 100.1 %copy-start = (bf16[2048,224]{0,1:T(8,128)(2,1)S(1)}, bf16[2048,224]{0,1:T(8,128)(2,1)}, u32[]{:S(2)}) copy-start(bf16[2048,224]{0,1:T(8,128)(2,1)} %param.13) | copy-start | bytes 2752516
  0.0 14.7 %copy-start.3 = (bf16[2,4,16,192]{3,2,1,0:T(8,128)(2,1)S(1)}, bf16[2,4,16,192]{3,2,1,0:T(8,128)(2,1)}, u32[]{:S(2)}) copy-start(bf16[2,4,16,192]{3,2,1,0:T(8,128)(2,1)} %queries_ref.1) | copy-start | bytes 147460
  0.0 14.8 %copy-start.1 = (bf16[16,128,512]{2,1,0:T(8,128)(2,1)S(1)}, bf16[16,128,512]{2,1,0:T(8,128)(2,1)}, u32[]{:S(2)}) copy-start(bf16[16,128,512]{2,1,0:T(8,128)(2,1)} %keys_ref.1) | copy-start | bytes 6291460
  2.4 12.9 %copy-start.4 = (bf16[2,4,576]{2,1,0:T(4,128)(2,1)S(1)}, bf16[2,4,576]{2,1,0:T(4,128)(2,1)}, u32[]{:S(2)}) copy-start(bf16[2,4,576]{2,1,0:T(4,128)(2,1)} %param.9) | copy-start | bytes 27652
  2.4 13.4 %copy-start.2 = (s32[32,32]{1,0:T(8,128)S(1)}, s32[32,32]{1,0:T(8,128)}, u32[]{:S(2)}) copy-start(s32[32,32]{1,0:T(8,128)} %slot_request_ref.1) | copy-start | bytes 12292
  2.4 13.6 %copy-start.5 = (s32[64]{0:T(128)S(1)}, s32[64]{0:T(128)}, u32[]{:S(2)}) copy-start(s32[64]{0:T(128)} %param.15) | copy-start | bytes 772
  2.4 31.5 %all-to-all-start = ((bf16[32,96,128]{2,1,0:T(8,128)(2,1)}), bf16[32,96,128]{2,1,0:T(8,128)(2,1)}, u32[]{:S(2)}, u32[]{:S(2)}) async-start(bf16[32,96,128]{2,1,0:T(8,128)(2,1)} %pack.1), calls=%async_computation | async-start | bytes 1572864 | tf_op jit(solution)/shard_map/all_to_all | solution.py:310
  43.6 25.1 %all-to-all-start.1 = ((bf16[32,80,128]{2,1,0:T(8,128)(2,1)}), bf16[32,80,128]{2,1,0:T(8,128)(2,1)S(1)}, u32[]{:S(2)}, u32[]{:S(2)}) async-start(bf16[32,80,128]{2,1,0:T(8,128)(2,1)} %lend.1), calls=%async_computation.1 | async-start | bytes 1310720 | tf_op jit(solution)/shard_map/all_to_all | solution.py:332

commit v3 on v2

--- a/solution.py
+++ b/solution.py
@@ -116,10 +116,23 @@
         at = pl.ds(t * group, group)
         return pltpu.make_async_copy(pool_any.at[at], pool_ref.at[at], sems.at[blocks + 2 + t])
 
-    def leaving(b):
-        at = pl.ds(16 * b, 16)
-        sem = sems.at[blocks + 2 + trips + b]
-        return pltpu.make_async_copy(out_ref.at[:, at], out_any.at[:, at], sem)
+    def leaving(t):
+        at = pl.ds(t * group, group)
+        return pltpu.make_async_copy(out_ref.at[at], out_any.at[at], sems.at[blocks + 2 + trips + t])
+
+    def project(at, count):
+        for block in range(blocks):
+            part = mean_ref[at : at + count, 16 * block : 16 * block + 16, :].astype(F32)
+            done = []
+            for half in range(16 // pair):
+                rows_in = part[:, pair * half : pair * half + pair].reshape(count * pair, latent)
+                h = 16 // drafts * block + 2 * half
+                both = jnp.concatenate([values_ref[h], values_ref[h + 1]], 1)
+                both = jnp.dot(rows_in.astype(BF16), both, preferred_element_type=F32)
+                both = jnp.where(first[: count * pair], both[:, :vhead], both[:, vhead:])
+                done.append(both.reshape(count, pair, vhead))
+            done = jnp.concatenate(done, 1).astype(BF16)
+            out_ref[at : at + count, 16 * block : 16 * block + 16, :] = done
 
     values_copy = pltpu.make_async_copy(values_any, values_ref, sems.at[blocks + 1])
     for b in range(blocks + 1):
@@ -150,7 +163,7 @@
     eye = lax.broadcasted_iota(jnp.int32, (rows, vhead), 0) == lax.broadcasted_iota(
         jnp.int32, (rows, vhead), 1
     )
-    line = lax.broadcasted_iota(jnp.int32, (16, vhead), 0)
+    line = lax.broadcasted_iota(jnp.int32, (8, vhead), 0)
     token = lax.broadcasted_iota(jnp.int32, (rows, tokens), 1)
 
     for t in range(trips):
@@ -179,24 +192,14 @@
             low = mass - high - middle
             parts = jnp.where(line == 0, high, jnp.where(line == 1, middle, low))
             out_ref[n, rows:, :] = jnp.where(line < PARTS, parts, 0.0).astype(BF16)
-
-    leaving(blocks).start()
-    values_copy.wait()
-    for block in range(blocks):
-        part = mean_ref[:, 16 * block : 16 * block + 16, :].astype(F32)
-        done = []
-        for half in range(16 // pair):
-            rows_in = part[:, pair * half : pair * half + pair].reshape(slots * pair, latent)
-            rows_in = rows_in.astype(BF16)
-            h = 16 // drafts * block + 2 * half
-            both = jnp.concatenate([values_ref[h], values_ref[h + 1]], 1)
-            both = jnp.dot(rows_in, both, preferred_element_type=F32)
-            both = jnp.where(first, both[:, :vhead], both[:, vhead:])
-            done.append(both.reshape(slots, pair, vhead))
-        out_ref[:, 16 * block : 16 * block + 16, :] = jnp.concatenate(done, 1).astype(BF16)
-        leaving(block).start()
-    for block in range(blocks + 1):
-        leaving(block).wait()
+        if t % 2 == 1:
+            if t == 1:
+                values_copy.wait()
+            project((t - 1) * group, 2 * group)
+            leaving(t - 1).start()
+            leaving(t).start()
+    for t in range(trips):
+        leaving(t).wait()
 
 
 def lend(live, arrived, key_absorb, value_absorb, pool, scale, group=8):
@@ -208,23 +211,23 @@
     hbm = pl.BlockSpec(memory_space=pl.ANY)
     return pl.pallas_call(
         functools.partial(lend_kernel, scale, group),
-        out_shape=pltpu.HBM((slots, rows + 16, vhead), BF16),
+        out_shape=pltpu.HBM((slots, rows + 8, vhead), BF16),
         in_specs=[pl.BlockSpec(memory_space=pltpu.SMEM), hbm, vmem, hbm, hbm],
         out_specs=pl.BlockSpec(memory_space=pltpu.HBM),
         scratch_shapes=[
-            pltpu.VMEM((slots, rows + 16, vhead), BF16),
+            pltpu.VMEM((slots, rows + 8, vhead), BF16),
             pltpu.VMEM(arrived.shape, BF16),
             pltpu.VMEM(value_absorb.shape, BF16),
             pltpu.VMEM(pool.shape, BF16),
             pltpu.VMEM((slots, rows, width), BF16),
             pltpu.VMEM((slots, rows, latent), BF16),
-            pltpu.SemaphoreType.DMA((2 * (rows // 16) + 3 + slots // group,)),
+            pltpu.SemaphoreType.DMA((rows // 16 + 2 + 2 * (slots // group),)),
         ],
         compiler_params=pltpu.CompilerParams(vmem_limit_bytes=28 * 2**20),
         name="lend",
     )(
         live,
-        pltpu.with_memory_space_constraint(arrived, pltpu.HBM),
+        arrived,
         key_absorb,
         pltpu.with_memory_space_constraint(value_absorb, pltpu.HBM),
         pltpu.with_memory_space_constraint(pool, pltpu.HBM),
@@ -284,6 +287,59 @@
     )(back, local, draft_scores, draft_values)
 
 
+def mix_kernel(place_ref, rows_ref, *refs):
+    weights, (own_ref, other_ref, late_ref, held_ref, sem) = list(refs[:-5]), refs[-5:]
+    blocks, size = own_ref.shape[:2]
+    late = pltpu.make_async_copy(weights[blocks - 1], late_ref, sem)
+    late.start()
+    weights[blocks - 1] = late_ref
+    half = rows_ref.shape[1] // 2
+    dot = functools.partial(
+        lax.dot_general,
+        dimension_numbers=(((1,), (1,)), ((), ())),
+        preferred_element_type=F32,
+    )
+    for k in range(blocks):
+        if k == blocks - 1:
+            late.wait()
+        if k == blocks // 2:
+            done = dot(rows_ref[:, :half], weights[k][...])
+            done += dot(rows_ref[:, half:], weights[blocks][...])
+        else:
+            done = dot(rows_ref[...], weights[k][...])
+        held_ref[k] = done.astype(BF16)
+    core = place_ref[blocks]
+    for k in range(blocks):
+        first = held_ref[place_ref[k], :size, :]
+        second = held_ref[place_ref[k], size:, :]
+        own_ref[k] = jnp.where(core == 0, first, second)
+        other_ref[k] = jnp.where(core == 0, second, first)
+
+
+def mix(place, rows, weights):
+    blocks = place.shape[0] - 1
+    features = weights[0].shape[0]
+    vmem = pl.BlockSpec(memory_space=pltpu.VMEM)
+    half = jax.ShapeDtypeStruct((blocks, rows.shape[0] // 2, features), BF16)
+    return pl.pallas_call(
+        mix_kernel,
+        out_shape=[half, half],
+        in_specs=[
+            pl.BlockSpec(memory_space=pltpu.SMEM),
+            vmem,
+            *[pl.BlockSpec(memory_space=pl.ANY) if i == blocks - 1 else vmem for i in range(5)],
+        ],
+        out_specs=[vmem, vmem],
+        scratch_shapes=[
+            pltpu.VMEM(weights[0].shape, BF16),
+            pltpu.VMEM((blocks, rows.shape[0], features), BF16),
+            pltpu.SemaphoreType.DMA,
+        ],
+        compiler_params=pltpu.CompilerParams(vmem_limit_bytes=12 * 2**20),
+        name="mix",
+    )(place, rows, *weights)
+
+
 def body(
     draft_queries,
     draft_latents,
@@ -302,9 +358,9 @@
     scale = width ** (-0.5) * MSCALE_SQ
 
     outgoing = pack(jnp.full((1,), home, jnp.int32), slot_request, draft_queries, nope)
-    outgoing, slot_request, context_lengths, draft_queries, draft_latents = (
+    outgoing, slot_request, context_lengths, draft_queries, draft_latents, out_proj = (
         lax.optimization_barrier(
-            (outgoing, slot_request, context_lengths, draft_queries, draft_latents)
+            (outgoing, slot_request, context_lengths, draft_queries, draft_latents, out_proj)
         )
     )
     arrived = lax.all_to_all(outgoing, "lender", split_axis=0, concat_axis=0, tiled=True)
@@ -312,6 +368,16 @@
     live_all = live_tokens(slot_request, context_lengths, tokens)
     live_here = lax.dynamic_slice_in_dim(live_all, home, 1, 0)[0]
     local = lax.dynamic_slice_in_dim(slot_request, home, 1, 1).reshape(1, -1) - home * reqs
+    lenders, column = latent_pool.shape[0], 8
+    planes = lenders // column
+    up = [(l, (l - column) % lenders) for l in range(lenders)]
+    down = [(l, (l + column) % lenders) for l in range(lenders)]
+    out_proj, local = lax.optimization_barrier((out_proj, local))
+    weight = out_proj.T
+    half = weight.shape[1] // 2
+    weight_up = lax.ppermute(weight, "lender", up)
+    weight_down = lax.ppermute(weight, "lender", down)
+
     part = jnp.einsum(
         "ishc,hcl->ihsl", draft_queries[..., :nope], key_absorb, preferred_element_type=F32
     ).astype(BF16)
@@ -329,28 +395,46 @@
     )
 
     sending = lend(live_here, arrived, key_absorb, value_absorb, latent_pool, scale)
+    sending, weight_up, weight_down = lax.optimization_barrier((sending, weight_up, weight_down))
     back = lax.all_to_all(sending, "lender", split_axis=0, concat_axis=0, tiled=True)
-
-    copies = settle(back, local, draft_scores, draft_values, 8)
-    lenders = latent_pool.shape[0]
-    inner = [[8 * y + z for z in range(8)] for y in range(lenders // 8)]
-    outer = [[8 * y + z for y in range(lenders // 8)] for z in range(8)]
+    far_left = lax.ppermute(weight_up[:, :half], "lender", up)
+    far_right = lax.ppermute(weight_down[:, half:], "lender", down)
+
+    copies = settle(back, local, draft_scores, draft_values, column)
+    inner = [[column * y + z for z in range(column)] for y in range(planes)]
     plane = lax.all_to_all(
         copies, "lender", split_axis=0, concat_axis=0, tiled=True, axis_index_groups=inner
     )
-    plane = jnp.broadcast_to(plane[None], (lenders // 8,) + plane.shape)
-    everyone = lax.all_to_all(
-        plane, "lender", split_axis=0, concat_axis=0, tiled=True, axis_index_groups=outer
-    )
-    partial = jnp.dot(
-        everyone.reshape(-1, everyone.shape[-1]), out_proj, preferred_element_type=F32
-    ).astype(BF16)
-    parts = lax.axis_size("tensor")
+    plane, far_left, far_right = lax.optimization_barrier((plane, far_left, far_right))
+    y = home // column
+    tensor = lax.axis_index("tensor")
+    x, core = tensor // 2, tensor % 2
+    place = jnp.stack([(k - y) % planes for k in range(planes)] + [core]).astype(jnp.int32)
+    weight_down = pltpu.with_memory_space_constraint(weight_down, pltpu.HBM)
+    weights = [weight, weight_up, far_left, weight_down, far_right]
+    own, other = mix(place, plane.reshape(-1, plane.shape[-1]), weights)
+
+    tensors = lax.axis_size("tensor")
+    swap = [(t, t ^ 1) for t in range(tensors)]
+    own = (own.astype(F32) + lax.ppermute(other, "tensor", swap).astype(F32)).astype(BF16)
+    chunks = jnp.broadcast_to(own[:, None], (planes, tensors // 2) + own.shape[1:])
+    chunks = chunks.reshape((planes * tensors // 2,) + own.shape[1:])
+    groups = [
+        [(column * p + z) * tensors + 2 * q + c for p in range(planes) for q in range(tensors // 2)]
+        for z in range(column)
+        for c in range(2)
+    ]
     terms = lax.all_to_all(
-        partial.reshape(parts, -1, partial.shape[-1]), "tensor", split_axis=0, concat_axis=0
-    )
-    mixed = jnp.sum(terms.astype(F32), axis=0).astype(BF16)
-    return mixed.reshape(-1, drafts, partial.shape[-1])
+        chunks,
+        ("lender", "tensor"),
+        split_axis=0,
+        concat_axis=0,
+        tiled=True,
+        axis_index_groups=groups,
+    )
+    terms = lax.dynamic_slice_in_dim(terms, x * (tensors // 2), tensors // 2, 0)
+    total = jnp.sum(terms.astype(F32), axis=0)
+    return total.astype(BF16).reshape(-1, drafts, total.shape[-1])
 
 
 def solution(mesh):

time: 116 us -> 111 us (0.957)
  blocking collectives: 43.7 us -> 0 us
  starting transfers between devices: 20.7 us -> 41.3 us
  waiting for transfers between devices: 31.7 us -> 42.6 us
  local copies, waits for them, and re-layouts: 1.05 us -> 4.6 us
  Pallas kernels: 13.5 us -> 16.5 us
    all_to_all x3 -> x0, blocking collectives: 43.7 us -> none  [the longest x1 15.3 us: body(): lax.all_to_all(plane, 'lender', split_axis=0, concat_axis=0, tiled=True,...]
    all_to_all x0 -> x2, waiting for transfers between devices: none -> 17.5 us  [the longest x1 9.39 us: body(): lax.all_to_all(copies, 'lender', split_axis=0, concat_axis=0, tiled=True,...]
    ppermute x0 -> x5, starting transfers between devices: none -> 11.3 us  [the longest x1 4.86 us: body(): lax.ppermute(other, 'tensor', swap).astype(F32)]
    all_to_all x0 -> x2, starting transfers between devices: none -> 10.7 us  [the longest x1 5.69 us: body(): lax.all_to_all(copies, 'lender', split_axis=0, concat_axis=0, tiled=True,...]
    all_to_all x1, waiting for transfers between devices: 16.7 us -> 8.5 us  [body(): lax.all_to_all(sending, 'lender', split_axis=0, concat_axis=0, tiled=True)]
    pallas_call x0 -> x1, Pallas kernels: none -> 2.99 us  [mix(): pl.pallas_call(mix_kernel, out_shape=[half, half], in_specs=[pl.BlockSpec...]
    slice x0 -> x2, local copies, waits for them, and re-layouts: none -> 2.95 us  [the longest x1 1.83 us: body(): far_right = lax.ppermute(weight_down[:, half:], 'lender', down)]
    all_to_all x1, starting transfers between devices: 12.3 us -> 9.84 us  [body(): lax.all_to_all(outgoing, 'lender', split_axis=0, concat_axis=0, tiled=True)]
  transfers between devices with their start and end apart: 2 -> 9, of which waited for: 2 -> 5; matrix products, arithmetic and copies ran while one was open for 4% -> 6% of each run, Pallas kernels for 0% -> 10%
where the time goes in v3:
time: 111 us; the launch traced here: 110 us
  waiting for transfers between devices  42.6 us (38%)
  starting transfers between devices  41.3 us (37%)
  Pallas kernels  16.5 us (15%)
  local copies, waits for them, and re-layouts  4.6 us (4%)
  matrix products  2.7 us (2%)
  other arithmetic  2.04 us (2%)
    all_to_all x1, waiting for transfers between devices, body(): lax.all_to_all(outgoing, 'lender', split_axis=0, concat_axis=0, tiled=True)  15.7 us
    all_to_all x1, starting transfers between devices, body(): lax.all_to_all(outgoing, 'lender', split_axis=0, concat_axis=0, tiled=True)  9.84 us
    all_to_all x1, starting transfers between devices, body(): lax.all_to_all(sending, 'lender', split_axis=0, concat_axis=0, tiled=True)  9.41 us
    all_to_all x1, waiting for transfers between devices, body(): lax.all_to_all(copies, 'lender', split_axis=0, concat_axis=0, tiled=True,...  9.39 us
    pallas_call x1, Pallas kernels, lend(): pl.pallas_call(functools.partial(lend_kernel, scale, group), out_shape=pl...  8.93 us
    all_to_all x1, waiting for transfers between devices, body(): lax.all_to_all(sending, 'lender', split_axis=0, concat_axis=0, tiled=True)  8.5 us
    all_to_all x1, waiting for transfers between devices, body(): lax.all_to_all(chunks, ('lender', 'tensor'), split_axis=0, concat_axis=0,...  8.11 us
    all_to_all x1, starting transfers between devices, body(): lax.all_to_all(copies, 'lender', split_axis=0, concat_axis=0, tiled=True,...  5.69 us
  transfers between devices with their start and end apart: 9, of which 5 were waited for; matrix products, arithmetic and copies ran while one was open for 6% of the time, Pallas kernels for 10%

profile of v3, /device:TPU:1, one launch (start us, length us, event | category | flops | bytes accessed | tf_op | source)
XLA Modules:
  0.0 110.0 jit_solution(13134394172143444815)
XLA Ops:
  0.0 0.0 copy-start.3
  0.0 0.0 copy-start
  0.0 2.3 %pack.1 = bf16[32,96,128]{2,1,0:T(8,128)(2,1)} custom-call(s32[1]{0:T(128)} %bitcast.5.home_ref, s32[32,32]{1,0:T(8,128)} %slot_request_ref.1, bf16[2,4,16,192]{3,2,1,0:T(8,128)(2,1)} %queries_ref.1), custom_call_target="tpu_custom_call" | custom-call | tf_op jit(solution)/shard_map/pack/pallas_call | solution.py:68
  2.3 0.9 subtract_reduce_fusion
  3.2 0.0 copy-start.4
  3.2 0.0 copy-start.2
  3.3 0.0 copy-start.5
  3.3 2.2 %collective-permute-start.1 = (bf16[224,2048]{1,0:T(8,128)(2,1)}, bf16[224,2048]{1,0:T(8,128)(2,1)}, u32[]{:S(2)}, u32[]{:S(2)}) collective-permute-start(bf16[224,2048]{1,0:T(8,128)(2,1)} %bitcast.40), channel_id=1, source_target_pairs={{0,64},{8,72},{16,80},{24,88},{32,96},{40,104},{48,112},{56,120},{... | collective-permute-start | bytes 2752520 | tf_op jit(solution)/shard_map/ppermute | solution.py:379
  5.5 1.5 %collective-permute-start = (bf16[224,2048]{1,0:T(8,128)(2,1)}, bf16[224,2048]{1,0:T(8,128)(2,1)}, u32[]{:S(2)}, u32[]{:S(2)}) collective-permute-start(bf16[224,2048]{1,0:T(8,128)(2,1)} %bitcast.41), channel_id=1, source_target_pairs={{0,192},{8,200},{16,208},{24,216},{32,224},{40,232},{48,240},{56,2... | collective-permute-start | bytes 2752520 | tf_op jit(solution)/shard_map/ppermute | solution.py:378
  7.0 9.8 %all-to-all-start = ((bf16[32,96,128]{2,1,0:T(8,128)(2,1)}), bf16[32,96,128]{2,1,0:T(8,128)(2,1)S(1)}, u32[]{:S(2)}, u32[]{:S(2)}) async-start(bf16[32,96,128]{2,1,0:T(8,128)(2,1)} %pack.1), calls=%async_computation | async-start | bytes 1572864 | tf_op jit(solution)/shard_map/all_to_all | solution.py:366
  16.9 0.0 copy-done.3
  16.9 0.0 copy-done
  17.0 0.4 fusion.7
  17.3 0.1 pad_maximum_fusion
  17.4 0.0 copy-done.4
  17.4 0.3 fusion.10
  17.8 0.1 copy.16
  17.9 0.0 copy-done.2
  17.9 0.0 copy-done.5
  18.0 0.8 select_reduce_fusion.1
  18.7 0.2 select_reduce_fusion
  19.0 2.0 %fusion.2 = f32[2,4,16,128]{3,1,2,0:T(4,128)S(1)} fusion(bf16[16,512,128]{2,1,0:T(8,128)(2,1)} %values_any.1, bf16[2,4,576]{2,1,0:T(4,128)(2,1)S(1)} %copy-done.4), kind=kOutput, calls=%fused_computation.2 | convolution fusion | flops 16777216 | bytes 2170880 | tf_op jit(solution)/shard_map/ijl,hlc->ijhc/dot_general | solution.py:390
  21.0 15.7 %all-to-all-done.arrived_any = bf16[32,96,128]{2,1,0:T(8,128)(2,1)S(1)} async-done(((bf16[32,96,128]{2,1,0:T(8,128)(2,1)}), bf16[32,96,128]{2,1,0:T(8,128)(2,1)S(1)}, u32[]{:S(2)}, u32[]{:S(2)}) %all-to-all-start) | async-done | bytes 786464 | tf_op jit(solution)/shard_map/all_to_all | solution.py:366
  36.7 8.9 %lend.1 = bf16[32,72,128]{2,1,0:T(8,128)(2,1)} custom-call(s32[32]{0:T(128)S(1)} %fusion.19.live_ref, bf16[32,96,128]{2,1,0:T(8,128)(2,1)S(1)} %all-to-all-done.arrived_any, bf16[16,128,512]{2,1,0:T(8,128)(2,1)S(1)} %copy-done, bf16[16,512,128]{2,1,0:T(8,128)(2,1)} %values_any.1, bf16[32,192,576]{2,1,0:T(8,128)(2,1)} %pool_any.1), custom_call_target="tpu_custom_call" | custom-call | tf_op jit(solution)/shard_map/lend/pallas_call | solution.py:212
  45.6 0.0 collective-permute-done.1.refs_3_
  45.6 0.0 collective-permute-done.refs_1_
  45.6 9.4 %all-to-all-start.1 = ((bf16[32,72,128]{2,1,0:T(8,128)(2,1)}), bf16[32,72,128]{2,1,0:T(8,128)(2,1)S(1)}, u32[]{:S(2)}, u32[]{:S(2)}) async-start(bf16[32,72,128]{2,1,0:T(8,128)(2,1)} %lend.1), calls=%async_computation.1 | async-start | bytes 1179648 | tf_op jit(solution)/shard_map/all_to_all | solution.py:399
  55.0 0.0 copy-start.1
  55.1 1.1 %slice.18 = bf16[224,1024]{1,0:T(8,128)(2,1)S(1)} slice(bf16[224,2048]{1,0:T(8,128)(2,1)} %collective-permute-done.refs_1_), slice={[0:224], [0:1024]} | slice | bytes 917504 | tf_op jit(solution)/shard_map/slice | solution.py:400
  56.2 1.8 %slice.19 = bf16[224,1024]{1,0:T(8,128)(2,1)} slice(bf16[224,2048]{1,0:T(8,128)(2,1)} %collective-permute-done.1.refs_3_), slice={[0:224], [1024:2048]} | slice | bytes 917504 | tf_op jit(solution)/shard_map/slice | solution.py:401
  58.0 1.2 %collective-permute-start.3 = (bf16[224,1024]{1,0:T(8,128)(2,1)}, bf16[224,1024]{1,0:T(8,128)(2,1)S(1)}, u32[]{:S(2)}, u32[]{:S(2)}) collective-permute-start(bf16[224,1024]{1,0:T(8,128)(2,1)} %slice.19), channel_id=1, source_target_pairs={{0,64},{8,72},{16,80},{24,88},{32,96},{40,104},{48,112},{56,120},{... | collective-permute-start | bytes 1376264 | tf_op jit(solution)/shard_map/ppermute | solution.py:401
  59.3 1.4 %collective-permute-start.2 = (bf16[224,1024]{1,0:T(8,128)(2,1)S(1)}, bf16[224,1024]{1,0:T(8,128)(2,1)S(1)}, u32[]{:S(2)}, u32[]{:S(2)}) collective-permute-start(bf16[224,1024]{1,0:T(8,128)(2,1)S(1)} %slice.18), channel_id=1, source_target_pairs={{0,192},{8,200},{16,208},{24,216},{32,224},{40,232},{48,240},{56,2... | collective-permute-start | bytes 1376264 | tf_op jit(solution)/shard_map/ppermute | solution.py:400
  60.7 8.5 %all-to-all-done.1.back_ref = bf16[32,72,128]{2,1,0:T(8,128)(2,1)S(1)} async-done(((bf16[32,72,128]{2,1,0:T(8,128)(2,1)}), bf16[32,72,128]{2,1,0:T(8,128)(2,1)S(1)}, u32[]{:S(2)}, u32[]{:S(2)}) %all-to-all-start.1) | async-done | bytes 589856 | tf_op jit(solution)/shard_map/all_to_all | solution.py:399
  69.2 2.3 %settle.1 = bf16[8,8,2048]{2,1,0:T(8,128)(2,1)} custom-call(bf16[32,72,128]{2,1,0:T(8,128)(2,1)S(1)} %all-to-all-done.1.back_ref, s32[1,32]{1,0:T(1,128)S(1)} %bitcast.44, f32[2,64,4]{2,1,0:T(8,128)S(1)} %bitcast.43, f32[2,4,16,128]{3,2,1,0:T(8,128)S(1)} %copy.17.draft_values_ref), custom_call_target="tpu_custom_call" | custom-call | tf_op jit(solution)/shard_map/settle/pallas_call | solution.py:276
  71.5 5.7 %all-to-all-start.2 = ((bf16[8,8,2048]{2,1,0:T(8,128)(2,1)}), bf16[8,8,2048]{2,1,0:T(8,128)(2,1)S(1)}, u32[]{:S(2)}, u32[]{:S(2)}) async-start(bf16[8,8,2048]{2,1,0:T(8,128)(2,1)} %settle.1), calls=%async_computation.2 | async-start | bytes 524288 | tf_op jit(solution)/shard_map/all_to_all | solution.py:405
  77.2 0.1 stack.23.place_ref
  77.3 0.0 collective-permute-done.3.refs_4_
  77.3 0.0 collective-permute-done.2.refs_2_
  77.3 9.4 %all-to-all-done.2 = bf16[8,8,2048]{2,1,0:T(8,128)(2,1)S(1)} async-done(((bf16[8,8,2048]{2,1,0:T(8,128)(2,1)}), bf16[8,8,2048]{2,1,0:T(8,128)(2,1)S(1)}, u32[]{:S(2)}, u32[]{:S(2)}) %all-to-all-start.2) | async-done | bytes 262176 | tf_op jit(solution)/shard_map/all_to_all | solution.py:405
  86.7 0.0 copy-done.1
  86.7 3.0 %mix.1 = (bf16[4,32,224]{2,1,0:T(8,128)(2,1)S(1)}, bf16[4,32,224]{2,1,0:T(8,128)(2,1)S(1)}) custom-call(s32[5]{0:T(128)S(1)} %stack.23.place_ref, bf16[64,2048]{1,0:T(8,128)(2,1)S(1)} %bitcast.39, bf16[224,2048]{1,0:T(8,128)(2,1)S(1)} %bitcast.42, bf16[224,2048]{1,0:T(8,128)(2,1)} %collective-permute-done.refs_1_, ...), custom_call_target="tpu_custom_call" | custom-call | tf_op jit(solution)/shard_map/mix/pallas_call | solution.py:324
  89.7 4.9 %collective-permute-start.4 = (bf16[4,32,224]{2,1,0:T(8,128)(2,1)S(1)}, bf16[4,32,224]{2,1,0:T(8,128)(2,1)S(1)}, u32[]{:S(2)}, u32[]{:S(2)}) collective-permute-start(bf16[4,32,224]{2,1,0:T(8,128)(2,1)S(1)} %get-tuple-element.46), channel_id=1, source_target_pairs={{0,1},{1,0},{2,3},{3,2},{4,5},{5,4},{6,7},{7,6},{8,9},{9,8},{10,11... | collective-permute-start | bytes 172040 | tf_op jit(solution)/shard_map/ppermute | solution.py:419
  94.5 0.9 collective-permute-done.4
  95.4 0.7 broadcast_in_dim.54
  96.2 5.1 %all-to-all-start.3 = ((bf16[16,32,224]{2,1,0:T(8,128)(2,1)}), bf16[16,32,224]{2,1,0:T(8,128)(2,1)S(1)}, u32[]{:S(2)}, u32[]{:S(2)}) async-start(bf16[16,32,224]{2,1,0:T(8,128)(2,1)} %bitcast.19), calls=%async_computation.3 | async-start | bytes 524288 | tf_op jit(solution)/shard_map/all_to_all | solution.py:427
  101.2 8.1 %all-to-all-done.3 = bf16[16,32,224]{2,1,0:T(8,128)(2,1)S(1)} async-done(((bf16[16,32,224]{2,1,0:T(8,128)(2,1)}), bf16[16,32,224]{2,1,0:T(8,128)(2,1)S(1)}, u32[]{:S(2)}, u32[]{:S(2)}) %all-to-all-start.3) | async-done | bytes 229408 | tf_op jit(solution)/shard_map/all_to_all | solution.py:427
  109.4 0.6 reshape.47
  (8 shorter events, 0.1 us)
Async XLA Ops:
  0.0 16.9 %copy-start.3 = (bf16[2,4,16,192]{3,2,1,0:T(8,128)(2,1)S(1)}, bf16[2,4,16,192]{3,2,1,0:T(8,128)(2,1)}, u32[]{:S(2)}) copy-start(bf16[2,4,16,192]{3,2,1,0:T(8,128)(2,1)} %queries_ref.1) | copy-start | bytes 147460
  0.0 16.9 %copy-start = (bf16[16,128,512]{2,1,0:T(8,128)(2,1)S(1)}, bf16[16,128,512]{2,1,0:T(8,128)(2,1)}, u32[]{:S(2)}) copy-start(bf16[16,128,512]{2,1,0:T(8,128)(2,1)} %keys_ref.1) | copy-start | bytes 6291460
  3.2 14.2 %copy-start.4 = (bf16[2,4,576]{2,1,0:T(4,128)(2,1)S(1)}, bf16[2,4,576]{2,1,0:T(4,128)(2,1)}, u32[]{:S(2)}) copy-start(bf16[2,4,576]{2,1,0:T(4,128)(2,1)} %param.9) | copy-start | bytes 27652
  3.2 14.7 %copy-start.2 = (s32[32,32]{1,0:T(8,128)S(1)}, s32[32,32]{1,0:T(8,128)}, u32[]{:S(2)}) copy-start(s32[32,32]{1,0:T(8,128)} %slot_request_ref.1) | copy-start | bytes 12292
  3.3 14.7 %copy-start.5 = (s32[64]{0:T(128)S(1)}, s32[64]{0:T(128)}, u32[]{:S(2)}) copy-start(s32[64]{0:T(128)} %param.15) | copy-start | bytes 772
  3.3 42.3 %collective-permute-start.1 = (bf16[224,2048]{1,0:T(8,128)(2,1)}, bf16[224,2048]{1,0:T(8,128)(2,1)}, u32[]{:S(2)}, u32[]{:S(2)}) collective-permute-start(bf16[224,2048]{1,0:T(8,128)(2,1)} %bitcast.40), channel_id=1, source_target_pairs={{0,64},{8,72},{16,80},{24,88},{32,96},{40,104},{48,112},{56,120},{... | collective-permute-start | bytes 2752520 | tf_op jit(solution)/shard_map/ppermute | solution.py:379
  5.5 40.1 %collective-permute-start = (bf16[224,2048]{1,0:T(8,128)(2,1)}, bf16[224,2048]{1,0:T(8,128)(2,1)}, u32[]{:S(2)}, u32[]{:S(2)}) collective-permute-start(bf16[224,2048]{1,0:T(8,128)(2,1)} %bitcast.41), channel_id=1, source_target_pairs={{0,192},{8,200},{16,208},{24,216},{32,224},{40,232},{48,240},{56,2... | collective-permute-start | bytes 2752520 | tf_op jit(solution)/shard_map/ppermute | solution.py:378
  7.0 29.7 %all-to-all-start = ((bf16[32,96,128]{2,1,0:T(8,128)(2,1)}), bf16[32,96,128]{2,1,0:T(8,128)(2,1)S(1)}, u32[]{:S(2)}, u32[]{:S(2)}) async-start(bf16[32,96,128]{2,1,0:T(8,128)(2,1)} %pack.1), calls=%async_computation | async-start | bytes 1572864 | tf_op jit(solution)/shard_map/all_to_all | solution.py:366
  45.6 23.6 %all-to-all-start.1 = ((bf16[32,72,128]{2,1,0:T(8,128)(2,1)}), bf16[32,72,128]{2,1,0:T(8,128)(2,1)S(1)}, u32[]{:S(2)}, u32[]{:S(2)}) async-start(bf16[32,72,128]{2,1,0:T(8,128)(2,1)} %lend.1), calls=%async_computation.1 | async-start | bytes 1179648 | tf_op jit(solution)/shard_map/all_to_all | solution.py:399
  55.0 31.6 %copy-start.1 = (bf16[2048,224]{0,1:T(8,128)(2,1)S(1)}, bf16[2048,224]{0,1:T(8,128)(2,1)}, u32[]{:S(2)}) copy-start(bf16[2048,224]{0,1:T(8,128)(2,1)} %param.13) | copy-start | bytes 2752516
  58.0 19.2 %collective-permute-start.3 = (bf16[224,1024]{1,0:T(8,128)(2,1)}, bf16[224,1024]{1,0:T(8,128)(2,1)S(1)}, u32[]{:S(2)}, u32[]{:S(2)}) collective-permute-start(bf16[224,1024]{1,0:T(8,128)(2,1)} %slice.19), channel_id=1, source_target_pairs={{0,64},{8,72},{16,80},{24,88},{32,96},{40,104},{48,112},{56,120},{... | collective-permute-start | bytes 1376264 | tf_op jit(solution)/shard_map/ppermute | solution.py:401
  59.3 18.0 %collective-permute-start.2 = (bf16[224,1024]{1,0:T(8,128)(2,1)S(1)}, bf16[224,1024]{1,0:T(8,128)(2,1)S(1)}, u32[]{:S(2)}, u32[]{:S(2)}) collective-permute-start(bf16[224,1024]{1,0:T(8,128)(2,1)S(1)} %slice.18), channel_id=1, source_target_pairs={{0,192},{8,200},{16,208},{24,216},{32,224},{40,232},{48,240},{56,2... | collective-permute-start | bytes 1376264 | tf_op jit(solution)/shard_map/ppermute | solution.py:400
  71.5 15.2 %all-to-all-start.2 = ((bf16[8,8,2048]{2,1,0:T(8,128)(2,1)}), bf16[8,8,2048]{2,1,0:T(8,128)(2,1)S(1)}, u32[]{:S(2)}, u32[]{:S(2)}) async-start(bf16[8,8,2048]{2,1,0:T(8,128)(2,1)} %settle.1), calls=%async_computation.2 | async-start | bytes 524288 | tf_op jit(solution)/shard_map/all_to_all | solution.py:405
  89.7 5.8 %collective-permute-start.4 = (bf16[4,32,224]{2,1,0:T(8,128)(2,1)S(1)}, bf16[4,32,224]{2,1,0:T(8,128)(2,1)S(1)}, u32[]{:S(2)}, u32[]{:S(2)}) collective-permute-start(bf16[4,32,224]{2,1,0:T(8,128)(2,1)S(1)} %get-tuple-element.46), channel_id=1, source_target_pairs={{0,1},{1,0},{2,3},{3,2},{4,5},{5,4},{6,7},{7,6},{8,9},{9,8},{10,11... | collective-permute-start | bytes 172040 | tf_op jit(solution)/shard_map/ppermute | solution.py:419
  96.2 13.2 %all-to-all-start.3 = ((bf16[16,32,224]{2,1,0:T(8,128)(2,1)}), bf16[16,32,224]{2,1,0:T(8,128)(2,1)S(1)}, u32[]{:S(2)}, u32[]{:S(2)}) async-start(bf16[16,32,224]{2,1,0:T(8,128)(2,1)} %bitcast.19), calls=%async_computation.3 | async-start | bytes 524288 | tf_op jit(solution)/shard_map/all_to_all | solution.py:427

commit v4 on v3

--- a/solution.py
+++ b/solution.py
@@ -84,13 +84,12 @@
     scale,
     group,
     live_ref,
-    arrived_any,
+    arrived_ref,
     keys_ref,
     values_any,
     pool_any,
     out_any,
     out_ref,
-    arrived_ref,
     values_ref,
     pool_ref,
     query_ref,
@@ -108,17 +107,13 @@
     blocks = rows // 16
     trips = slots // group
 
-    def arrival(b):
-        at = pl.ds(16 * b, 16) if b < blocks else pl.ds(rows, rows // 2)
-        return pltpu.make_async_copy(arrived_any.at[:, at], arrived_ref.at[:, at], sems.at[b])
-
     def pool_part(t):
         at = pl.ds(t * group, group)
-        return pltpu.make_async_copy(pool_any.at[at], pool_ref.at[at], sems.at[blocks + 2 + t])
+        return pltpu.make_async_copy(pool_any.at[at], pool_ref.at[at], sems.at[t])
 
     def leaving(t):
         at = pl.ds(t * group, group)
-        return pltpu.make_async_copy(out_ref.at[at], out_any.at[at], sems.at[blocks + 2 + trips + t])
+        return pltpu.make_async_copy(out_ref.at[at], out_any.at[at], sems.at[trips + t])
 
     def project(at, count):
         for block in range(blocks):
@@ -134,9 +129,7 @@
             done = jnp.concatenate(done, 1).astype(BF16)
             out_ref[at : at + count, 16 * block : 16 * block + 16, :] = done
 
-    values_copy = pltpu.make_async_copy(values_any, values_ref, sems.at[blocks + 1])
-    for b in range(blocks + 1):
-        arrival(b).start()
+    values_copy = pltpu.make_async_copy(values_any, values_ref, sems.at[2 * trips])
     for t in range(trips):
         pool_part(t).start()
     values_copy.start()
@@ -144,7 +137,6 @@
     first = lax.broadcasted_iota(jnp.int32, (slots * pair, 1), 0) % pair < drafts
 
     for block in range(blocks):
-        arrival(block).wait()
         part = arrived_ref[:, 16 * block : 16 * block + 16, :].astype(F32)
         done = []
         for half in range(16 // pair):
@@ -155,7 +147,6 @@
             two = jnp.dot(rows_in, keys_ref[h + 1], preferred_element_type=F32)
             done.append(jnp.where(first, one, two).reshape(slots, pair, latent))
         query_ref[:, 16 * block : 16 * block + 16, :latent] = jnp.concatenate(done, 1).astype(BF16)
-    arrival(blocks).wait()
     half_rows = rows // 2
     query_ref[:, :half_rows, latent:] = arrived_ref[:, rows : rows + half_rows, :rope]
     query_ref[:, half_rows:, latent:] = arrived_ref[:, rows : rows + half_rows, rope : 2 * rope]
@@ -212,16 +203,15 @@
     return pl.pallas_call(
         functools.partial(lend_kernel, scale, group),
         out_shape=pltpu.HBM((slots, rows + 8, vhead), BF16),
-        in_specs=[pl.BlockSpec(memory_space=pltpu.SMEM), hbm, vmem, hbm, hbm],
+        in_specs=[pl.BlockSpec(memory_space=pltpu.SMEM), vmem, vmem, hbm, hbm],
         out_specs=pl.BlockSpec(memory_space=pltpu.HBM),
         scratch_shapes=[
             pltpu.VMEM((slots, rows + 8, vhead), BF16),
-            pltpu.VMEM(arrived.shape, BF16),
             pltpu.VMEM(value_absorb.shape, BF16),
             pltpu.VMEM(pool.shape, BF16),
             pltpu.VMEM((slots, rows, width), BF16),
             pltpu.VMEM((slots, rows, latent), BF16),
-            pltpu.SemaphoreType.DMA((rows // 16 + 2 + 2 * (slots // group),)),
+            pltpu.SemaphoreType.DMA((2 * (slots // group) + 1,)),
         ],
         compiler_params=pltpu.CompilerParams(vmem_limit_bytes=28 * 2**20),
         name="lend",
@@ -288,52 +278,51 @@
 
 
 def mix_kernel(place_ref, rows_ref, *refs):
-    weights, (own_ref, other_ref, late_ref, held_ref, sem) = list(refs[:-5]), refs[-5:]
-    blocks, size = own_ref.shape[:2]
-    late = pltpu.make_async_copy(weights[blocks - 1], late_ref, sem)
-    late.start()
-    weights[blocks - 1] = late_ref
-    half = rows_ref.shape[1] // 2
+    weights, (own_ref, other_ref, late_ref, held_ref, sems) = refs[:-5], refs[-5:]
+    blocks = own_ref.shape[0]
+    size, features = held_ref.shape[-2] // 2, held_ref.shape[-1]
+    late = {
+        k: pltpu.make_async_copy(weights[k], late_ref.at[n], sems.at[n])
+        for n, k in enumerate((1, 2))
+    }
+    for copy in late.values():
+        copy.start()
     dot = functools.partial(
         lax.dot_general,
         dimension_numbers=(((1,), (1,)), ((), ())),
         preferred_element_type=F32,
     )
-    for k in range(blocks):
-        if k == blocks - 1:
-            late.wait()
-        if k == blocks // 2:
-            done = dot(rows_ref[:, :half], weights[k][...])
-            done += dot(rows_ref[:, half:], weights[blocks][...])
-        else:
-            done = dot(rows_ref[...], weights[k][...])
-        held_ref[k] = done.astype(BF16)
+    for k in (0, 3, 1, 2):
+        if k in late:
+            late[k].wait()
+        done = dot(rows_ref[...], late_ref[k - 1] if k in late else weights[k][...])
+        held_ref[k] = done
     core = place_ref[blocks]
     for k in range(blocks):
-        first = held_ref[place_ref[k], :size, :]
-        second = held_ref[place_ref[k], size:, :]
-        own_ref[k] = jnp.where(core == 0, first, second)
-        other_ref[k] = jnp.where(core == 0, second, first)
-
-
-def mix(place, rows, weights):
+        both = [held_ref[place_ref[k], n * size : (n + 1) * size, :] for n in range(2)]
+        for n, out_ref in enumerate((own_ref, other_ref)):
+            piece = jnp.where(core == n, both[0], both[1])
+            out_ref[k] = piece.reshape(own_ref.shape[1:]).astype(BF16)
+
+
+def mix(place, rows, weights, drafts):
     blocks = place.shape[0] - 1
     features = weights[0].shape[0]
     vmem = pl.BlockSpec(memory_space=pltpu.VMEM)
-    half = jax.ShapeDtypeStruct((blocks, rows.shape[0] // 2, features), BF16)
+    half = jax.ShapeDtypeStruct((blocks, rows.shape[0] // 2 // drafts, drafts, features), BF16)
     return pl.pallas_call(
         mix_kernel,
         out_shape=[half, half],
         in_specs=[
             pl.BlockSpec(memory_space=pltpu.SMEM),
             vmem,
-            *[pl.BlockSpec(memory_space=pl.ANY) if i == blocks - 1 else vmem for i in range(5)],
+            *[pl.BlockSpec(memory_space=pl.ANY) if i in (1, 2) else vmem for i in range(blocks)],
         ],
         out_specs=[vmem, vmem],
         scratch_shapes=[
-            pltpu.VMEM(weights[0].shape, BF16),
-            pltpu.VMEM((blocks, rows.shape[0], features), BF16),
-            pltpu.SemaphoreType.DMA,
+            pltpu.VMEM((2,) + weights[0].shape, BF16),
+            pltpu.VMEM((blocks, rows.shape[0], features), F32),
+            pltpu.SemaphoreType.DMA((2,)),
         ],
         compiler_params=pltpu.CompilerParams(vmem_limit_bytes=12 * 2**20),
         name="mix",
@@ -372,11 +361,8 @@
     planes = lenders // column
     up = [(l, (l - column) % lenders) for l in range(lenders)]
     down = [(l, (l + column) % lenders) for l in range(lenders)]
-    out_proj, local = lax.optimization_barrier((out_proj, local))
     weight = out_proj.T
-    half = weight.shape[1] // 2
     weight_up = lax.ppermute(weight, "lender", up)
-    weight_down = lax.ppermute(weight, "lender", down)
 
     part = jnp.einsum(
         "ishc,hcl->ihsl", draft_queries[..., :nope], key_absorb, preferred_element_type=F32
@@ -395,46 +381,40 @@
     )
 
     sending = lend(live_here, arrived, key_absorb, value_absorb, latent_pool, scale)
-    sending, weight_up, weight_down = lax.optimization_barrier((sending, weight_up, weight_down))
+    sending, weight = lax.optimization_barrier((sending, weight))
     back = lax.all_to_all(sending, "lender", split_axis=0, concat_axis=0, tiled=True)
-    far_left = lax.ppermute(weight_up[:, :half], "lender", up)
-    far_right = lax.ppermute(weight_down[:, half:], "lender", down)
+    weight_far = lax.ppermute(weight_up, "lender", up)
+    weight_down = lax.ppermute(weight, "lender", down)
 
     copies = settle(back, local, draft_scores, draft_values, column)
     inner = [[column * y + z for z in range(column)] for y in range(planes)]
     plane = lax.all_to_all(
         copies, "lender", split_axis=0, concat_axis=0, tiled=True, axis_index_groups=inner
     )
-    plane, far_left, far_right = lax.optimization_barrier((plane, far_left, far_right))
+    plane, weight_far, weight_down = lax.optimization_barrier((plane, weight_far, weight_down))
     y = home // column
     tensor = lax.axis_index("tensor")
     x, core = tensor // 2, tensor % 2
-    place = jnp.stack([(k - y) % planes for k in range(planes)] + [core]).astype(jnp.int32)
-    weight_down = pltpu.with_memory_space_constraint(weight_down, pltpu.HBM)
-    weights = [weight, weight_up, far_left, weight_down, far_right]
-    own, other = mix(place, plane.reshape(-1, plane.shape[-1]), weights)
+    place = jnp.stack([(x + k - y) % planes for k in range(planes)] + [core]).astype(jnp.int32)
+    weight_up, weight_far = (
+        pltpu.with_memory_space_constraint(w, pltpu.HBM) for w in (weight_up, weight_far)
+    )
+    weights = [weight, weight_up, weight_far, weight_down]
+    own, other = mix(place, plane.reshape(-1, plane.shape[-1]), weights, drafts)
 
     tensors = lax.axis_size("tensor")
     swap = [(t, t ^ 1) for t in range(tensors)]
     own = (own.astype(F32) + lax.ppermute(other, "tensor", swap).astype(F32)).astype(BF16)
-    chunks = jnp.broadcast_to(own[:, None], (planes, tensors // 2) + own.shape[1:])
-    chunks = chunks.reshape((planes * tensors // 2,) + own.shape[1:])
-    groups = [
-        [(column * p + z) * tensors + 2 * q + c for p in range(planes) for q in range(tensors // 2)]
-        for z in range(column)
-        for c in range(2)
-    ]
-    terms = lax.all_to_all(
-        chunks,
-        ("lender", "tensor"),
-        split_axis=0,
-        concat_axis=0,
-        tiled=True,
-        axis_index_groups=groups,
-    )
-    terms = lax.dynamic_slice_in_dim(terms, x * (tensors // 2), tensors // 2, 0)
-    total = jnp.sum(terms.astype(F32), axis=0)
-    return total.astype(BF16).reshape(-1, drafts, total.shape[-1])
+    total = None
+    for k in range(planes):
+        pairs = []
+        for index in range(lenders * tensors):
+            (source_y, z), source = divmod(index // tensors, column), index % tensors
+            lender = (source // 2 + k) % planes * column + z
+            pairs.append((index, lender * tensors + source_y * 2 + source % 2))
+        piece = lax.ppermute(own[k], ("lender", "tensor"), pairs).astype(F32)
+        total = piece if total is None else total + piece
+    return total.astype(BF16)
 
 
 def solution(mesh):

time: 111 us -> 105 us (0.946)
  local copies, waits for them, and re-layouts: 4.6 us -> 0.33 us
  waiting for transfers between devices: 42.6 us -> 39.5 us
  starting transfers between devices: 41.3 us -> 43.8 us
    ppermute x2 -> x5, waiting for transfers between devices: 0.01 us -> 8.79 us  [the longest x4 4.4 us: body(): piece = lax.ppermute(own[k], ('lender', 'tensor'), pairs).astype(F32)]
    all_to_all x1 -> x0, waiting for transfers between devices: 8.11 us -> none  [body(): lax.all_to_all(chunks, ('lender', 'tensor'), split_axis=0, concat_axis=0,...]
    ppermute x2 -> x5, starting transfers between devices: 2.68 us -> 10.8 us  [the longest x4 8.2 us: body(): piece = lax.ppermute(own[k], ('lender', 'tensor'), pairs).astype(F32)]
    all_to_all x1, waiting for transfers between devices: 9.39 us -> 2.5 us  [body(): lax.all_to_all(copies, 'lender', split_axis=0, concat_axis=0, tiled=True,...]
    all_to_all x1 -> x0, starting transfers between devices: 5.05 us -> none  [body(): lax.all_to_all(chunks, ('lender', 'tensor'), split_axis=0, concat_axis=0,...]
    all_to_all x1, waiting for transfers between devices: 8.5 us -> 12.4 us  [body(): lax.all_to_all(sending, 'lender', split_axis=0, concat_axis=0, tiled=True)]
    all_to_all x1, waiting for transfers between devices: 15.7 us -> 12.4 us  [body(): lax.all_to_all(outgoing, 'lender', split_axis=0, concat_axis=0, tiled=True)]
    slice x2 -> x0, local copies, waits for them, and re-layouts: 2.95 us -> none  [the longest x1 1.83 us: body(): far_right = lax.ppermute(weight_down[:, half:], 'lender', down)]
  transfers between devices with their start and end apart: 9 -> 11, of which waited for: 5 -> 8; matrix products, arithmetic and copies ran while one was open for 6% -> 4% of each run, Pallas kernels for 10% -> 10%
where the time goes in v4:
time: 105 us
  starting transfers between devices  43.8 us (42%)
  waiting for transfers between devices  39.5 us (38%)
  Pallas kernels  16.1 us (15%)
  matrix products  2.7 us (3%)
  other arithmetic  1.95 us (2%)
    all_to_all x1, waiting for transfers between devices, body(): lax.all_to_all(sending, 'lender', split_axis=0, concat_axis=0, tiled=True)  12.4 us
    all_to_all x1, waiting for transfers between devices, body(): lax.all_to_all(outgoing, 'lender', split_axis=0, concat_axis=0, tiled=True)  12.4 us
    all_to_all x1, starting transfers between devices, body(): lax.all_to_all(outgoing, 'lender', split_axis=0, concat_axis=0, tiled=True)  12.2 us
    pallas_call x1, Pallas kernels, lend(): pl.pallas_call(functools.partial(lend_kernel, scale, group), out_shape=pl...  8.5 us
    all_to_all x1, starting transfers between devices, body(): lax.all_to_all(sending, 'lender', split_axis=0, concat_axis=0, tiled=True)  8.49 us
    ppermute x4, starting transfers between devices, body(): piece = lax.ppermute(own[k], ('lender', 'tensor'), pairs).astype(F32)  8.2 us
    all_to_all x1, starting transfers between devices, body(): lax.all_to_all(copies, 'lender', split_axis=0, concat_axis=0, tiled=True,...  5.63 us
    ppermute x4, waiting for transfers between devices, body(): piece = lax.ppermute(own[k], ('lender', 'tensor'), pairs).astype(F32)  4.4 us
  transfers between devices with their start and end apart: 11, of which 8 were waited for; matrix products, arithmetic and copies ran while one was open for 4% of the time, Pallas kernels for 10%

profile of v4, /device:TPU:1, one launch (start us, length us, event | category | flops | bytes accessed | tf_op | source)
XLA Modules:
  0.0 104.6 jit_solution(4441384276435480756)
XLA Ops:
  0.0 0.0 copy-start.3
  0.0 0.0 copy-start
  0.0 2.3 %pack.1 = bf16[32,96,128]{2,1,0:T(8,128)(2,1)} custom-call(s32[1]{0:T(128)} %bitcast.5.home_ref, s32[32,32]{1,0:T(8,128)} %slot_request_ref.1, bf16[2,4,16,192]{3,2,1,0:T(8,128)(2,1)} %queries_ref.1), custom_call_target="tpu_custom_call" | custom-call | tf_op jit(solution)/shard_map/pack/pallas_call | solution.py:68
  2.4 0.0 copy-start.4
  2.4 0.0 copy-start.2
  2.4 0.0 copy-start.5
  2.4 12.2 %all-to-all-start = ((bf16[32,96,128]{2,1,0:T(8,128)(2,1)}), bf16[32,96,128]{2,1,0:T(8,128)(2,1)S(1)}, u32[]{:S(2)}, u32[]{:S(2)}) async-start(bf16[32,96,128]{2,1,0:T(8,128)(2,1)} %pack.1), calls=%async_computation | async-start | bytes 1572864 | tf_op jit(solution)/shard_map/all_to_all | solution.py:355
  14.6 2.6 %collective-permute-start = (bf16[224,2048]{1,0:T(8,128)(2,1)}, bf16[224,2048]{1,0:T(8,128)(2,1)}, u32[]{:S(2)}, u32[]{:S(2)}) collective-permute-start(bf16[224,2048]{1,0:T(8,128)(2,1)} %bitcast.47), channel_id=1, source_target_pairs={{0,192},{8,200},{16,208},{24,216},{32,224},{40,232},{48,240},{56,2... | collective-permute-start | bytes 2752520 | tf_op jit(solution)/shard_map/ppermute | solution.py:365
  17.1 0.0 copy-done.3
  17.2 0.0 copy-done
  17.2 0.4 fusion.7
  17.6 0.1 pad_maximum_fusion
  17.7 0.0 copy-done.4
  17.7 0.3 fusion.10
  18.0 0.1 copy.16
  18.2 0.0 copy-done.2
  18.2 0.2 subtract_reduce_fusion
  18.4 0.0 copy-done.5
  18.4 0.8 select_reduce_fusion.1
  19.2 0.2 select_reduce_fusion
  19.4 2.0 %fusion.2 = f32[2,4,16,128]{3,1,2,0:T(4,128)S(1)} fusion(bf16[16,512,128]{2,1,0:T(8,128)(2,1)} %values_any.1, bf16[2,4,576]{2,1,0:T(4,128)(2,1)S(1)} %copy-done.4), kind=kOutput, calls=%fused_computation.2 | convolution fusion | flops 16777216 | bytes 2170880 | tf_op jit(solution)/shard_map/ijl,hlc->ijhc/dot_general | solution.py:376
  21.4 12.4 %all-to-all-done.arrived_ref = bf16[32,96,128]{2,1,0:T(8,128)(2,1)S(1)} async-done(((bf16[32,96,128]{2,1,0:T(8,128)(2,1)}), bf16[32,96,128]{2,1,0:T(8,128)(2,1)S(1)}, u32[]{:S(2)}, u32[]{:S(2)}) %all-to-all-start) | async-done | bytes 786464 | tf_op jit(solution)/shard_map/all_to_all | solution.py:355
  33.8 8.5 %lend.1 = bf16[32,72,128]{2,1,0:T(8,128)(2,1)} custom-call(s32[32]{0:T(128)S(1)} %fusion.19.live_ref, bf16[32,96,128]{2,1,0:T(8,128)(2,1)S(1)} %all-to-all-done.arrived_ref, bf16[16,128,512]{2,1,0:T(8,128)(2,1)S(1)} %copy-done, bf16[16,512,128]{2,1,0:T(8,128)(2,1)} %values_any.1, bf16[32,192,576]{2,1,0:T(8,128)(2,1)} %pool_any.1), custom_call_target="tpu_custom_call" | custom-call | tf_op jit(solution)/shard_map/lend/pallas_call | solution.py:203
  42.3 0.0 copy-start.1
  42.4 8.5 %all-to-all-start.1 = ((bf16[32,72,128]{2,1,0:T(8,128)(2,1)}), bf16[32,72,128]{2,1,0:T(8,128)(2,1)S(1)}, u32[]{:S(2)}, u32[]{:S(2)}) async-start(bf16[32,72,128]{2,1,0:T(8,128)(2,1)} %lend.1), calls=%async_computation.1 | async-start | bytes 1179648 | tf_op jit(solution)/shard_map/all_to_all | solution.py:385
  50.9 0.0 collective-permute-done.refs_1_
  50.9 2.6 %collective-permute-start.1 = (bf16[224,2048]{1,0:T(8,128)(2,1)}, bf16[224,2048]{1,0:T(8,128)(2,1)}, u32[]{:S(2)}, u32[]{:S(2)}) collective-permute-start(bf16[224,2048]{1,0:T(8,128)(2,1)} %collective-permute-done.refs_1_), channel_id=1, source_target_pairs={{0,192},{8,200},{16,208},{24,216},{32,224},{40,232},{48,240},{56,2... | collective-permute-start | bytes 2752520 | tf_op jit(solution)/shard_map/ppermute | solution.py:386
  53.4 0.0 collective-permute-start.2
  53.4 12.4 %all-to-all-done.1.back_ref = bf16[32,72,128]{2,1,0:T(8,128)(2,1)S(1)} async-done(((bf16[32,72,128]{2,1,0:T(8,128)(2,1)}), bf16[32,72,128]{2,1,0:T(8,128)(2,1)S(1)}, u32[]{:S(2)}, u32[]{:S(2)}) %all-to-all-start.1) | async-done | bytes 589856 | tf_op jit(solution)/shard_map/all_to_all | solution.py:385
  65.9 2.3 %settle.1 = bf16[8,8,2048]{2,1,0:T(8,128)(2,1)} custom-call(bf16[32,72,128]{2,1,0:T(8,128)(2,1)S(1)} %all-to-all-done.1.back_ref, s32[1,32]{1,0:T(1,128)S(1)} %bitcast.51, f32[2,64,4]{2,1,0:T(8,128)S(1)} %bitcast.50, f32[2,4,16,128]{3,2,1,0:T(8,128)S(1)} %copy.17.draft_values_ref), custom_call_target="tpu_custom_call" | custom-call | tf_op jit(solution)/shard_map/settle/pallas_call | solution.py:266
  68.2 5.6 %all-to-all-start.2 = ((bf16[8,8,2048]{2,1,0:T(8,128)(2,1)}), bf16[8,8,2048]{2,1,0:T(8,128)(2,1)S(1)}, u32[]{:S(2)}, u32[]{:S(2)}) async-start(bf16[8,8,2048]{2,1,0:T(8,128)(2,1)} %settle.1), calls=%async_computation.2 | async-start | bytes 524288 | tf_op jit(solution)/shard_map/all_to_all | solution.py:391
  73.8 0.1 stack.23.place_ref
  73.9 4.4 %collective-permute-done.1.refs_2_ = bf16[224,2048]{1,0:T(8,128)(2,1)} collective-permute-done((bf16[224,2048]{1,0:T(8,128)(2,1)}, bf16[224,2048]{1,0:T(8,128)(2,1)}, u32[]{:S(2)}, u32[]{:S(2)}) %collective-permute-start.1) | collective-permute-done | bytes 917536 | tf_op jit(solution)/shard_map/ppermute | solution.py:386
  78.3 2.4 %collective-permute-done.2.refs_3_ = bf16[224,2048]{1,0:T(8,128)(2,1)S(1)} collective-permute-done((bf16[224,2048]{1,0:T(8,128)(2,1)}, bf16[224,2048]{1,0:T(8,128)(2,1)S(1)}, u32[]{:S(2)}, u32[]{:S(2)}) %collective-permute-start.2) | collective-permute-done | bytes 917536 | tf_op jit(solution)/shard_map/ppermute | solution.py:387
  80.7 2.5 %all-to-all-done.2 = bf16[8,8,2048]{2,1,0:T(8,128)(2,1)S(1)} async-done(((bf16[8,8,2048]{2,1,0:T(8,128)(2,1)}), bf16[8,8,2048]{2,1,0:T(8,128)(2,1)S(1)}, u32[]{:S(2)}, u32[]{:S(2)}) %all-to-all-start.2) | async-done | bytes 262176 | tf_op jit(solution)/shard_map/all_to_all | solution.py:391
  83.2 0.0 copy-done.1
  83.2 3.0 %mix.1 = (bf16[4,8,4,224]{3,2,1,0:T(4,128)(2,1)S(1)}, bf16[4,8,4,224]{3,2,1,0:T(4,128)(2,1)S(1)}) custom-call(s32[5]{0:T(128)S(1)} %stack.23.place_ref, bf16[64,2048]{1,0:T(8,128)(2,1)S(1)} %bitcast.46, bf16[224,2048]{1,0:T(8,128)(2,1)S(1)} %bitcast.49, bf16[224,2048]{1,0:T(8,128)(2,1)} %collective-permute-done.refs_1_, ...), custom_call_target="tpu_custom_call" | custom-call | tf_op jit(solution)/shard_map/mix/pallas_call | solution.py:313
  86.2 4.2 %collective-permute-start.3 = (bf16[4,8,4,224]{3,2,1,0:T(4,128)(2,1)S(1)}, bf16[4,8,4,224]{3,2,1,0:T(4,128)(2,1)S(1)}, u32[]{:S(2)}, u32[]{:S(2)}) collective-permute-start(bf16[4,8,4,224]{3,2,1,0:T(4,128)(2,1)S(1)} %get-tuple-element.40), channel_id=1, source_target_pairs={{0,1},{1,0},{2,3},{3,2},{4,5},{5,4},{6,7},{7,6},{8,9},{9,8},{10,11... | collective-permute-start | bytes 172040 | tf_op jit(solution)/shard_map/ppermute | solution.py:407
  90.4 0.9 collective-permute-done.3
  91.3 0.7 collective-permute-start.4
  92.0 6.2 %collective-permute-start.7 = (bf16[8,4,224]{2,1,0:T(4,128)(2,1)S(1)}, bf16[8,4,224]{2,1,0:T(4,128)(2,1)S(1)}, u32[]{:S(2)}, u32[]{:S(2)}) collective-permute-start(bf16[8,4,224]{2,1,0:T(4,128)(2,1)S(1)} %get-tuple-element.42), channel_id=1, source_target_pairs={{0,192},{1,193},{2,0},{3,1},{4,64},{5,65},{6,128},{7,129},{8,200},... | collective-permute-start | bytes 43016 | tf_op jit(solution)/shard_map/ppermute | solution.py:415
  98.2 1.4 %collective-permute-start.6 = (bf16[8,4,224]{2,1,0:T(4,128)(2,1)S(1)}, bf16[8,4,224]{2,1,0:T(4,128)(2,1)S(1)}, u32[]{:S(2)}, u32[]{:S(2)}) collective-permute-start(bf16[8,4,224]{2,1,0:T(4,128)(2,1)S(1)} %get-tuple-element.43), channel_id=1, source_target_pairs={{0,128},{1,129},{2,192},{3,193},{4,0},{5,1},{6,64},{7,65},{8,136},... | collective-permute-start | bytes 43016 | tf_op jit(solution)/shard_map/ppermute | solution.py:415
  99.5 0.0 collective-permute-start.5
  99.5 0.0 collective-permute-done.4
  99.5 0.0 collective-permute-done.7
  99.6 2.8 %collective-permute-done.6 = bf16[8,4,224]{2,1,0:T(4,128)(2,1)S(1)} collective-permute-done((bf16[8,4,224]{2,1,0:T(4,128)(2,1)S(1)}, bf16[8,4,224]{2,1,0:T(4,128)(2,1)S(1)}, u32[]{:S(2)}, u32[]{:S(2)}) %collective-permute-start.6) | collective-permute-done | bytes 14368 | tf_op jit(solution)/shard_map/ppermute | solution.py:415
  102.4 1.6 %collective-permute-done.5 = bf16[8,4,224]{2,1,0:T(4,128)(2,1)S(1)} collective-permute-done((bf16[8,4,224]{2,1,0:T(4,128)(2,1)S(1)}, bf16[8,4,224]{2,1,0:T(4,128)(2,1)S(1)}, u32[]{:S(2)}, u32[]{:S(2)}) %collective-permute-start.5) | collective-permute-done | bytes 14368 | tf_op jit(solution)/shard_map/ppermute | solution.py:415
  104.0 0.6 add_convert_fusion.1
  (8 shorter events, 0.2 us)
Async XLA Ops:
  0.0 17.1 %copy-start.3 = (bf16[2,4,16,192]{3,2,1,0:T(8,128)(2,1)S(1)}, bf16[2,4,16,192]{3,2,1,0:T(8,128)(2,1)}, u32[]{:S(2)}) copy-start(bf16[2,4,16,192]{3,2,1,0:T(8,128)(2,1)} %queries_ref.1) | copy-start | bytes 147460
  0.0 17.2 %copy-start = (bf16[16,128,512]{2,1,0:T(8,128)(2,1)S(1)}, bf16[16,128,512]{2,1,0:T(8,128)(2,1)}, u32[]{:S(2)}) copy-start(bf16[16,128,512]{2,1,0:T(8,128)(2,1)} %keys_ref.1) | copy-start | bytes 6291460
  2.4 15.3 %copy-start.4 = (bf16[2,4,576]{2,1,0:T(4,128)(2,1)S(1)}, bf16[2,4,576]{2,1,0:T(4,128)(2,1)}, u32[]{:S(2)}) copy-start(bf16[2,4,576]{2,1,0:T(4,128)(2,1)} %param.9) | copy-start | bytes 27652
  2.4 15.8 %copy-start.2 = (s32[32,32]{1,0:T(8,128)S(1)}, s32[32,32]{1,0:T(8,128)}, u32[]{:S(2)}) copy-start(s32[32,32]{1,0:T(8,128)} %slot_request_ref.1) | copy-start | bytes 12292
  2.4 16.0 %copy-start.5 = (s32[64]{0:T(128)S(1)}, s32[64]{0:T(128)}, u32[]{:S(2)}) copy-start(s32[64]{0:T(128)} %param.15) | copy-start | bytes 772
  2.4 31.4 %all-to-all-start = ((bf16[32,96,128]{2,1,0:T(8,128)(2,1)}), bf16[32,96,128]{2,1,0:T(8,128)(2,1)S(1)}, u32[]{:S(2)}, u32[]{:S(2)}) async-start(bf16[32,96,128]{2,1,0:T(8,128)(2,1)} %pack.1), calls=%async_computation | async-start | bytes 1572864 | tf_op jit(solution)/shard_map/all_to_all | solution.py:355
  14.6 36.3 %collective-permute-start = (bf16[224,2048]{1,0:T(8,128)(2,1)}, bf16[224,2048]{1,0:T(8,128)(2,1)}, u32[]{:S(2)}, u32[]{:S(2)}) collective-permute-start(bf16[224,2048]{1,0:T(8,128)(2,1)} %bitcast.47), channel_id=1, source_target_pairs={{0,192},{8,200},{16,208},{24,216},{32,224},{40,232},{48,240},{56,2... | collective-permute-start | bytes 2752520 | tf_op jit(solution)/shard_map/ppermute | solution.py:365
  42.3 40.9 %copy-start.1 = (bf16[2048,224]{0,1:T(8,128)(2,1)S(1)}, bf16[2048,224]{0,1:T(8,128)(2,1)}, u32[]{:S(2)}) copy-start(bf16[2048,224]{0,1:T(8,128)(2,1)} %param.13) | copy-start | bytes 2752516
  42.4 23.5 %all-to-all-start.1 = ((bf16[32,72,128]{2,1,0:T(8,128)(2,1)}), bf16[32,72,128]{2,1,0:T(8,128)(2,1)S(1)}, u32[]{:S(2)}, u32[]{:S(2)}) async-start(bf16[32,72,128]{2,1,0:T(8,128)(2,1)} %lend.1), calls=%async_computation.1 | async-start | bytes 1179648 | tf_op jit(solution)/shard_map/all_to_all | solution.py:385
  50.9 27.4 %collective-permute-start.1 = (bf16[224,2048]{1,0:T(8,128)(2,1)}, bf16[224,2048]{1,0:T(8,128)(2,1)}, u32[]{:S(2)}, u32[]{:S(2)}) collective-permute-start(bf16[224,2048]{1,0:T(8,128)(2,1)} %collective-permute-done.refs_1_), channel_id=1, source_target_pairs={{0,192},{8,200},{16,208},{24,216},{32,224},{40,232},{48,240},{56,2... | collective-permute-start | bytes 2752520 | tf_op jit(solution)/shard_map/ppermute | solution.py:386
  53.4 27.3 %collective-permute-start.2 = (bf16[224,2048]{1,0:T(8,128)(2,1)}, bf16[224,2048]{1,0:T(8,128)(2,1)S(1)}, u32[]{:S(2)}, u32[]{:S(2)}) collective-permute-start(bf16[224,2048]{1,0:T(8,128)(2,1)} %bitcast.48), channel_id=1, source_target_pairs={{0,64},{8,72},{16,80},{24,88},{32,96},{40,104},{48,112},{56,120},{... | collective-permute-start | bytes 2752520 | tf_op jit(solution)/shard_map/ppermute | solution.py:387
  68.2 15.0 %all-to-all-start.2 = ((bf16[8,8,2048]{2,1,0:T(8,128)(2,1)}), bf16[8,8,2048]{2,1,0:T(8,128)(2,1)S(1)}, u32[]{:S(2)}, u32[]{:S(2)}) async-start(bf16[8,8,2048]{2,1,0:T(8,128)(2,1)} %settle.1), calls=%async_computation.2 | async-start | bytes 524288 | tf_op jit(solution)/shard_map/all_to_all | solution.py:391
  86.2 5.1 %collective-permute-start.3 = (bf16[4,8,4,224]{3,2,1,0:T(4,128)(2,1)S(1)}, bf16[4,8,4,224]{3,2,1,0:T(4,128)(2,1)S(1)}, u32[]{:S(2)}, u32[]{:S(2)}) collective-permute-start(bf16[4,8,4,224]{3,2,1,0:T(4,128)(2,1)S(1)} %get-tuple-element.40), channel_id=1, source_target_pairs={{0,1},{1,0},{2,3},{3,2},{4,5},{5,4},{6,7},{7,6},{8,9},{9,8},{10,11... | collective-permute-start | bytes 172040 | tf_op jit(solution)/shard_map/ppermute | solution.py:407
  91.3 8.2 %collective-permute-start.4 = (bf16[8,4,224]{2,1,0:T(4,128)(2,1)S(1)}, bf16[8,4,224]{2,1,0:T(4,128)(2,1)S(1)}, u32[]{:S(2)}, u32[]{:S(2)}) collective-permute-start(bf16[8,4,224]{2,1,0:T(4,128)(2,1)S(1)} %get-tuple-element.41), channel_id=1, source_target_pairs={{0,0},{1,1},{2,64},{3,65},{4,128},{5,129},{6,192},{7,193},{8,8},{9... | collective-permute-start | bytes 43016 | tf_op jit(solution)/shard_map/ppermute | solution.py:415
  92.0 7.5 %collective-permute-start.7 = (bf16[8,4,224]{2,1,0:T(4,128)(2,1)S(1)}, bf16[8,4,224]{2,1,0:T(4,128)(2,1)S(1)}, u32[]{:S(2)}, u32[]{:S(2)}) collective-permute-start(bf16[8,4,224]{2,1,0:T(4,128)(2,1)S(1)} %get-tuple-element.42), channel_id=1, source_target_pairs={{0,192},{1,193},{2,0},{3,1},{4,64},{5,65},{6,128},{7,129},{8,200},... | collective-permute-start | bytes 43016 | tf_op jit(solution)/shard_map/ppermute | solution.py:415
  98.2 4.2 %collective-permute-start.6 = (bf16[8,4,224]{2,1,0:T(4,128)(2,1)S(1)}, bf16[8,4,224]{2,1,0:T(4,128)(2,1)S(1)}, u32[]{:S(2)}, u32[]{:S(2)}) collective-permute-start(bf16[8,4,224]{2,1,0:T(4,128)(2,1)S(1)} %get-tuple-element.43), channel_id=1, source_target_pairs={{0,128},{1,129},{2,192},{3,193},{4,0},{5,1},{6,64},{7,65},{8,136},... | collective-permute-start | bytes 43016 | tf_op jit(solution)/shard_map/ppermute | solution.py:415
  99.5 4.4 %collective-permute-start.5 = (bf16[8,4,224]{2,1,0:T(4,128)(2,1)S(1)}, bf16[8,4,224]{2,1,0:T(4,128)(2,1)S(1)}, u32[]{:S(2)}, u32[]{:S(2)}) collective-permute-start(bf16[8,4,224]{2,1,0:T(4,128)(2,1)S(1)} %get-tuple-element.44), channel_id=1, source_target_pairs={{0,64},{1,65},{2,128},{3,129},{4,192},{5,193},{6,0},{7,1},{8,72},{... | collective-permute-start | bytes 43016 | tf_op jit(solution)/shard_map/ppermute | solution.py:415

commit v5 on v4

--- a/solution.py
+++ b/solution.py
@@ -279,8 +279,7 @@
 
 def mix_kernel(place_ref, rows_ref, *refs):
     weights, (own_ref, other_ref, late_ref, held_ref, sems) = refs[:-5], refs[-5:]
-    blocks = own_ref.shape[0]
-    size, features = held_ref.shape[-2] // 2, held_ref.shape[-1]
+    blocks = held_ref.shape[0]
     late = {
         k: pltpu.make_async_copy(weights[k], late_ref.at[n], sems.at[n])
         for n, k in enumerate((1, 2))
@@ -297,19 +296,17 @@
             late[k].wait()
         done = dot(rows_ref[...], late_ref[k - 1] if k in late else weights[k][...])
         held_ref[k] = done
-    core = place_ref[blocks]
-    for k in range(blocks):
-        both = [held_ref[place_ref[k], n * size : (n + 1) * size, :] for n in range(2)]
-        for n, out_ref in enumerate((own_ref, other_ref)):
-            piece = jnp.where(core == n, both[0], both[1])
-            out_ref[k] = piece.reshape(own_ref.shape[1:]).astype(BF16)
+    for n in range(blocks):
+        out_ref = (own_ref, other_ref)[n * 2 // blocks]
+        piece = held_ref[place_ref[n]]
+        out_ref[n % (blocks // 2)] = piece.reshape(out_ref.shape[1:]).astype(BF16)
 
 
 def mix(place, rows, weights, drafts):
-    blocks = place.shape[0] - 1
+    blocks = place.shape[0]
     features = weights[0].shape[0]
     vmem = pl.BlockSpec(memory_space=pltpu.VMEM)
-    half = jax.ShapeDtypeStruct((blocks, rows.shape[0] // 2 // drafts, drafts, features), BF16)
+    half = jax.ShapeDtypeStruct((blocks // 2, rows.shape[0] // drafts, drafts, features), BF16)
     return pl.pallas_call(
         mix_kernel,
         out_shape=[half, half],
@@ -395,7 +392,8 @@
     y = home // column
     tensor = lax.axis_index("tensor")
     x, core = tensor // 2, tensor % 2
-    place = jnp.stack([(x + k - y) % planes for k in range(planes)] + [core]).astype(jnp.int32)
+    turns = [core, core + 2, 1 - core, 3 - core]
+    place = jnp.stack([(x + k - y) % planes for k in turns]).astype(jnp.int32)
     weight_up, weight_far = (
         pltpu.with_memory_space_constraint(w, pltpu.HBM) for w in (weight_up, weight_far)
     )
@@ -406,15 +404,18 @@
     swap = [(t, t ^ 1) for t in range(tensors)]
     own = (own.astype(F32) + lax.ppermute(other, "tensor", swap).astype(F32)).astype(BF16)
     total = None
-    for k in range(planes):
+    for j in range(planes // 2):
         pairs = []
         for index in range(lenders * tensors):
             (source_y, z), source = divmod(index // tensors, column), index % tensors
-            lender = (source // 2 + k) % planes * column + z
+            lender = (source // 2 + source % 2 + 2 * j) % planes * column + z
             pairs.append((index, lender * tensors + source_y * 2 + source % 2))
-        piece = lax.ppermute(own[k], ("lender", "tensor"), pairs).astype(F32)
+        piece = lax.ppermute(own[j], ("lender", "tensor"), pairs).astype(F32)
         total = piece if total is None else total + piece
-    return total.astype(BF16)
+    half = total.shape[0] // 2
+    mine = jnp.where(core == 0, total[:half], total[half:])
+    theirs = jnp.where(core == 0, total[half:], total[:half])
+    return (mine + lax.ppermute(theirs, "tensor", swap)).astype(BF16)
 
 
 def solution(mesh):

time: 105 us -> 103 us (0.981)
  waiting for transfers between devices: 39.5 us -> 37 us
    ppermute x4 -> x3, waiting for transfers between devices: 4.4 us -> 1.88 us  [the longest x2 1.02 us: body(): piece = lax.ppermute(own[j], ('lender', 'tensor'), pairs).astype(F32)]
    ppermute x4 -> x3, starting transfers between devices: 8.2 us -> 8.99 us  [the longest x2 7.17 us: body(): piece = lax.ppermute(own[j], ('lender', 'tensor'), pairs).astype(F32)]
  transfers between devices with their start and end apart: 11 -> 10, of which waited for: 8 -> 8; matrix products, arithmetic and copies ran while one was open for 4% -> 4% of each run, Pallas kernels for 10% -> 10%
where the time goes in v5:
time: 103 us
  starting transfers between devices  44.6 us (43%)
  waiting for transfers between devices  37 us (36%)
  Pallas kernels  16.1 us (16%)
  matrix products  2.7 us (3%)
  other arithmetic  2.04 us (2%)
    all_to_all x1, waiting for transfers between devices, body(): lax.all_to_all(sending, 'lender', split_axis=0, concat_axis=0, tiled=True)  12.4 us
    all_to_all x1, waiting for transfers between devices, body(): lax.all_to_all(outgoing, 'lender', split_axis=0, concat_axis=0, tiled=True)  12.4 us
    all_to_all x1, starting transfers between devices, body(): lax.all_to_all(outgoing, 'lender', split_axis=0, concat_axis=0, tiled=True)  12.2 us
    all_to_all x1, starting transfers between devices, body(): lax.all_to_all(sending, 'lender', split_axis=0, concat_axis=0, tiled=True)  8.5 us
    pallas_call x1, Pallas kernels, lend(): pl.pallas_call(functools.partial(lend_kernel, scale, group), out_shape=pl...  8.5 us
    ppermute x2, starting transfers between devices, body(): piece = lax.ppermute(own[j], ('lender', 'tensor'), pairs).astype(F32)  7.17 us
    all_to_all x1, starting transfers between devices, body(): lax.all_to_all(copies, 'lender', split_axis=0, concat_axis=0, tiled=True,...  5.63 us
    ppermute x1, waiting for transfers between devices, body(): weight_far = lax.ppermute(weight_up, 'lender', up)  4.4 us
  transfers between devices with their start and end apart: 10, of which 8 were waited for; matrix products, arithmetic and copies ran while one was open for 4% of the time, Pallas kernels for 10%

profile of v5, /device:TPU:1, one launch (start us, length us, event | category | flops | bytes accessed | tf_op | source)
XLA Modules:
  0.0 102.9 jit_solution(5610766733719112249)
XLA Ops:
  0.0 0.0 copy-start.3
  0.0 0.0 copy-start
  0.0 2.3 %pack.1 = bf16[32,96,128]{2,1,0:T(8,128)(2,1)} custom-call(s32[1]{0:T(128)} %bitcast.4.home_ref, s32[32,32]{1,0:T(8,128)} %slot_request_ref.1, bf16[2,4,16,192]{3,2,1,0:T(8,128)(2,1)} %queries_ref.1), custom_call_target="tpu_custom_call" | custom-call | tf_op jit(solution)/shard_map/pack/pallas_call | solution.py:68
  2.4 0.0 copy-start.4
  2.4 0.0 copy-start.2
  2.4 0.0 copy-start.5
  2.4 12.2 %all-to-all-start = ((bf16[32,96,128]{2,1,0:T(8,128)(2,1)}), bf16[32,96,128]{2,1,0:T(8,128)(2,1)S(1)}, u32[]{:S(2)}, u32[]{:S(2)}) async-start(bf16[32,96,128]{2,1,0:T(8,128)(2,1)} %pack.1), calls=%async_computation | async-start | bytes 1572864 | tf_op jit(solution)/shard_map/all_to_all | solution.py:352
  14.6 2.6 %collective-permute-start = (bf16[224,2048]{1,0:T(8,128)(2,1)}, bf16[224,2048]{1,0:T(8,128)(2,1)}, u32[]{:S(2)}, u32[]{:S(2)}) collective-permute-start(bf16[224,2048]{1,0:T(8,128)(2,1)} %bitcast.45), channel_id=1, source_target_pairs={{0,192},{8,200},{16,208},{24,216},{32,224},{40,232},{48,240},{56,2... | collective-permute-start | bytes 2752520 | tf_op jit(solution)/shard_map/ppermute | solution.py:362
  17.1 0.0 copy-done.3
  17.2 0.0 copy-done
  17.2 0.4 fusion.7
  17.6 0.1 pad_maximum_fusion
  17.7 0.0 copy-done.4
  17.7 0.3 fusion.10
  18.1 0.1 copy.16
  18.2 0.0 copy-done.2
  18.2 0.2 subtract_reduce_fusion
  18.4 0.0 copy-done.5
  18.4 0.8 select_reduce_fusion.1
  19.2 0.2 select_reduce_fusion
  19.4 2.0 %fusion.2 = f32[2,4,16,128]{3,1,2,0:T(4,128)S(1)} fusion(bf16[16,512,128]{2,1,0:T(8,128)(2,1)} %values_any.1, bf16[2,4,576]{2,1,0:T(4,128)(2,1)S(1)} %copy-done.4), kind=kOutput, calls=%fused_computation.2 | convolution fusion | flops 16777216 | bytes 2170880 | tf_op jit(solution)/shard_map/ijl,hlc->ijhc/dot_general | solution.py:373
  21.4 12.4 %all-to-all-done.arrived_ref = bf16[32,96,128]{2,1,0:T(8,128)(2,1)S(1)} async-done(((bf16[32,96,128]{2,1,0:T(8,128)(2,1)}), bf16[32,96,128]{2,1,0:T(8,128)(2,1)S(1)}, u32[]{:S(2)}, u32[]{:S(2)}) %all-to-all-start) | async-done | bytes 786464 | tf_op jit(solution)/shard_map/all_to_all | solution.py:352
  33.8 8.5 %lend.1 = bf16[32,72,128]{2,1,0:T(8,128)(2,1)} custom-call(s32[32]{0:T(128)S(1)} %fusion.19.live_ref, bf16[32,96,128]{2,1,0:T(8,128)(2,1)S(1)} %all-to-all-done.arrived_ref, bf16[16,128,512]{2,1,0:T(8,128)(2,1)S(1)} %copy-done, bf16[16,512,128]{2,1,0:T(8,128)(2,1)} %values_any.1, bf16[32,192,576]{2,1,0:T(8,128)(2,1)} %pool_any.1), custom_call_target="tpu_custom_call" | custom-call | tf_op jit(solution)/shard_map/lend/pallas_call | solution.py:203
  42.3 0.0 copy-start.1
  42.4 8.5 %all-to-all-start.1 = ((bf16[32,72,128]{2,1,0:T(8,128)(2,1)}), bf16[32,72,128]{2,1,0:T(8,128)(2,1)S(1)}, u32[]{:S(2)}, u32[]{:S(2)}) async-start(bf16[32,72,128]{2,1,0:T(8,128)(2,1)} %lend.1), calls=%async_computation.1 | async-start | bytes 1179648 | tf_op jit(solution)/shard_map/all_to_all | solution.py:382
  50.9 0.0 collective-permute-done.refs_1_
  50.9 2.6 %collective-permute-start.1 = (bf16[224,2048]{1,0:T(8,128)(2,1)}, bf16[224,2048]{1,0:T(8,128)(2,1)}, u32[]{:S(2)}, u32[]{:S(2)}) collective-permute-start(bf16[224,2048]{1,0:T(8,128)(2,1)} %collective-permute-done.refs_1_), channel_id=1, source_target_pairs={{0,192},{8,200},{16,208},{24,216},{32,224},{40,232},{48,240},{56,2... | collective-permute-start | bytes 2752520 | tf_op jit(solution)/shard_map/ppermute | solution.py:383
  53.4 0.0 collective-permute-start.2
  53.5 12.4 %all-to-all-done.1.back_ref = bf16[32,72,128]{2,1,0:T(8,128)(2,1)S(1)} async-done(((bf16[32,72,128]{2,1,0:T(8,128)(2,1)}), bf16[32,72,128]{2,1,0:T(8,128)(2,1)S(1)}, u32[]{:S(2)}, u32[]{:S(2)}) %all-to-all-start.1) | async-done | bytes 589856 | tf_op jit(solution)/shard_map/all_to_all | solution.py:382
  65.9 2.3 %settle.1 = bf16[8,8,2048]{2,1,0:T(8,128)(2,1)} custom-call(bf16[32,72,128]{2,1,0:T(8,128)(2,1)S(1)} %all-to-all-done.1.back_ref, s32[1,32]{1,0:T(1,128)S(1)} %bitcast.49, f32[2,64,4]{2,1,0:T(8,128)S(1)} %bitcast.48, f32[2,4,16,128]{3,2,1,0:T(8,128)S(1)} %copy.17.draft_values_ref), custom_call_target="tpu_custom_call" | custom-call | tf_op jit(solution)/shard_map/settle/pallas_call | solution.py:266
  68.2 5.6 %all-to-all-start.2 = ((bf16[8,8,2048]{2,1,0:T(8,128)(2,1)}), bf16[8,8,2048]{2,1,0:T(8,128)(2,1)S(1)}, u32[]{:S(2)}, u32[]{:S(2)}) async-start(bf16[8,8,2048]{2,1,0:T(8,128)(2,1)} %settle.1), calls=%async_computation.2 | async-start | bytes 524288 | tf_op jit(solution)/shard_map/all_to_all | solution.py:388
  73.8 0.1 pad_add_fusion.place_ref
  73.9 4.4 %collective-permute-done.1.refs_2_ = bf16[224,2048]{1,0:T(8,128)(2,1)} collective-permute-done((bf16[224,2048]{1,0:T(8,128)(2,1)}, bf16[224,2048]{1,0:T(8,128)(2,1)}, u32[]{:S(2)}, u32[]{:S(2)}) %collective-permute-start.1) | collective-permute-done | bytes 917536 | tf_op jit(solution)/shard_map/ppermute | solution.py:383
  78.3 2.4 %collective-permute-done.2.refs_3_ = bf16[224,2048]{1,0:T(8,128)(2,1)S(1)} collective-permute-done((bf16[224,2048]{1,0:T(8,128)(2,1)}, bf16[224,2048]{1,0:T(8,128)(2,1)S(1)}, u32[]{:S(2)}, u32[]{:S(2)}) %collective-permute-start.2) | collective-permute-done | bytes 917536 | tf_op jit(solution)/shard_map/ppermute | solution.py:384
  80.7 2.5 %all-to-all-done.2 = bf16[8,8,2048]{2,1,0:T(8,128)(2,1)S(1)} async-done(((bf16[8,8,2048]{2,1,0:T(8,128)(2,1)}), bf16[8,8,2048]{2,1,0:T(8,128)(2,1)S(1)}, u32[]{:S(2)}, u32[]{:S(2)}) %all-to-all-start.2) | async-done | bytes 262176 | tf_op jit(solution)/shard_map/all_to_all | solution.py:388
  83.2 0.0 copy-done.1
  83.2 3.0 %mix.1 = (bf16[2,16,4,224]{3,2,1,0:T(4,128)(2,1)S(1)}, bf16[2,16,4,224]{3,2,1,0:T(4,128)(2,1)S(1)}) custom-call(s32[4]{0:T(128)S(1)} %pad_add_fusion.place_ref, bf16[64,2048]{1,0:T(8,128)(2,1)S(1)} %bitcast.44, bf16[224,2048]{1,0:T(8,128)(2,1)S(1)} %bitcast.47, bf16[224,2048]{1,0:T(8,128)(2,1)} %collective-permute-done.refs_1_, ...), custom_call_target="tpu_custom_call" | custom-call | tf_op jit(solution)/shard_map/mix/pallas_call | solution.py:310
  86.2 4.2 %collective-permute-start.3 = (bf16[2,16,4,224]{3,2,1,0:T(4,128)(2,1)S(1)}, bf16[2,16,4,224]{3,2,1,0:T(4,128)(2,1)S(1)}, u32[]{:S(2)}, u32[]{:S(2)}) collective-permute-start(bf16[2,16,4,224]{3,2,1,0:T(4,128)(2,1)S(1)} %get-tuple-element.40), channel_id=1, source_target_pairs={{0,1},{1,0},{2,3},{3,2},{4,5},{5,4},{6,7},{7,6},{8,9},{9,8},{10,11... | collective-permute-start | bytes 172040 | tf_op jit(solution)/shard_map/ppermute | solution.py:405
  90.4 0.9 collective-permute-done.3
  91.3 2.5 %collective-permute-start.4 = (bf16[16,4,224]{2,1,0:T(4,128)(2,1)S(1)}, bf16[16,4,224]{2,1,0:T(4,128)(2,1)S(1)}, u32[]{:S(2)}, u32[]{:S(2)}) collective-permute-start(bf16[16,4,224]{2,1,0:T(4,128)(2,1)S(1)} %get-tuple-element.41), channel_id=1, source_target_pairs={{0,0},{1,65},{2,64},{3,129},{4,128},{5,193},{6,192},{7,1},{8,8},{9... | collective-permute-start | bytes 86024 | tf_op jit(solution)/shard_map/ppermute | solution.py:413
  93.9 4.7 %collective-permute-start.5 = (bf16[16,4,224]{2,1,0:T(4,128)(2,1)S(1)}, bf16[16,4,224]{2,1,0:T(4,128)(2,1)S(1)}, u32[]{:S(2)}, u32[]{:S(2)}) collective-permute-start(bf16[16,4,224]{2,1,0:T(4,128)(2,1)S(1)} %get-tuple-element.42), channel_id=1, source_target_pairs={{0,128},{1,193},{2,192},{3,1},{4,0},{5,65},{6,64},{7,129},{8,136},... | collective-permute-start | bytes 86024 | tf_op jit(solution)/shard_map/ppermute | solution.py:413
  98.5 0.0 collective-permute-done.4
  98.5 1.0 collective-permute-done.5
  99.6 1.8 %collective-permute-start.6 = (f32[8,4,224]{2,1,0:T(4,128)S(1)}, f32[8,4,224]{2,1,0:T(4,128)S(1)}, u32[]{:S(2)}, u32[]{:S(2)}) collective-permute-start(f32[8,4,224]{2,1,0:T(4,128)S(1)} %slice_select_fusion), channel_id=1, source_target_pairs={{0,1},{1,0},{2,3},{3,2},{4,5},{5,4},{6,7},{7,6},{8,9},{9,8},{10,11... | collective-permute-start | bytes 86024 | tf_op jit(solution)/shard_map/ppermute | solution.py:418
  101.4 0.9 collective-permute-done.6
  102.3 0.6 add_convert_fusion.1
  (10 shorter events, 0.2 us)
Async XLA Ops:
  0.0 17.1 %copy-start.3 = (bf16[2,4,16,192]{3,2,1,0:T(8,128)(2,1)S(1)}, bf16[2,4,16,192]{3,2,1,0:T(8,128)(2,1)}, u32[]{:S(2)}) copy-start(bf16[2,4,16,192]{3,2,1,0:T(8,128)(2,1)} %queries_ref.1) | copy-start | bytes 147460
  0.0 17.2 %copy-start = (bf16[16,128,512]{2,1,0:T(8,128)(2,1)S(1)}, bf16[16,128,512]{2,1,0:T(8,128)(2,1)}, u32[]{:S(2)}) copy-start(bf16[16,128,512]{2,1,0:T(8,128)(2,1)} %keys_ref.1) | copy-start | bytes 6291460
  2.4 15.3 %copy-start.4 = (bf16[2,4,576]{2,1,0:T(4,128)(2,1)S(1)}, bf16[2,4,576]{2,1,0:T(4,128)(2,1)}, u32[]{:S(2)}) copy-start(bf16[2,4,576]{2,1,0:T(4,128)(2,1)} %param.9) | copy-start | bytes 27652
  2.4 15.8 %copy-start.2 = (s32[32,32]{1,0:T(8,128)S(1)}, s32[32,32]{1,0:T(8,128)}, u32[]{:S(2)}) copy-start(s32[32,32]{1,0:T(8,128)} %slot_request_ref.1) | copy-start | bytes 12292
  2.4 16.0 %copy-start.5 = (s32[64]{0:T(128)S(1)}, s32[64]{0:T(128)}, u32[]{:S(2)}) copy-start(s32[64]{0:T(128)} %param.15) | copy-start | bytes 772
  2.4 31.4 %all-to-all-start = ((bf16[32,96,128]{2,1,0:T(8,128)(2,1)}), bf16[32,96,128]{2,1,0:T(8,128)(2,1)S(1)}, u32[]{:S(2)}, u32[]{:S(2)}) async-start(bf16[32,96,128]{2,1,0:T(8,128)(2,1)} %pack.1), calls=%async_computation | async-start | bytes 1572864 | tf_op jit(solution)/shard_map/all_to_all | solution.py:352
  14.6 36.3 %collective-permute-start = (bf16[224,2048]{1,0:T(8,128)(2,1)}, bf16[224,2048]{1,0:T(8,128)(2,1)}, u32[]{:S(2)}, u32[]{:S(2)}) collective-permute-start(bf16[224,2048]{1,0:T(8,128)(2,1)} %bitcast.45), channel_id=1, source_target_pairs={{0,192},{8,200},{16,208},{24,216},{32,224},{40,232},{48,240},{56,2... | collective-permute-start | bytes 2752520 | tf_op jit(solution)/shard_map/ppermute | solution.py:362
  42.3 40.9 %copy-start.1 = (bf16[2048,224]{0,1:T(8,128)(2,1)S(1)}, bf16[2048,224]{0,1:T(8,128)(2,1)}, u32[]{:S(2)}) copy-start(bf16[2048,224]{0,1:T(8,128)(2,1)} %param.13) | copy-start | bytes 2752516
  42.4 23.5 %all-to-all-start.1 = ((bf16[32,72,128]{2,1,0:T(8,128)(2,1)}), bf16[32,72,128]{2,1,0:T(8,128)(2,1)S(1)}, u32[]{:S(2)}, u32[]{:S(2)}) async-start(bf16[32,72,128]{2,1,0:T(8,128)(2,1)} %lend.1), calls=%async_computation.1 | async-start | bytes 1179648 | tf_op jit(solution)/shard_map/all_to_all | solution.py:382
  50.9 27.4 %collective-permute-start.1 = (bf16[224,2048]{1,0:T(8,128)(2,1)}, bf16[224,2048]{1,0:T(8,128)(2,1)}, u32[]{:S(2)}, u32[]{:S(2)}) collective-permute-start(bf16[224,2048]{1,0:T(8,128)(2,1)} %collective-permute-done.refs_1_), channel_id=1, source_target_pairs={{0,192},{8,200},{16,208},{24,216},{32,224},{40,232},{48,240},{56,2... | collective-permute-start | bytes 2752520 | tf_op jit(solution)/shard_map/ppermute | solution.py:383
  53.4 27.3 %collective-permute-start.2 = (bf16[224,2048]{1,0:T(8,128)(2,1)}, bf16[224,2048]{1,0:T(8,128)(2,1)S(1)}, u32[]{:S(2)}, u32[]{:S(2)}) collective-permute-start(bf16[224,2048]{1,0:T(8,128)(2,1)} %bitcast.46), channel_id=1, source_target_pairs={{0,64},{8,72},{16,80},{24,88},{32,96},{40,104},{48,112},{56,120},{... | collective-permute-start | bytes 2752520 | tf_op jit(solution)/shard_map/ppermute | solution.py:384
  68.2 15.0 %all-to-all-start.2 = ((bf16[8,8,2048]{2,1,0:T(8,128)(2,1)}), bf16[8,8,2048]{2,1,0:T(8,128)(2,1)S(1)}, u32[]{:S(2)}, u32[]{:S(2)}) async-start(bf16[8,8,2048]{2,1,0:T(8,128)(2,1)} %settle.1), calls=%async_computation.2 | async-start | bytes 524288 | tf_op jit(solution)/shard_map/all_to_all | solution.py:388
  86.2 5.1 %collective-permute-start.3 = (bf16[2,16,4,224]{3,2,1,0:T(4,128)(2,1)S(1)}, bf16[2,16,4,224]{3,2,1,0:T(4,128)(2,1)S(1)}, u32[]{:S(2)}, u32[]{:S(2)}) collective-permute-start(bf16[2,16,4,224]{3,2,1,0:T(4,128)(2,1)S(1)} %get-tuple-element.40), channel_id=1, source_target_pairs={{0,1},{1,0},{2,3},{3,2},{4,5},{5,4},{6,7},{7,6},{8,9},{9,8},{10,11... | collective-permute-start | bytes 172040 | tf_op jit(solution)/shard_map/ppermute | solution.py:405
  91.3 7.2 %collective-permute-start.4 = (bf16[16,4,224]{2,1,0:T(4,128)(2,1)S(1)}, bf16[16,4,224]{2,1,0:T(4,128)(2,1)S(1)}, u32[]{:S(2)}, u32[]{:S(2)}) collective-permute-start(bf16[16,4,224]{2,1,0:T(4,128)(2,1)S(1)} %get-tuple-element.41), channel_id=1, source_target_pairs={{0,0},{1,65},{2,64},{3,129},{4,128},{5,193},{6,192},{7,1},{8,8},{9... | collective-permute-start | bytes 86024 | tf_op jit(solution)/shard_map/ppermute | solution.py:413
  93.9 5.7 %collective-permute-start.5 = (bf16[16,4,224]{2,1,0:T(4,128)(2,1)S(1)}, bf16[16,4,224]{2,1,0:T(4,128)(2,1)S(1)}, u32[]{:S(2)}, u32[]{:S(2)}) collective-permute-start(bf16[16,4,224]{2,1,0:T(4,128)(2,1)S(1)} %get-tuple-element.42), channel_id=1, source_target_pairs={{0,128},{1,193},{2,192},{3,1},{4,0},{5,65},{6,64},{7,129},{8,136},... | collective-permute-start | bytes 86024 | tf_op jit(solution)/shard_map/ppermute | solution.py:413
  99.6 2.7 %collective-permute-start.6 = (f32[8,4,224]{2,1,0:T(4,128)S(1)}, f32[8,4,224]{2,1,0:T(4,128)S(1)}, u32[]{:S(2)}, u32[]{:S(2)}) collective-permute-start(f32[8,4,224]{2,1,0:T(4,128)S(1)} %slice_select_fusion), channel_id=1, source_target_pairs={{0,1},{1,0},{2,3},{3,2},{4,5},{5,4},{6,7},{7,6},{8,9},{9,8},{10,11... | collective-permute-start | bytes 86024 | tf_op jit(solution)/shard_map/ppermute | solution.py:418

commit v6 on v5

--- a/solution.py
+++ b/solution.py
@@ -13,6 +13,11 @@
 BF16 = jnp.bfloat16
 F32 = jnp.float32
 PARTS = 3
+TURN = (0, 2, 4, 6, 1, 3, 5, 7)
+
+
+def in_turn(n):
+    return n // len(TURN) * len(TURN) + TURN[n % len(TURN)]
 
 
 def live_tokens(slot_request, context_lengths, slot_tokens):
@@ -47,7 +52,9 @@
     home = home_ref[0]
     copies = [
         pltpu.make_async_copy(
-            packed_ref.at[jnp.clip(slot_request_ref[d, home] - home * reqs, 0, reqs - 1)],
+            packed_ref.at[
+                jnp.clip(slot_request_ref[in_turn(d), home] - home * reqs, 0, reqs - 1)
+            ],
             out_ref.at[d],
             sems.at[d],
         )
@@ -162,17 +169,20 @@
         ns = [t * group + k for k in range(group)]
         scores = [
             lax.dot_general(
-                query_ref[n], pool_ref[n], (((1,), (1,)), ((), ())), preferred_element_type=F32
+                query_ref[n],
+                pool_ref[in_turn(n)],
+                (((1,), (1,)), ((), ())),
+                preferred_element_type=F32,
             )
             * scale
             for n in ns
         ]
-        scores = [jnp.where(token < live_ref[n], x, NEG_FILL) for n, x in zip(ns, scores)]
+        scores = [jnp.where(token < live_ref[in_turn(n)], x, NEG_FILL) for n, x in zip(ns, scores)]
         tops = [jnp.max(x, axis=1, keepdims=True) for x in scores]
         weights = [jnp.exp(x - top) for x, top in zip(scores, tops)]
         totals = [jnp.sum(x, axis=1, keepdims=True) for x in weights]
         weighted = [
-            jnp.dot(x.astype(BF16), pool_ref[n, :, :latent], preferred_element_type=F32)
+            jnp.dot(x.astype(BF16), pool_ref[in_turn(n), :, :latent], preferred_element_type=F32)
             for n, x in zip(ns, weights)
         ]
         for n, top, total, x in zip(ns, tops, totals, weighted):
@@ -349,11 +359,17 @@
             (outgoing, slot_request, context_lengths, draft_queries, draft_latents, out_proj)
         )
     )
-    arrived = lax.all_to_all(outgoing, "lender", split_axis=0, concat_axis=0, tiled=True)
+    slots = latent_pool.shape[0]
+    turn = [in_turn(n) for n in range(slots)]
+    arrived = lax.all_to_all(
+        outgoing, "lender", split_axis=0, concat_axis=0, tiled=True, axis_index_groups=[turn]
+    )
 
     live_all = live_tokens(slot_request, context_lengths, tokens)
     live_here = lax.dynamic_slice_in_dim(live_all, home, 1, 0)[0]
-    local = lax.dynamic_slice_in_dim(slot_request, home, 1, 1).reshape(1, -1) - home * reqs
+    local = lax.dynamic_slice_in_dim(slot_request, home, 1, 1)[:, 0] - home * reqs
+    local = local.reshape(-1, len(TURN) // 2, 2)
+    local = jnp.concatenate([local[:, :, 0], local[:, :, 1]], axis=1).reshape(1, -1)
     lenders, column = latent_pool.shape[0], 8
     planes = lenders // column
     up = [(l, (l - column) % lenders) for l in range(lenders)]
@@ -379,7 +395,9 @@
 
     sending = lend(live_here, arrived, key_absorb, value_absorb, latent_pool, scale)
     sending, weight = lax.optimization_barrier((sending, weight))
-    back = lax.all_to_all(sending, "lender", split_axis=0, concat_axis=0, tiled=True)
+    back = lax.all_to_all(
+        sending, "lender", split_axis=0, concat_axis=0, tiled=True, axis_index_groups=[turn]
+    )
     weight_far = lax.ppermute(weight_up, "lender", up)
     weight_down = lax.ppermute(weight, "lender", down)
 

time: 103 us -> 103 us (level)
  starting transfers between devices: 44.6 us -> 43.3 us
    ppermute x1, waiting for transfers between devices: 4.4 us -> 2.55 us  [body(): weight_far = lax.ppermute(weight_up, 'lender', up)]
    all_to_all x1, waiting for transfers between devices: 2.5 us -> 4.15 us  [body(): lax.all_to_all(copies, 'lender', split_axis=0, concat_axis=0, tiled=True,...]
    all_to_all x2, starting transfers between devices: 20.7 us -> 19.1 us  [the longest x1 12 us: body(): lax.all_to_all(outgoing, 'lender', split_axis=0, concat_axis=0, tiled=Tru...]
    all_to_all x1, starting transfers between devices: 5.63 us -> 6.79 us  [body(): lax.all_to_all(copies, 'lender', split_axis=0, concat_axis=0, tiled=True,...]
  transfers between devices with their start and end apart: 10 -> 10, of which waited for: 8 -> 8; matrix products, arithmetic and copies ran while one was open for 4% -> 5% of each run, Pallas kernels for 10% -> 10%
where the time goes in v6:
time: 103 us
  starting transfers between devices  43.3 us (42%)
  waiting for transfers between devices  37.6 us (37%)
  Pallas kernels  16.1 us (16%)
  matrix products  2.71 us (3%)
  other arithmetic  2.11 us (2%)
    all_to_all x1, waiting for transfers between devices, body(): lax.all_to_all(sending, 'lender', split_axis=0, concat_axis=0, tiled=True...  12.7 us
    all_to_all x1, waiting for transfers between devices, body(): lax.all_to_all(outgoing, 'lender', split_axis=0, concat_axis=0, tiled=Tru...  12.6 us
    all_to_all x1, starting transfers between devices, body(): lax.all_to_all(outgoing, 'lender', split_axis=0, concat_axis=0, tiled=Tru...  12 us
    pallas_call x1, Pallas kernels, lend(): pl.pallas_call(functools.partial(lend_kernel, scale, group), out_shape=pl...  8.48 us
    all_to_all x1, starting transfers between devices, body(): lax.all_to_all(sending, 'lender', split_axis=0, concat_axis=0, tiled=True...  7.03 us
    ppermute x2, starting transfers between devices, body(): piece = lax.ppermute(own[j], ('lender', 'tensor'), pairs).astype(F32)  6.89 us
    all_to_all x1, starting transfers between devices, body(): lax.all_to_all(copies, 'lender', split_axis=0, concat_axis=0, tiled=True,...  6.79 us
    all_to_all x1, waiting for transfers between devices, body(): lax.all_to_all(copies, 'lender', split_axis=0, concat_axis=0, tiled=True,...  4.15 us
  transfers between devices with their start and end apart: 10, of which 8 were waited for; matrix products, arithmetic and copies ran while one was open for 5% of the time, Pallas kernels for 10%

profile of v6, /device:TPU:1, one launch (start us, length us, event | category | flops | bytes accessed | tf_op | source)
XLA Modules:
  0.0 102.6 jit_solution(11859954659602292553)
XLA Ops:
  0.0 0.0 copy-start.2
  0.0 2.4 %pack.1 = bf16[32,96,128]{2,1,0:T(8,128)(2,1)} custom-call(s32[1]{0:T(128)} %bitcast.4.home_ref, s32[32,32]{1,0:T(8,128)} %slot_request_ref.1, bf16[2,4,16,192]{3,2,1,0:T(8,128)(2,1)} %queries_ref.1), custom_call_target="tpu_custom_call" | custom-call | tf_op jit(solution)/shard_map/pack/pallas_call | solution.py:75
  2.4 0.0 copy-start.4
  2.4 0.0 copy-start.5
  2.4 12.0 %all-to-all-start = ((bf16[32,96,128]{2,1,0:T(8,128)(2,1)}), bf16[32,96,128]{2,1,0:T(8,128)(2,1)S(1)}, u32[]{:S(2)}, u32[]{:S(2)}) async-start(bf16[32,96,128]{2,1,0:T(8,128)(2,1)} %pack.1), calls=%async_computation | async-start | bytes 1572864 | tf_op jit(solution)/shard_map/all_to_all | solution.py:364
  14.5 2.6 %collective-permute-start = (bf16[224,2048]{1,0:T(8,128)(2,1)}, bf16[224,2048]{1,0:T(8,128)(2,1)}, u32[]{:S(2)}, u32[]{:S(2)}) collective-permute-start(bf16[224,2048]{1,0:T(8,128)(2,1)} %bitcast.44), channel_id=1, source_target_pairs={{0,192},{8,200},{16,208},{24,216},{32,224},{40,232},{48,240},{56,2... | collective-permute-start | bytes 2752520 | tf_op jit(solution)/shard_map/ppermute | solution.py:378
  17.0 0.0 copy-done.2
  17.0 0.2 subtract_reduce_fusion
  17.2 0.1 sub.49
  17.3 0.3 slice_reduce_fusion.1
  17.6 0.0 copy-done.3
  17.6 0.1 pad_add_fusion
  17.7 0.1 reshape.29.local_ref
  17.8 0.0 copy-done
  17.8 0.4 fusion.7
  18.2 0.1 pad_maximum_fusion
  18.3 0.0 copy-done.4
  18.3 0.3 fusion.10
  18.6 0.1 copy.16
  18.8 0.0 copy-done.5
  18.8 0.8 select_reduce_fusion.1
  19.6 0.2 select_reduce_fusion
  19.8 2.0 %fusion.2 = f32[2,4,16,128]{3,1,2,0:T(4,128)S(1)} fusion(bf16[16,512,128]{2,1,0:T(8,128)(2,1)} %values_any.1, bf16[2,4,576]{2,1,0:T(4,128)(2,1)S(1)} %copy-done.4), kind=kOutput, calls=%fused_computation.2 | convolution fusion | flops 16777216 | bytes 2170880 | tf_op jit(solution)/shard_map/ijl,hlc->ijhc/dot_general | solution.py:389
  21.8 12.6 %all-to-all-done.arrived_ref = bf16[32,96,128]{2,1,0:T(8,128)(2,1)S(1)} async-done(((bf16[32,96,128]{2,1,0:T(8,128)(2,1)}), bf16[32,96,128]{2,1,0:T(8,128)(2,1)S(1)}, u32[]{:S(2)}, u32[]{:S(2)}) %all-to-all-start) | async-done | bytes 786464 | tf_op jit(solution)/shard_map/all_to_all | solution.py:364
  34.4 8.5 %lend.1 = bf16[32,72,128]{2,1,0:T(8,128)(2,1)} custom-call(s32[32]{0:T(128)S(1)} %fusion.19.live_ref, bf16[32,96,128]{2,1,0:T(8,128)(2,1)S(1)} %all-to-all-done.arrived_ref, bf16[16,128,512]{2,1,0:T(8,128)(2,1)S(1)} %copy-done, bf16[16,512,128]{2,1,0:T(8,128)(2,1)} %values_any.1, bf16[32,192,576]{2,1,0:T(8,128)(2,1)} %pool_any.1), custom_call_target="tpu_custom_call" | custom-call | tf_op jit(solution)/shard_map/lend/pallas_call | solution.py:213
  42.9 0.0 copy-start.1
  42.9 7.0 %all-to-all-start.1 = ((bf16[32,72,128]{2,1,0:T(8,128)(2,1)}), bf16[32,72,128]{2,1,0:T(8,128)(2,1)S(1)}, u32[]{:S(2)}, u32[]{:S(2)}) async-start(bf16[32,72,128]{2,1,0:T(8,128)(2,1)} %lend.1), calls=%async_computation.1 | async-start | bytes 1179648 | tf_op jit(solution)/shard_map/all_to_all | solution.py:398
  49.9 0.0 collective-permute-done.refs_1_
  49.9 2.6 %collective-permute-start.1 = (bf16[224,2048]{1,0:T(8,128)(2,1)}, bf16[224,2048]{1,0:T(8,128)(2,1)}, u32[]{:S(2)}, u32[]{:S(2)}) collective-permute-start(bf16[224,2048]{1,0:T(8,128)(2,1)} %collective-permute-done.refs_1_), channel_id=1, source_target_pairs={{0,192},{8,200},{16,208},{24,216},{32,224},{40,232},{48,240},{56,2... | collective-permute-start | bytes 2752520 | tf_op jit(solution)/shard_map/ppermute | solution.py:401
  52.5 0.0 collective-permute-start.2
  52.5 12.7 %all-to-all-done.1.back_ref = bf16[32,72,128]{2,1,0:T(8,128)(2,1)S(1)} async-done(((bf16[32,72,128]{2,1,0:T(8,128)(2,1)}), bf16[32,72,128]{2,1,0:T(8,128)(2,1)S(1)}, u32[]{:S(2)}, u32[]{:S(2)}) %all-to-all-start.1) | async-done | bytes 589856 | tf_op jit(solution)/shard_map/all_to_all | solution.py:398
  65.2 2.3 %settle.1 = bf16[8,8,2048]{2,1,0:T(8,128)(2,1)} custom-call(bf16[32,72,128]{2,1,0:T(8,128)(2,1)S(1)} %all-to-all-done.1.back_ref, s32[1,32]{1,0:T(1,128)S(1)} %reshape.29.local_ref, f32[2,64,4]{2,1,0:T(8,128)S(1)} %bitcast.47, f32[2,4,16,128]{3,2,1,0:T(8,128)S(1)} %copy.17.draft_values_ref), custom_call_target="tpu_custom_call" | custom-call | tf_op jit(solution)/shard_map/settle/pallas_call | solution.py:276
  67.4 6.8 %all-to-all-start.2 = ((bf16[8,8,2048]{2,1,0:T(8,128)(2,1)}), bf16[8,8,2048]{2,1,0:T(8,128)(2,1)S(1)}, u32[]{:S(2)}, u32[]{:S(2)}) async-start(bf16[8,8,2048]{2,1,0:T(8,128)(2,1)} %settle.1), calls=%async_computation.2 | async-start | bytes 524288 | tf_op jit(solution)/shard_map/all_to_all | solution.py:406
  74.2 0.1 pad_add_fusion.1.place_ref
  74.3 2.5 %collective-permute-done.1.refs_2_ = bf16[224,2048]{1,0:T(8,128)(2,1)} collective-permute-done((bf16[224,2048]{1,0:T(8,128)(2,1)}, bf16[224,2048]{1,0:T(8,128)(2,1)}, u32[]{:S(2)}, u32[]{:S(2)}) %collective-permute-start.1) | collective-permute-done | bytes 917536 | tf_op jit(solution)/shard_map/ppermute | solution.py:401
  76.8 2.9 %collective-permute-done.2.refs_3_ = bf16[224,2048]{1,0:T(8,128)(2,1)S(1)} collective-permute-done((bf16[224,2048]{1,0:T(8,128)(2,1)}, bf16[224,2048]{1,0:T(8,128)(2,1)S(1)}, u32[]{:S(2)}, u32[]{:S(2)}) %collective-permute-start.2) | collective-permute-done | bytes 917536 | tf_op jit(solution)/shard_map/ppermute | solution.py:402
  79.7 4.1 %all-to-all-done.2 = bf16[8,8,2048]{2,1,0:T(8,128)(2,1)S(1)} async-done(((bf16[8,8,2048]{2,1,0:T(8,128)(2,1)}), bf16[8,8,2048]{2,1,0:T(8,128)(2,1)S(1)}, u32[]{:S(2)}, u32[]{:S(2)}) %all-to-all-start.2) | async-done | bytes 262176 | tf_op jit(solution)/shard_map/all_to_all | solution.py:406
  83.9 0.0 copy-done.1
  83.9 3.0 %mix.1 = (bf16[2,16,4,224]{3,2,1,0:T(4,128)(2,1)S(1)}, bf16[2,16,4,224]{3,2,1,0:T(4,128)(2,1)S(1)}) custom-call(s32[4]{0:T(128)S(1)} %pad_add_fusion.1.place_ref, bf16[64,2048]{1,0:T(8,128)(2,1)S(1)} %bitcast.43, bf16[224,2048]{1,0:T(8,128)(2,1)S(1)} %bitcast.46, bf16[224,2048]{1,0:T(8,128)(2,1)} %collective-permute-done.refs_1_, ...), custom_call_target="tpu_custom_call" | custom-call | tf_op jit(solution)/shard_map/mix/pallas_call | solution.py:320
  86.8 3.3 %collective-permute-start.3 = (bf16[2,16,4,224]{3,2,1,0:T(4,128)(2,1)S(1)}, bf16[2,16,4,224]{3,2,1,0:T(4,128)(2,1)S(1)}, u32[]{:S(2)}, u32[]{:S(2)}) collective-permute-start(bf16[2,16,4,224]{3,2,1,0:T(4,128)(2,1)S(1)} %get-tuple-element.40), channel_id=1, source_target_pairs={{0,1},{1,0},{2,3},{3,2},{4,5},{5,4},{6,7},{7,6},{8,9},{9,8},{10,11... | collective-permute-start | bytes 172040 | tf_op jit(solution)/shard_map/ppermute | solution.py:423
  90.1 0.9 collective-permute-done.3
  91.1 2.2 %collective-permute-start.4 = (bf16[16,4,224]{2,1,0:T(4,128)(2,1)S(1)}, bf16[16,4,224]{2,1,0:T(4,128)(2,1)S(1)}, u32[]{:S(2)}, u32[]{:S(2)}) collective-permute-start(bf16[16,4,224]{2,1,0:T(4,128)(2,1)S(1)} %get-tuple-element.43), channel_id=1, source_target_pairs={{0,0},{1,65},{2,64},{3,129},{4,128},{5,193},{6,192},{7,1},{8,8},{9... | collective-permute-start | bytes 86024 | tf_op jit(solution)/shard_map/ppermute | solution.py:431
  93.3 4.7 %collective-permute-start.5 = (bf16[16,4,224]{2,1,0:T(4,128)(2,1)S(1)}, bf16[16,4,224]{2,1,0:T(4,128)(2,1)S(1)}, u32[]{:S(2)}, u32[]{:S(2)}) collective-permute-start(bf16[16,4,224]{2,1,0:T(4,128)(2,1)S(1)} %get-tuple-element.44), channel_id=1, source_target_pairs={{0,128},{1,193},{2,192},{3,1},{4,0},{5,65},{6,64},{7,129},{8,136},... | collective-permute-start | bytes 86024 | tf_op jit(solution)/shard_map/ppermute | solution.py:431
  98.0 0.0 collective-permute-done.4
  98.0 1.0 collective-permute-done.5
  99.1 2.1 %collective-permute-start.6 = (f32[8,4,224]{2,1,0:T(4,128)S(1)}, f32[8,4,224]{2,1,0:T(4,128)S(1)}, u32[]{:S(2)}, u32[]{:S(2)}) collective-permute-start(f32[8,4,224]{2,1,0:T(4,128)S(1)} %slice_select_fusion), channel_id=1, source_target_pairs={{0,1},{1,0},{2,3},{3,2},{4,5},{5,4},{6,7},{7,6},{8,9},{9,8},{10,11... | collective-permute-start | bytes 86024 | tf_op jit(solution)/shard_map/ppermute | solution.py:436
  101.2 0.9 collective-permute-done.6
  102.0 0.6 add_convert_fusion.1
  (12 shorter events, 0.2 us)
Async XLA Ops:
  0.0 17.0 %copy-start.2 = (s32[32,32]{1,0:T(8,128)S(1)}, s32[32,32]{1,0:T(8,128)}, u32[]{:S(2)}) copy-start(s32[32,32]{1,0:T(8,128)} %slot_request_ref.1) | copy-start | bytes 12292
  0.0 17.6 %copy-start.3 = (bf16[2,4,16,192]{3,2,1,0:T(8,128)(2,1)S(1)}, bf16[2,4,16,192]{3,2,1,0:T(8,128)(2,1)}, u32[]{:S(2)}) copy-start(bf16[2,4,16,192]{3,2,1,0:T(8,128)(2,1)} %queries_ref.1) | copy-start | bytes 147460
  0.0 17.8 %copy-start = (bf16[16,128,512]{2,1,0:T(8,128)(2,1)S(1)}, bf16[16,128,512]{2,1,0:T(8,128)(2,1)}, u32[]{:S(2)}) copy-start(bf16[16,128,512]{2,1,0:T(8,128)(2,1)} %keys_ref.1) | copy-start | bytes 6291460
  2.4 15.9 %copy-start.4 = (bf16[2,4,576]{2,1,0:T(4,128)(2,1)S(1)}, bf16[2,4,576]{2,1,0:T(4,128)(2,1)}, u32[]{:S(2)}) copy-start(bf16[2,4,576]{2,1,0:T(4,128)(2,1)} %param.9) | copy-start | bytes 27652
  2.4 16.4 %copy-start.5 = (s32[64]{0:T(128)S(1)}, s32[64]{0:T(128)}, u32[]{:S(2)}) copy-start(s32[64]{0:T(128)} %param.15) | copy-start | bytes 772
  2.4 32.0 %all-to-all-start = ((bf16[32,96,128]{2,1,0:T(8,128)(2,1)}), bf16[32,96,128]{2,1,0:T(8,128)(2,1)S(1)}, u32[]{:S(2)}, u32[]{:S(2)}) async-start(bf16[32,96,128]{2,1,0:T(8,128)(2,1)} %pack.1), calls=%async_computation | async-start | bytes 1572864 | tf_op jit(solution)/shard_map/all_to_all | solution.py:364
  14.5 35.5 %collective-permute-start = (bf16[224,2048]{1,0:T(8,128)(2,1)}, bf16[224,2048]{1,0:T(8,128)(2,1)}, u32[]{:S(2)}, u32[]{:S(2)}) collective-permute-start(bf16[224,2048]{1,0:T(8,128)(2,1)} %bitcast.44), channel_id=1, source_target_pairs={{0,192},{8,200},{16,208},{24,216},{32,224},{40,232},{48,240},{56,2... | collective-permute-start | bytes 2752520 | tf_op jit(solution)/shard_map/ppermute | solution.py:378
  42.9 41.0 %copy-start.1 = (bf16[2048,224]{0,1:T(8,128)(2,1)S(1)}, bf16[2048,224]{0,1:T(8,128)(2,1)}, u32[]{:S(2)}) copy-start(bf16[2048,224]{0,1:T(8,128)(2,1)} %param.13) | copy-start | bytes 2752516
  42.9 22.3 %all-to-all-start.1 = ((bf16[32,72,128]{2,1,0:T(8,128)(2,1)}), bf16[32,72,128]{2,1,0:T(8,128)(2,1)S(1)}, u32[]{:S(2)}, u32[]{:S(2)}) async-start(bf16[32,72,128]{2,1,0:T(8,128)(2,1)} %lend.1), calls=%async_computation.1 | async-start | bytes 1179648 | tf_op jit(solution)/shard_map/all_to_all | solution.py:398
  49.9 26.9 %collective-permute-start.1 = (bf16[224,2048]{1,0:T(8,128)(2,1)}, bf16[224,2048]{1,0:T(8,128)(2,1)}, u32[]{:S(2)}, u32[]{:S(2)}) collective-permute-start(bf16[224,2048]{1,0:T(8,128)(2,1)} %collective-permute-done.refs_1_), channel_id=1, source_target_pairs={{0,192},{8,200},{16,208},{24,216},{32,224},{40,232},{48,240},{56,2... | collective-permute-start | bytes 2752520 | tf_op jit(solution)/shard_map/ppermute | solution.py:401
  52.5 27.2 %collective-permute-start.2 = (bf16[224,2048]{1,0:T(8,128)(2,1)}, bf16[224,2048]{1,0:T(8,128)(2,1)S(1)}, u32[]{:S(2)}, u32[]{:S(2)}) collective-permute-start(bf16[224,2048]{1,0:T(8,128)(2,1)} %bitcast.45), channel_id=1, source_target_pairs={{0,64},{8,72},{16,80},{24,88},{32,96},{40,104},{48,112},{56,120},{... | collective-permute-start | bytes 2752520 | tf_op jit(solution)/shard_map/ppermute | solution.py:402
  67.4 16.4 %all-to-all-start.2 = ((bf16[8,8,2048]{2,1,0:T(8,128)(2,1)}), bf16[8,8,2048]{2,1,0:T(8,128)(2,1)S(1)}, u32[]{:S(2)}, u32[]{:S(2)}) async-start(bf16[8,8,2048]{2,1,0:T(8,128)(2,1)} %settle.1), calls=%async_computation.2 | async-start | bytes 524288 | tf_op jit(solution)/shard_map/all_to_all | solution.py:406
  86.8 4.2 %collective-permute-start.3 = (bf16[2,16,4,224]{3,2,1,0:T(4,128)(2,1)S(1)}, bf16[2,16,4,224]{3,2,1,0:T(4,128)(2,1)S(1)}, u32[]{:S(2)}, u32[]{:S(2)}) collective-permute-start(bf16[2,16,4,224]{3,2,1,0:T(4,128)(2,1)S(1)} %get-tuple-element.40), channel_id=1, source_target_pairs={{0,1},{1,0},{2,3},{3,2},{4,5},{5,4},{6,7},{7,6},{8,9},{9,8},{10,11... | collective-permute-start | bytes 172040 | tf_op jit(solution)/shard_map/ppermute | solution.py:423
  91.1 6.9 %collective-permute-start.4 = (bf16[16,4,224]{2,1,0:T(4,128)(2,1)S(1)}, bf16[16,4,224]{2,1,0:T(4,128)(2,1)S(1)}, u32[]{:S(2)}, u32[]{:S(2)}) collective-permute-start(bf16[16,4,224]{2,1,0:T(4,128)(2,1)S(1)} %get-tuple-element.43), channel_id=1, source_target_pairs={{0,0},{1,65},{2,64},{3,129},{4,128},{5,193},{6,192},{7,1},{8,8},{9... | collective-permute-start | bytes 86024 | tf_op jit(solution)/shard_map/ppermute | solution.py:431
  93.3 5.7 %collective-permute-start.5 = (bf16[16,4,224]{2,1,0:T(4,128)(2,1)S(1)}, bf16[16,4,224]{2,1,0:T(4,128)(2,1)S(1)}, u32[]{:S(2)}, u32[]{:S(2)}) collective-permute-start(bf16[16,4,224]{2,1,0:T(4,128)(2,1)S(1)} %get-tuple-element.44), channel_id=1, source_target_pairs={{0,128},{1,193},{2,192},{3,1},{4,0},{5,65},{6,64},{7,129},{8,136},... | collective-permute-start | bytes 86024 | tf_op jit(solution)/shard_map/ppermute | solution.py:431
  99.1 3.0 %collective-permute-start.6 = (f32[8,4,224]{2,1,0:T(4,128)S(1)}, f32[8,4,224]{2,1,0:T(4,128)S(1)}, u32[]{:S(2)}, u32[]{:S(2)}) collective-permute-start(f32[8,4,224]{2,1,0:T(4,128)S(1)} %slice_select_fusion), channel_id=1, source_target_pairs={{0,1},{1,0},{2,3},{3,2},{4,5},{5,4},{6,7},{7,6},{8,9},{9,8},{10,11... | collective-permute-start | bytes 86024 | tf_op jit(solution)/shard_map/ppermute | solution.py:436

commit v7 on v6

--- a/solution.py
+++ b/solution.py
@@ -309,6 +309,9 @@
     for n in range(blocks):
         out_ref = (own_ref, other_ref)[n * 2 // blocks]
         piece = held_ref[place_ref[n]]
+        size = piece.shape[0] // len(TURN)
+        places = [TURN.index(z) * size for z in range(len(TURN))]
+        piece = jnp.concatenate([piece[at : at + size] for at in places])
         out_ref[n % (blocks // 2)] = piece.reshape(out_ref.shape[1:]).astype(BF16)
 
 
@@ -402,7 +405,7 @@
     weight_down = lax.ppermute(weight, "lender", down)
 
     copies = settle(back, local, draft_scores, draft_values, column)
-    inner = [[column * y + z for z in range(column)] for y in range(planes)]
+    inner = [[in_turn(column * y + z) for z in range(column)] for y in range(planes)]
     plane = lax.all_to_all(
         copies, "lender", split_axis=0, concat_axis=0, tiled=True, axis_index_groups=inner
     )

time: 103 us -> 102 us (level)
  waiting for transfers between devices: 37.6 us -> 35.7 us
    all_to_all x1, waiting for transfers between devices: 4.15 us -> 2.29 us  [body(): lax.all_to_all(copies, 'lender', split_axis=0, concat_axis=0, tiled=True,...]
  transfers between devices with their start and end apart: 10 -> 10, of which waited for: 8 -> 8; matrix products, arithmetic and copies ran while one was open for 5% -> 5% of each run, Pallas kernels for 10% -> 11%
where the time goes in v7:
time: 102 us; the launch traced here: 101 us
  starting transfers between devices  43.7 us (43%)
  waiting for transfers between devices  35.7 us (35%)
  Pallas kernels  16.1 us (16%)
  matrix products  2.71 us (3%)
  other arithmetic  2.11 us (2%)
    all_to_all x1, waiting for transfers between devices, body(): lax.all_to_all(sending, 'lender', split_axis=0, concat_axis=0, tiled=True...  12.7 us
    all_to_all x1, waiting for transfers between devices, body(): lax.all_to_all(outgoing, 'lender', split_axis=0, concat_axis=0, tiled=Tru...  12.6 us
    all_to_all x1, starting transfers between devices, body(): lax.all_to_all(outgoing, 'lender', split_axis=0, concat_axis=0, tiled=Tru...  12 us
    pallas_call x1, Pallas kernels, lend(): pl.pallas_call(functools.partial(lend_kernel, scale, group), out_shape=pl...  8.48 us
    all_to_all x1, starting transfers between devices, body(): lax.all_to_all(sending, 'lender', split_axis=0, concat_axis=0, tiled=True...  7.03 us
    all_to_all x1, starting transfers between devices, body(): lax.all_to_all(copies, 'lender', split_axis=0, concat_axis=0, tiled=True,...  6.79 us
    ppermute x2, starting transfers between devices, body(): piece = lax.ppermute(own[j], ('lender', 'tensor'), pairs).astype(F32)  6.76 us
    ppermute x1, starting transfers between devices, body(): lax.ppermute(other, 'tensor', swap).astype(F32)  3.48 us
  transfers between devices with their start and end apart: 10, of which 8 were waited for; matrix products, arithmetic and copies ran while one was open for 5% of the time, Pallas kernels for 11%

profile of v7, /device:TPU:1, one launch (start us, length us, event | category | flops | bytes accessed | tf_op | source)
XLA Modules:
  0.0 101.2 jit_solution(17436106617636054657)
XLA Ops:
  0.0 0.0 copy-start.2
  0.0 2.4 %pack.1 = bf16[32,96,128]{2,1,0:T(8,128)(2,1)} custom-call(s32[1]{0:T(128)} %bitcast.4.home_ref, s32[32,32]{1,0:T(8,128)} %slot_request_ref.1, bf16[2,4,16,192]{3,2,1,0:T(8,128)(2,1)} %queries_ref.1), custom_call_target="tpu_custom_call" | custom-call | tf_op jit(solution)/shard_map/pack/pallas_call | solution.py:75
  2.4 0.0 copy-start.4
  2.4 0.0 copy-start.5
  2.4 12.0 %all-to-all-start = ((bf16[32,96,128]{2,1,0:T(8,128)(2,1)}), bf16[32,96,128]{2,1,0:T(8,128)(2,1)S(1)}, u32[]{:S(2)}, u32[]{:S(2)}) async-start(bf16[32,96,128]{2,1,0:T(8,128)(2,1)} %pack.1), calls=%async_computation | async-start | bytes 1572864 | tf_op jit(solution)/shard_map/all_to_all | solution.py:367
  14.5 2.6 %collective-permute-start = (bf16[224,2048]{1,0:T(8,128)(2,1)}, bf16[224,2048]{1,0:T(8,128)(2,1)}, u32[]{:S(2)}, u32[]{:S(2)}) collective-permute-start(bf16[224,2048]{1,0:T(8,128)(2,1)} %bitcast.44), channel_id=1, source_target_pairs={{0,192},{8,200},{16,208},{24,216},{32,224},{40,232},{48,240},{56,2... | collective-permute-start | bytes 2752520 | tf_op jit(solution)/shard_map/ppermute | solution.py:381
  17.0 0.0 copy-done.2
  17.0 0.2 subtract_reduce_fusion
  17.2 0.1 sub.49
  17.3 0.3 slice_reduce_fusion.1
  17.6 0.0 copy-done.3
  17.6 0.1 pad_add_fusion
  17.7 0.1 reshape.29.local_ref
  17.8 0.0 copy-done
  17.8 0.4 fusion.7
  18.2 0.1 pad_maximum_fusion
  18.3 0.0 copy-done.4
  18.3 0.3 fusion.10
  18.6 0.1 copy.16
  18.8 0.0 copy-done.5
  18.8 0.8 select_reduce_fusion.1
  19.6 0.2 select_reduce_fusion
  19.8 2.0 %fusion.2 = f32[2,4,16,128]{3,1,2,0:T(4,128)S(1)} fusion(bf16[16,512,128]{2,1,0:T(8,128)(2,1)} %values_any.1, bf16[2,4,576]{2,1,0:T(4,128)(2,1)S(1)} %copy-done.4), kind=kOutput, calls=%fused_computation.2 | convolution fusion | flops 16777216 | bytes 2170880 | tf_op jit(solution)/shard_map/ijl,hlc->ijhc/dot_general | solution.py:392
  21.8 12.6 %all-to-all-done.arrived_ref = bf16[32,96,128]{2,1,0:T(8,128)(2,1)S(1)} async-done(((bf16[32,96,128]{2,1,0:T(8,128)(2,1)}), bf16[32,96,128]{2,1,0:T(8,128)(2,1)S(1)}, u32[]{:S(2)}, u32[]{:S(2)}) %all-to-all-start) | async-done | bytes 786464 | tf_op jit(solution)/shard_map/all_to_all | solution.py:367
  34.4 8.5 %lend.1 = bf16[32,72,128]{2,1,0:T(8,128)(2,1)} custom-call(s32[32]{0:T(128)S(1)} %fusion.19.live_ref, bf16[32,96,128]{2,1,0:T(8,128)(2,1)S(1)} %all-to-all-done.arrived_ref, bf16[16,128,512]{2,1,0:T(8,128)(2,1)S(1)} %copy-done, bf16[16,512,128]{2,1,0:T(8,128)(2,1)} %values_any.1, bf16[32,192,576]{2,1,0:T(8,128)(2,1)} %pool_any.1), custom_call_target="tpu_custom_call" | custom-call | tf_op jit(solution)/shard_map/lend/pallas_call | solution.py:213
  42.9 0.0 copy-start.1
  42.9 7.0 %all-to-all-start.1 = ((bf16[32,72,128]{2,1,0:T(8,128)(2,1)}), bf16[32,72,128]{2,1,0:T(8,128)(2,1)S(1)}, u32[]{:S(2)}, u32[]{:S(2)}) async-start(bf16[32,72,128]{2,1,0:T(8,128)(2,1)} %lend.1), calls=%async_computation.1 | async-start | bytes 1179648 | tf_op jit(solution)/shard_map/all_to_all | solution.py:401
  49.9 0.0 collective-permute-done.refs_1_
  49.9 2.6 %collective-permute-start.1 = (bf16[224,2048]{1,0:T(8,128)(2,1)}, bf16[224,2048]{1,0:T(8,128)(2,1)}, u32[]{:S(2)}, u32[]{:S(2)}) collective-permute-start(bf16[224,2048]{1,0:T(8,128)(2,1)} %collective-permute-done.refs_1_), channel_id=1, source_target_pairs={{0,192},{8,200},{16,208},{24,216},{32,224},{40,232},{48,240},{56,2... | collective-permute-start | bytes 2752520 | tf_op jit(solution)/shard_map/ppermute | solution.py:404
  52.5 0.0 collective-permute-start.2
  52.5 12.7 %all-to-all-done.1.back_ref = bf16[32,72,128]{2,1,0:T(8,128)(2,1)S(1)} async-done(((bf16[32,72,128]{2,1,0:T(8,128)(2,1)}), bf16[32,72,128]{2,1,0:T(8,128)(2,1)S(1)}, u32[]{:S(2)}, u32[]{:S(2)}) %all-to-all-start.1) | async-done | bytes 589856 | tf_op jit(solution)/shard_map/all_to_all | solution.py:401
  65.2 2.3 %settle.1 = bf16[8,8,2048]{2,1,0:T(8,128)(2,1)} custom-call(bf16[32,72,128]{2,1,0:T(8,128)(2,1)S(1)} %all-to-all-done.1.back_ref, s32[1,32]{1,0:T(1,128)S(1)} %reshape.29.local_ref, f32[2,64,4]{2,1,0:T(8,128)S(1)} %bitcast.47, f32[2,4,16,128]{3,2,1,0:T(8,128)S(1)} %copy.17.draft_values_ref), custom_call_target="tpu_custom_call" | custom-call | tf_op jit(solution)/shard_map/settle/pallas_call | solution.py:276
  67.4 6.8 %all-to-all-start.2 = ((bf16[8,8,2048]{2,1,0:T(8,128)(2,1)}), bf16[8,8,2048]{2,1,0:T(8,128)(2,1)S(1)}, u32[]{:S(2)}, u32[]{:S(2)}) async-start(bf16[8,8,2048]{2,1,0:T(8,128)(2,1)} %settle.1), calls=%async_computation.2 | async-start | bytes 524288 | tf_op jit(solution)/shard_map/all_to_all | solution.py:409
  74.2 0.1 pad_add_fusion.1.place_ref
  74.3 2.5 %collective-permute-done.1.refs_2_ = bf16[224,2048]{1,0:T(8,128)(2,1)} collective-permute-done((bf16[224,2048]{1,0:T(8,128)(2,1)}, bf16[224,2048]{1,0:T(8,128)(2,1)}, u32[]{:S(2)}, u32[]{:S(2)}) %collective-permute-start.1) | collective-permute-done | bytes 917536 | tf_op jit(solution)/shard_map/ppermute | solution.py:404
  76.8 2.9 %collective-permute-done.2.refs_3_ = bf16[224,2048]{1,0:T(8,128)(2,1)S(1)} collective-permute-done((bf16[224,2048]{1,0:T(8,128)(2,1)}, bf16[224,2048]{1,0:T(8,128)(2,1)S(1)}, u32[]{:S(2)}, u32[]{:S(2)}) %collective-permute-start.2) | collective-permute-done | bytes 917536 | tf_op jit(solution)/shard_map/ppermute | solution.py:405
  79.7 2.3 %all-to-all-done.2 = bf16[8,8,2048]{2,1,0:T(8,128)(2,1)S(1)} async-done(((bf16[8,8,2048]{2,1,0:T(8,128)(2,1)}), bf16[8,8,2048]{2,1,0:T(8,128)(2,1)S(1)}, u32[]{:S(2)}, u32[]{:S(2)}) %all-to-all-start.2) | async-done | bytes 262176 | tf_op jit(solution)/shard_map/all_to_all | solution.py:409
  82.0 0.0 copy-done.1
  82.0 3.0 %mix.1 = (bf16[2,16,4,224]{3,2,1,0:T(4,128)(2,1)S(1)}, bf16[2,16,4,224]{3,2,1,0:T(4,128)(2,1)S(1)}) custom-call(s32[4]{0:T(128)S(1)} %pad_add_fusion.1.place_ref, bf16[64,2048]{1,0:T(8,128)(2,1)S(1)} %bitcast.43, bf16[224,2048]{1,0:T(8,128)(2,1)S(1)} %bitcast.46, bf16[224,2048]{1,0:T(8,128)(2,1)} %collective-permute-done.refs_1_, ...), custom_call_target="tpu_custom_call" | custom-call | tf_op jit(solution)/shard_map/mix/pallas_call | solution.py:323
  85.0 3.5 %collective-permute-start.3 = (bf16[2,16,4,224]{3,2,1,0:T(4,128)(2,1)S(1)}, bf16[2,16,4,224]{3,2,1,0:T(4,128)(2,1)S(1)}, u32[]{:S(2)}, u32[]{:S(2)}) collective-permute-start(bf16[2,16,4,224]{3,2,1,0:T(4,128)(2,1)S(1)} %get-tuple-element.40), channel_id=1, source_target_pairs={{0,1},{1,0},{2,3},{3,2},{4,5},{5,4},{6,7},{7,6},{8,9},{9,8},{10,11... | collective-permute-start | bytes 172040 | tf_op jit(solution)/shard_map/ppermute | solution.py:426
  88.5 0.9 collective-permute-done.3
  89.5 2.1 %collective-permute-start.4 = (bf16[16,4,224]{2,1,0:T(4,128)(2,1)S(1)}, bf16[16,4,224]{2,1,0:T(4,128)(2,1)S(1)}, u32[]{:S(2)}, u32[]{:S(2)}) collective-permute-start(bf16[16,4,224]{2,1,0:T(4,128)(2,1)S(1)} %get-tuple-element.43), channel_id=1, source_target_pairs={{0,0},{1,65},{2,64},{3,129},{4,128},{5,193},{6,192},{7,1},{8,8},{9... | collective-permute-start | bytes 86024 | tf_op jit(solution)/shard_map/ppermute | solution.py:434
  91.6 4.7 %collective-permute-start.5 = (bf16[16,4,224]{2,1,0:T(4,128)(2,1)S(1)}, bf16[16,4,224]{2,1,0:T(4,128)(2,1)S(1)}, u32[]{:S(2)}, u32[]{:S(2)}) collective-permute-start(bf16[16,4,224]{2,1,0:T(4,128)(2,1)S(1)} %get-tuple-element.44), channel_id=1, source_target_pairs={{0,128},{1,193},{2,192},{3,1},{4,0},{5,65},{6,64},{7,129},{8,136},... | collective-permute-start | bytes 86024 | tf_op jit(solution)/shard_map/ppermute | solution.py:434
  96.2 0.0 collective-permute-done.4
  96.2 1.0 %collective-permute-done.5 = bf16[16,4,224]{2,1,0:T(4,128)(2,1)S(1)} collective-permute-done((bf16[16,4,224]{2,1,0:T(4,128)(2,1)S(1)}, bf16[16,4,224]{2,1,0:T(4,128)(2,1)S(1)}, u32[]{:S(2)}, u32[]{:S(2)}) %collective-permute-start.5) | collective-permute-done | bytes 28704 | tf_op jit(solution)/shard_map/ppermute | solution.py:434
  97.3 2.4 %collective-permute-start.6 = (f32[8,4,224]{2,1,0:T(4,128)S(1)}, f32[8,4,224]{2,1,0:T(4,128)S(1)}, u32[]{:S(2)}, u32[]{:S(2)}) collective-permute-start(f32[8,4,224]{2,1,0:T(4,128)S(1)} %slice_select_fusion), channel_id=1, source_target_pairs={{0,1},{1,0},{2,3},{3,2},{4,5},{5,4},{6,7},{7,6},{8,9},{9,8},{10,11... | collective-permute-start | bytes 86024 | tf_op jit(solution)/shard_map/ppermute | solution.py:439
  99.7 0.9 collective-permute-done.6
  100.6 0.6 add_convert_fusion.1
  (12 shorter events, 0.2 us)
Async XLA Ops:
  0.0 17.0 %copy-start.2 = (s32[32,32]{1,0:T(8,128)S(1)}, s32[32,32]{1,0:T(8,128)}, u32[]{:S(2)}) copy-start(s32[32,32]{1,0:T(8,128)} %slot_request_ref.1) | copy-start | bytes 12292
  0.0 17.6 %copy-start.3 = (bf16[2,4,16,192]{3,2,1,0:T(8,128)(2,1)S(1)}, bf16[2,4,16,192]{3,2,1,0:T(8,128)(2,1)}, u32[]{:S(2)}) copy-start(bf16[2,4,16,192]{3,2,1,0:T(8,128)(2,1)} %queries_ref.1) | copy-start | bytes 147460
  0.0 17.8 %copy-start = (bf16[16,128,512]{2,1,0:T(8,128)(2,1)S(1)}, bf16[16,128,512]{2,1,0:T(8,128)(2,1)}, u32[]{:S(2)}) copy-start(bf16[16,128,512]{2,1,0:T(8,128)(2,1)} %keys_ref.1) | copy-start | bytes 6291460
  2.4 15.9 %copy-start.4 = (bf16[2,4,576]{2,1,0:T(4,128)(2,1)S(1)}, bf16[2,4,576]{2,1,0:T(4,128)(2,1)}, u32[]{:S(2)}) copy-start(bf16[2,4,576]{2,1,0:T(4,128)(2,1)} %param.9) | copy-start | bytes 27652
  2.4 16.4 %copy-start.5 = (s32[64]{0:T(128)S(1)}, s32[64]{0:T(128)}, u32[]{:S(2)}) copy-start(s32[64]{0:T(128)} %param.15) | copy-start | bytes 772
  2.4 32.0 %all-to-all-start = ((bf16[32,96,128]{2,1,0:T(8,128)(2,1)}), bf16[32,96,128]{2,1,0:T(8,128)(2,1)S(1)}, u32[]{:S(2)}, u32[]{:S(2)}) async-start(bf16[32,96,128]{2,1,0:T(8,128)(2,1)} %pack.1), calls=%async_computation | async-start | bytes 1572864 | tf_op jit(solution)/shard_map/all_to_all | solution.py:367
  14.5 35.5 %collective-permute-start = (bf16[224,2048]{1,0:T(8,128)(2,1)}, bf16[224,2048]{1,0:T(8,128)(2,1)}, u32[]{:S(2)}, u32[]{:S(2)}) collective-permute-start(bf16[224,2048]{1,0:T(8,128)(2,1)} %bitcast.44), channel_id=1, source_target_pairs={{0,192},{8,200},{16,208},{24,216},{32,224},{40,232},{48,240},{56,2... | collective-permute-start | bytes 2752520 | tf_op jit(solution)/shard_map/ppermute | solution.py:381
  42.9 39.1 %copy-start.1 = (bf16[2048,224]{0,1:T(8,128)(2,1)S(1)}, bf16[2048,224]{0,1:T(8,128)(2,1)}, u32[]{:S(2)}) copy-start(bf16[2048,224]{0,1:T(8,128)(2,1)} %param.13) | copy-start | bytes 2752516
  42.9 22.3 %all-to-all-start.1 = ((bf16[32,72,128]{2,1,0:T(8,128)(2,1)}), bf16[32,72,128]{2,1,0:T(8,128)(2,1)S(1)}, u32[]{:S(2)}, u32[]{:S(2)}) async-start(bf16[32,72,128]{2,1,0:T(8,128)(2,1)} %lend.1), calls=%async_computation.1 | async-start | bytes 1179648 | tf_op jit(solution)/shard_map/all_to_all | solution.py:401
  49.9 26.9 %collective-permute-start.1 = (bf16[224,2048]{1,0:T(8,128)(2,1)}, bf16[224,2048]{1,0:T(8,128)(2,1)}, u32[]{:S(2)}, u32[]{:S(2)}) collective-permute-start(bf16[224,2048]{1,0:T(8,128)(2,1)} %collective-permute-done.refs_1_), channel_id=1, source_target_pairs={{0,192},{8,200},{16,208},{24,216},{32,224},{40,232},{48,240},{56,2... | collective-permute-start | bytes 2752520 | tf_op jit(solution)/shard_map/ppermute | solution.py:404
  52.5 27.2 %collective-permute-start.2 = (bf16[224,2048]{1,0:T(8,128)(2,1)}, bf16[224,2048]{1,0:T(8,128)(2,1)S(1)}, u32[]{:S(2)}, u32[]{:S(2)}) collective-permute-start(bf16[224,2048]{1,0:T(8,128)(2,1)} %bitcast.45), channel_id=1, source_target_pairs={{0,64},{8,72},{16,80},{24,88},{32,96},{40,104},{48,112},{56,120},{... | collective-permute-start | bytes 2752520 | tf_op jit(solution)/shard_map/ppermute | solution.py:405
  67.4 14.6 %all-to-all-start.2 = ((bf16[8,8,2048]{2,1,0:T(8,128)(2,1)}), bf16[8,8,2048]{2,1,0:T(8,128)(2,1)S(1)}, u32[]{:S(2)}, u32[]{:S(2)}) async-start(bf16[8,8,2048]{2,1,0:T(8,128)(2,1)} %settle.1), calls=%async_computation.2 | async-start | bytes 524288 | tf_op jit(solution)/shard_map/all_to_all | solution.py:409
  85.0 4.4 %collective-permute-start.3 = (bf16[2,16,4,224]{3,2,1,0:T(4,128)(2,1)S(1)}, bf16[2,16,4,224]{3,2,1,0:T(4,128)(2,1)S(1)}, u32[]{:S(2)}, u32[]{:S(2)}) collective-permute-start(bf16[2,16,4,224]{3,2,1,0:T(4,128)(2,1)S(1)} %get-tuple-element.40), channel_id=1, source_target_pairs={{0,1},{1,0},{2,3},{3,2},{4,5},{5,4},{6,7},{7,6},{8,9},{9,8},{10,11... | collective-permute-start | bytes 172040 | tf_op jit(solution)/shard_map/ppermute | solution.py:426
  89.5 6.8 %collective-permute-start.4 = (bf16[16,4,224]{2,1,0:T(4,128)(2,1)S(1)}, bf16[16,4,224]{2,1,0:T(4,128)(2,1)S(1)}, u32[]{:S(2)}, u32[]{:S(2)}) collective-permute-start(bf16[16,4,224]{2,1,0:T(4,128)(2,1)S(1)} %get-tuple-element.43), channel_id=1, source_target_pairs={{0,0},{1,65},{2,64},{3,129},{4,128},{5,193},{6,192},{7,1},{8,8},{9... | collective-permute-start | bytes 86024 | tf_op jit(solution)/shard_map/ppermute | solution.py:434
  91.6 5.7 %collective-permute-start.5 = (bf16[16,4,224]{2,1,0:T(4,128)(2,1)S(1)}, bf16[16,4,224]{2,1,0:T(4,128)(2,1)S(1)}, u32[]{:S(2)}, u32[]{:S(2)}) collective-permute-start(bf16[16,4,224]{2,1,0:T(4,128)(2,1)S(1)} %get-tuple-element.44), channel_id=1, source_target_pairs={{0,128},{1,193},{2,192},{3,1},{4,0},{5,65},{6,64},{7,129},{8,136},... | collective-permute-start | bytes 86024 | tf_op jit(solution)/shard_map/ppermute | solution.py:434
  97.3 3.3 %collective-permute-start.6 = (f32[8,4,224]{2,1,0:T(4,128)S(1)}, f32[8,4,224]{2,1,0:T(4,128)S(1)}, u32[]{:S(2)}, u32[]{:S(2)}) collective-permute-start(f32[8,4,224]{2,1,0:T(4,128)S(1)} %slice_select_fusion), channel_id=1, source_target_pairs={{0,1},{1,0},{2,3},{3,2},{4,5},{5,4},{6,7},{7,6},{8,9},{9,8},{10,11... | collective-permute-start | bytes 86024 | tf_op jit(solution)/shard_map/ppermute | solution.py:439

commit v8 on v7

--- a/solution.py
+++ b/solution.py
@@ -13,7 +13,7 @@
 BF16 = jnp.bfloat16
 F32 = jnp.float32
 PARTS = 3
-TURN = (0, 2, 4, 6, 1, 3, 5, 7)
+TURN = (0, 4, 2, 6, 1, 5, 3, 7)
 
 
 def in_turn(n):
@@ -371,8 +371,8 @@
     live_all = live_tokens(slot_request, context_lengths, tokens)
     live_here = lax.dynamic_slice_in_dim(live_all, home, 1, 0)[0]
     local = lax.dynamic_slice_in_dim(slot_request, home, 1, 1)[:, 0] - home * reqs
-    local = local.reshape(-1, len(TURN) // 2, 2)
-    local = jnp.concatenate([local[:, :, 0], local[:, :, 1]], axis=1).reshape(1, -1)
+    local = local.reshape(-1, len(TURN))
+    local = jnp.stack([local[:, z] for z in TURN], axis=1).reshape(1, -1)
     lenders, column = latent_pool.shape[0], 8
     planes = lenders // column
     up = [(l, (l - column) % lenders) for l in range(lenders)]

time: 102 us -> 101 us (level)
  starting transfers between devices: 43.7 us -> 41.1 us
  waiting for transfers between devices: 35.7 us -> 37.7 us
    all_to_all x1, starting transfers between devices: 6.79 us -> 4.32 us  [body(): lax.all_to_all(copies, 'lender', split_axis=0, concat_axis=0, tiled=True,...]
    all_to_all x1, waiting for transfers between devices: 2.29 us -> 0.01 us  [body(): lax.all_to_all(copies, 'lender', split_axis=0, concat_axis=0, tiled=True,...]
    ppermute x1, waiting for transfers between devices: 2.55 us -> 4.59 us  [body(): weight_far = lax.ppermute(weight_up, 'lender', up)]
    all_to_all x1, waiting for transfers between devices: 12.6 us -> 13.6 us  [body(): lax.all_to_all(outgoing, 'lender', split_axis=0, concat_axis=0, tiled=Tru...]
  transfers between devices with their start and end apart: 10 -> 10, of which waited for: 8 -> 7; matrix products, arithmetic and copies ran while one was open for 5% -> 5% of each run, Pallas kernels for 11% -> 11%
where the time goes in v8:
time: 101 us; the launch traced here: 100 us
  starting transfers between devices  41.1 us (41%)
  waiting for transfers between devices  37.7 us (37%)
  Pallas kernels  16.1 us (16%)
  matrix products  2.71 us (3%)
  other arithmetic  2.04 us (2%)
    all_to_all x1, waiting for transfers between devices, body(): lax.all_to_all(outgoing, 'lender', split_axis=0, concat_axis=0, tiled=Tru...  13.6 us
    all_to_all x1, waiting for transfers between devices, body(): lax.all_to_all(sending, 'lender', split_axis=0, concat_axis=0, tiled=True...  13.4 us
    all_to_all x1, starting transfers between devices, body(): lax.all_to_all(outgoing, 'lender', split_axis=0, concat_axis=0, tiled=Tru...  12 us
    pallas_call x1, Pallas kernels, lend(): pl.pallas_call(functools.partial(lend_kernel, scale, group), out_shape=pl...  8.49 us
    all_to_all x1, starting transfers between devices, body(): lax.all_to_all(sending, 'lender', split_axis=0, concat_axis=0, tiled=True...  6.92 us
    ppermute x2, starting transfers between devices, body(): piece = lax.ppermute(own[j], ('lender', 'tensor'), pairs).astype(F32)  6.88 us
    ppermute x1, waiting for transfers between devices, body(): weight_far = lax.ppermute(weight_up, 'lender', up)  4.59 us
    all_to_all x1, starting transfers between devices, body(): lax.all_to_all(copies, 'lender', split_axis=0, concat_axis=0, tiled=True,...  4.32 us
  transfers between devices with their start and end apart: 10, of which 7 were waited for; matrix products, arithmetic and copies ran while one was open for 5% of the time, Pallas kernels for 11%

profile of v8, /device:TPU:1, one launch (start us, length us, event | category | flops | bytes accessed | tf_op | source)
XLA Modules:
  0.0 100.4 jit_solution(11599213940734645785)
XLA Ops:
  0.0 0.0 copy-start.2
  0.0 2.3 %pack.1 = bf16[32,96,128]{2,1,0:T(8,128)(2,1)} custom-call(s32[1]{0:T(128)} %bitcast.4.home_ref, s32[32,32]{1,0:T(8,128)} %slot_request_ref.1, bf16[2,4,16,192]{3,2,1,0:T(8,128)(2,1)} %queries_ref.1), custom_call_target="tpu_custom_call" | custom-call | tf_op jit(solution)/shard_map/pack/pallas_call | solution.py:75
  2.4 0.0 copy-start.4
  2.4 0.0 copy-start.5
  2.4 12.0 %all-to-all-start = ((bf16[32,96,128]{2,1,0:T(8,128)(2,1)}), bf16[32,96,128]{2,1,0:T(8,128)(2,1)S(1)}, u32[]{:S(2)}, u32[]{:S(2)}) async-start(bf16[32,96,128]{2,1,0:T(8,128)(2,1)} %pack.1), calls=%async_computation | async-start | bytes 1572864 | tf_op jit(solution)/shard_map/all_to_all | solution.py:367
  14.4 2.6 %collective-permute-start = (bf16[224,2048]{1,0:T(8,128)(2,1)}, bf16[224,2048]{1,0:T(8,128)(2,1)}, u32[]{:S(2)}, u32[]{:S(2)}) collective-permute-start(bf16[224,2048]{1,0:T(8,128)(2,1)} %bitcast.44), channel_id=1, source_target_pairs={{0,192},{8,200},{16,208},{24,216},{32,224},{40,232},{48,240},{56,2... | collective-permute-start | bytes 2752520 | tf_op jit(solution)/shard_map/ppermute | solution.py:381
  17.0 0.0 copy-done.2
  17.0 0.2 subtract_reduce_fusion
  17.2 0.1 sub.49
  17.3 0.0 copy-done.3
  17.4 0.1 fusion.20
  17.4 0.1 stack.23
  17.5 0.1 reshape.29.local_ref
  17.6 0.0 copy-done
  17.6 0.4 fusion.7
  18.0 0.1 pad_maximum_fusion
  18.1 0.0 copy-done.4
  18.1 0.3 fusion.10
  18.5 0.1 copy.16
  18.6 0.0 copy-done.5
  18.6 0.8 select_reduce_fusion.1
  19.4 0.2 select_reduce_fusion
  19.6 2.0 %fusion.2 = f32[2,4,16,128]{3,1,2,0:T(4,128)S(1)} fusion(bf16[16,512,128]{2,1,0:T(8,128)(2,1)} %values_any.1, bf16[2,4,576]{2,1,0:T(4,128)(2,1)S(1)} %copy-done.4), kind=kOutput, calls=%fused_computation.2 | convolution fusion | flops 16777216 | bytes 2170880 | tf_op jit(solution)/shard_map/ijl,hlc->ijhc/dot_general | solution.py:392
  21.6 13.6 %all-to-all-done.arrived_ref = bf16[32,96,128]{2,1,0:T(8,128)(2,1)S(1)} async-done(((bf16[32,96,128]{2,1,0:T(8,128)(2,1)}), bf16[32,96,128]{2,1,0:T(8,128)(2,1)S(1)}, u32[]{:S(2)}, u32[]{:S(2)}) %all-to-all-start) | async-done | bytes 786464 | tf_op jit(solution)/shard_map/all_to_all | solution.py:367
  35.3 8.5 %lend.1 = bf16[32,72,128]{2,1,0:T(8,128)(2,1)} custom-call(s32[32]{0:T(128)S(1)} %fusion.19.live_ref, bf16[32,96,128]{2,1,0:T(8,128)(2,1)S(1)} %all-to-all-done.arrived_ref, bf16[16,128,512]{2,1,0:T(8,128)(2,1)S(1)} %copy-done, bf16[16,512,128]{2,1,0:T(8,128)(2,1)} %values_any.1, bf16[32,192,576]{2,1,0:T(8,128)(2,1)} %pool_any.1), custom_call_target="tpu_custom_call" | custom-call | tf_op jit(solution)/shard_map/lend/pallas_call | solution.py:213
  43.8 0.0 copy-start.1
  43.8 6.9 %all-to-all-start.1 = ((bf16[32,72,128]{2,1,0:T(8,128)(2,1)}), bf16[32,72,128]{2,1,0:T(8,128)(2,1)S(1)}, u32[]{:S(2)}, u32[]{:S(2)}) async-start(bf16[32,72,128]{2,1,0:T(8,128)(2,1)} %lend.1), calls=%async_computation.1 | async-start | bytes 1179648 | tf_op jit(solution)/shard_map/all_to_all | solution.py:401
  50.7 0.0 collective-permute-done.refs_1_
  50.7 2.6 %collective-permute-start.1 = (bf16[224,2048]{1,0:T(8,128)(2,1)}, bf16[224,2048]{1,0:T(8,128)(2,1)}, u32[]{:S(2)}, u32[]{:S(2)}) collective-permute-start(bf16[224,2048]{1,0:T(8,128)(2,1)} %collective-permute-done.refs_1_), channel_id=1, source_target_pairs={{0,192},{8,200},{16,208},{24,216},{32,224},{40,232},{48,240},{56,2... | collective-permute-start | bytes 2752520 | tf_op jit(solution)/shard_map/ppermute | solution.py:404
  53.3 0.0 collective-permute-start.2
  53.3 13.4 %all-to-all-done.1.back_ref = bf16[32,72,128]{2,1,0:T(8,128)(2,1)S(1)} async-done(((bf16[32,72,128]{2,1,0:T(8,128)(2,1)}), bf16[32,72,128]{2,1,0:T(8,128)(2,1)S(1)}, u32[]{:S(2)}, u32[]{:S(2)}) %all-to-all-start.1) | async-done | bytes 589856 | tf_op jit(solution)/shard_map/all_to_all | solution.py:401
  66.7 2.3 %settle.1 = bf16[8,8,2048]{2,1,0:T(8,128)(2,1)} custom-call(bf16[32,72,128]{2,1,0:T(8,128)(2,1)S(1)} %all-to-all-done.1.back_ref, s32[1,32]{1,0:T(1,128)S(1)} %reshape.29.local_ref, f32[2,64,4]{2,1,0:T(8,128)S(1)} %bitcast.47, f32[2,4,16,128]{3,2,1,0:T(8,128)S(1)} %copy.17.draft_values_ref), custom_call_target="tpu_custom_call" | custom-call | tf_op jit(solution)/shard_map/settle/pallas_call | solution.py:276
  69.0 4.3 %all-to-all-start.2 = ((bf16[8,8,2048]{2,1,0:T(8,128)(2,1)}), bf16[8,8,2048]{2,1,0:T(8,128)(2,1)S(1)}, u32[]{:S(2)}, u32[]{:S(2)}) async-start(bf16[8,8,2048]{2,1,0:T(8,128)(2,1)} %settle.1), calls=%async_computation.2 | async-start | bytes 524288 | tf_op jit(solution)/shard_map/all_to_all | solution.py:409
  73.3 0.1 pad_add_fusion.place_ref
  73.4 4.6 %collective-permute-done.1.refs_2_ = bf16[224,2048]{1,0:T(8,128)(2,1)} collective-permute-done((bf16[224,2048]{1,0:T(8,128)(2,1)}, bf16[224,2048]{1,0:T(8,128)(2,1)}, u32[]{:S(2)}, u32[]{:S(2)}) %collective-permute-start.1) | collective-permute-done | bytes 917536 | tf_op jit(solution)/shard_map/ppermute | solution.py:404
  78.0 3.2 %collective-permute-done.2.refs_3_ = bf16[224,2048]{1,0:T(8,128)(2,1)S(1)} collective-permute-done((bf16[224,2048]{1,0:T(8,128)(2,1)}, bf16[224,2048]{1,0:T(8,128)(2,1)S(1)}, u32[]{:S(2)}, u32[]{:S(2)}) %collective-permute-start.2) | collective-permute-done | bytes 917536 | tf_op jit(solution)/shard_map/ppermute | solution.py:405
  81.2 0.0 all-to-all-done.2
  81.2 0.0 copy-done.1
  81.2 3.0 %mix.1 = (bf16[2,16,4,224]{3,2,1,0:T(4,128)(2,1)S(1)}, bf16[2,16,4,224]{3,2,1,0:T(4,128)(2,1)S(1)}) custom-call(s32[4]{0:T(128)S(1)} %pad_add_fusion.place_ref, bf16[64,2048]{1,0:T(8,128)(2,1)S(1)} %bitcast.43, bf16[224,2048]{1,0:T(8,128)(2,1)S(1)} %bitcast.46, bf16[224,2048]{1,0:T(8,128)(2,1)} %collective-permute-done.refs_1_, ...), custom_call_target="tpu_custom_call" | custom-call | tf_op jit(solution)/shard_map/mix/pallas_call | solution.py:323
  84.2 3.7 %collective-permute-start.3 = (bf16[2,16,4,224]{3,2,1,0:T(4,128)(2,1)S(1)}, bf16[2,16,4,224]{3,2,1,0:T(4,128)(2,1)S(1)}, u32[]{:S(2)}, u32[]{:S(2)}) collective-permute-start(bf16[2,16,4,224]{3,2,1,0:T(4,128)(2,1)S(1)} %get-tuple-element.40), channel_id=1, source_target_pairs={{0,1},{1,0},{2,3},{3,2},{4,5},{5,4},{6,7},{7,6},{8,9},{9,8},{10,11... | collective-permute-start | bytes 172040 | tf_op jit(solution)/shard_map/ppermute | solution.py:426
  87.9 0.9 collective-permute-done.3
  88.9 2.2 %collective-permute-start.4 = (bf16[16,4,224]{2,1,0:T(4,128)(2,1)S(1)}, bf16[16,4,224]{2,1,0:T(4,128)(2,1)S(1)}, u32[]{:S(2)}, u32[]{:S(2)}) collective-permute-start(bf16[16,4,224]{2,1,0:T(4,128)(2,1)S(1)} %get-tuple-element.41), channel_id=1, source_target_pairs={{0,0},{1,65},{2,64},{3,129},{4,128},{5,193},{6,192},{7,1},{8,8},{9... | collective-permute-start | bytes 86024 | tf_op jit(solution)/shard_map/ppermute | solution.py:434
  91.1 4.7 %collective-permute-start.5 = (bf16[16,4,224]{2,1,0:T(4,128)(2,1)S(1)}, bf16[16,4,224]{2,1,0:T(4,128)(2,1)S(1)}, u32[]{:S(2)}, u32[]{:S(2)}) collective-permute-start(bf16[16,4,224]{2,1,0:T(4,128)(2,1)S(1)} %get-tuple-element.42), channel_id=1, source_target_pairs={{0,128},{1,193},{2,192},{3,1},{4,0},{5,65},{6,64},{7,129},{8,136},... | collective-permute-start | bytes 86024 | tf_op jit(solution)/shard_map/ppermute | solution.py:434
  95.8 0.0 collective-permute-done.4
  95.8 1.0 %collective-permute-done.5 = bf16[16,4,224]{2,1,0:T(4,128)(2,1)S(1)} collective-permute-done((bf16[16,4,224]{2,1,0:T(4,128)(2,1)S(1)}, bf16[16,4,224]{2,1,0:T(4,128)(2,1)S(1)}, u32[]{:S(2)}, u32[]{:S(2)}) %collective-permute-start.5) | collective-permute-done | bytes 28704 | tf_op jit(solution)/shard_map/ppermute | solution.py:434
  96.8 2.1 %collective-permute-start.6 = (f32[8,4,224]{2,1,0:T(4,128)S(1)}, f32[8,4,224]{2,1,0:T(4,128)S(1)}, u32[]{:S(2)}, u32[]{:S(2)}) collective-permute-start(f32[8,4,224]{2,1,0:T(4,128)S(1)} %slice_select_fusion), channel_id=1, source_target_pairs={{0,1},{1,0},{2,3},{3,2},{4,5},{5,4},{6,7},{7,6},{8,9},{9,8},{10,11... | collective-permute-start | bytes 86024 | tf_op jit(solution)/shard_map/ppermute | solution.py:439
  99.0 0.9 collective-permute-done.6
  99.8 0.6 add_convert_fusion.1
  (12 shorter events, 0.2 us)
Async XLA Ops:
  0.0 17.0 %copy-start.2 = (s32[32,32]{1,0:T(8,128)S(1)}, s32[32,32]{1,0:T(8,128)}, u32[]{:S(2)}) copy-start(s32[32,32]{1,0:T(8,128)} %slot_request_ref.1) | copy-start | bytes 12292
  0.0 17.3 %copy-start.3 = (bf16[2,4,16,192]{3,2,1,0:T(8,128)(2,1)S(1)}, bf16[2,4,16,192]{3,2,1,0:T(8,128)(2,1)}, u32[]{:S(2)}) copy-start(bf16[2,4,16,192]{3,2,1,0:T(8,128)(2,1)} %queries_ref.1) | copy-start | bytes 147460
  0.0 17.6 %copy-start = (bf16[16,128,512]{2,1,0:T(8,128)(2,1)S(1)}, bf16[16,128,512]{2,1,0:T(8,128)(2,1)}, u32[]{:S(2)}) copy-start(bf16[16,128,512]{2,1,0:T(8,128)(2,1)} %keys_ref.1) | copy-start | bytes 6291460
  2.4 15.7 %copy-start.4 = (bf16[2,4,576]{2,1,0:T(4,128)(2,1)S(1)}, bf16[2,4,576]{2,1,0:T(4,128)(2,1)}, u32[]{:S(2)}) copy-start(bf16[2,4,576]{2,1,0:T(4,128)(2,1)} %param.9) | copy-start | bytes 27652
  2.4 16.2 %copy-start.5 = (s32[64]{0:T(128)S(1)}, s32[64]{0:T(128)}, u32[]{:S(2)}) copy-start(s32[64]{0:T(128)} %param.15) | copy-start | bytes 772
  2.4 32.9 %all-to-all-start = ((bf16[32,96,128]{2,1,0:T(8,128)(2,1)}), bf16[32,96,128]{2,1,0:T(8,128)(2,1)S(1)}, u32[]{:S(2)}, u32[]{:S(2)}) async-start(bf16[32,96,128]{2,1,0:T(8,128)(2,1)} %pack.1), calls=%async_computation | async-start | bytes 1572864 | tf_op jit(solution)/shard_map/all_to_all | solution.py:367
  14.4 36.3 %collective-permute-start = (bf16[224,2048]{1,0:T(8,128)(2,1)}, bf16[224,2048]{1,0:T(8,128)(2,1)}, u32[]{:S(2)}, u32[]{:S(2)}) collective-permute-start(bf16[224,2048]{1,0:T(8,128)(2,1)} %bitcast.44), channel_id=1, source_target_pairs={{0,192},{8,200},{16,208},{24,216},{32,224},{40,232},{48,240},{56,2... | collective-permute-start | bytes 2752520 | tf_op jit(solution)/shard_map/ppermute | solution.py:381
  43.8 37.5 %copy-start.1 = (bf16[2048,224]{0,1:T(8,128)(2,1)S(1)}, bf16[2048,224]{0,1:T(8,128)(2,1)}, u32[]{:S(2)}) copy-start(bf16[2048,224]{0,1:T(8,128)(2,1)} %param.13) | copy-start | bytes 2752516
  43.8 22.9 %all-to-all-start.1 = ((bf16[32,72,128]{2,1,0:T(8,128)(2,1)}), bf16[32,72,128]{2,1,0:T(8,128)(2,1)S(1)}, u32[]{:S(2)}, u32[]{:S(2)}) async-start(bf16[32,72,128]{2,1,0:T(8,128)(2,1)} %lend.1), calls=%async_computation.1 | async-start | bytes 1179648 | tf_op jit(solution)/shard_map/all_to_all | solution.py:401
  50.7 27.3 %collective-permute-start.1 = (bf16[224,2048]{1,0:T(8,128)(2,1)}, bf16[224,2048]{1,0:T(8,128)(2,1)}, u32[]{:S(2)}, u32[]{:S(2)}) collective-permute-start(bf16[224,2048]{1,0:T(8,128)(2,1)} %collective-permute-done.refs_1_), channel_id=1, source_target_pairs={{0,192},{8,200},{16,208},{24,216},{32,224},{40,232},{48,240},{56,2... | collective-permute-start | bytes 2752520 | tf_op jit(solution)/shard_map/ppermute | solution.py:404
  53.3 27.9 %collective-permute-start.2 = (bf16[224,2048]{1,0:T(8,128)(2,1)}, bf16[224,2048]{1,0:T(8,128)(2,1)S(1)}, u32[]{:S(2)}, u32[]{:S(2)}) collective-permute-start(bf16[224,2048]{1,0:T(8,128)(2,1)} %bitcast.45), channel_id=1, source_target_pairs={{0,64},{8,72},{16,80},{24,88},{32,96},{40,104},{48,112},{56,120},{... | collective-permute-start | bytes 2752520 | tf_op jit(solution)/shard_map/ppermute | solution.py:405
  69.0 12.2 %all-to-all-start.2 = ((bf16[8,8,2048]{2,1,0:T(8,128)(2,1)}), bf16[8,8,2048]{2,1,0:T(8,128)(2,1)S(1)}, u32[]{:S(2)}, u32[]{:S(2)}) async-start(bf16[8,8,2048]{2,1,0:T(8,128)(2,1)} %settle.1), calls=%async_computation.2 | async-start | bytes 524288 | tf_op jit(solution)/shard_map/all_to_all | solution.py:409
  84.2 4.6 %collective-permute-start.3 = (bf16[2,16,4,224]{3,2,1,0:T(4,128)(2,1)S(1)}, bf16[2,16,4,224]{3,2,1,0:T(4,128)(2,1)S(1)}, u32[]{:S(2)}, u32[]{:S(2)}) collective-permute-start(bf16[2,16,4,224]{3,2,1,0:T(4,128)(2,1)S(1)} %get-tuple-element.40), channel_id=1, source_target_pairs={{0,1},{1,0},{2,3},{3,2},{4,5},{5,4},{6,7},{7,6},{8,9},{9,8},{10,11... | collective-permute-start | bytes 172040 | tf_op jit(solution)/shard_map/ppermute | solution.py:426
  88.9 6.9 %collective-permute-start.4 = (bf16[16,4,224]{2,1,0:T(4,128)(2,1)S(1)}, bf16[16,4,224]{2,1,0:T(4,128)(2,1)S(1)}, u32[]{:S(2)}, u32[]{:S(2)}) collective-permute-start(bf16[16,4,224]{2,1,0:T(4,128)(2,1)S(1)} %get-tuple-element.41), channel_id=1, source_target_pairs={{0,0},{1,65},{2,64},{3,129},{4,128},{5,193},{6,192},{7,1},{8,8},{9... | collective-permute-start | bytes 86024 | tf_op jit(solution)/shard_map/ppermute | solution.py:434
  91.1 5.7 %collective-permute-start.5 = (bf16[16,4,224]{2,1,0:T(4,128)(2,1)S(1)}, bf16[16,4,224]{2,1,0:T(4,128)(2,1)S(1)}, u32[]{:S(2)}, u32[]{:S(2)}) collective-permute-start(bf16[16,4,224]{2,1,0:T(4,128)(2,1)S(1)} %get-tuple-element.42), channel_id=1, source_target_pairs={{0,128},{1,193},{2,192},{3,1},{4,0},{5,65},{6,64},{7,129},{8,136},... | collective-permute-start | bytes 86024 | tf_op jit(solution)/shard_map/ppermute | solution.py:434
  96.8 3.0 %collective-permute-start.6 = (f32[8,4,224]{2,1,0:T(4,128)S(1)}, f32[8,4,224]{2,1,0:T(4,128)S(1)}, u32[]{:S(2)}, u32[]{:S(2)}) collective-permute-start(f32[8,4,224]{2,1,0:T(4,128)S(1)} %slice_select_fusion), channel_id=1, source_target_pairs={{0,1},{1,0},{2,3},{3,2},{4,5},{5,4},{6,7},{7,6},{8,9},{9,8},{10,11... | collective-permute-start | bytes 86024 | tf_op jit(solution)/shard_map/ppermute | solution.py:439
